TPU v7x, 32 devices: a whole 2x2x4 slice. The times are simulated.
32 devices in a mesh: dp: 4 (over x, core), fsdp: 8 (over z, y).
Axes of the slice: x: 2, y: 2, z: 4, core: 2. Of those that a mesh axis runs over, the one named last changes fastest.
Arguments:
- x_query: bfloat16 [64, 256, 768], P(('dp', 'fsdp')), may hold values from -6 to 6
- x_key: bfloat16 [64, 256, 768], P(('dp', 'fsdp')), may hold values from -6 to 6
- len_query: int32 [64], P(('dp', 'fsdp')), may hold values from 1 to 256, as said below
- len_key: int32 [64], P(('dp', 'fsdp')), may hold values from 1 to 256, as said below
- queue: bfloat16 [16384, 768], P(('dp', 'fsdp')), may hold values from -0.875 to 0.875
- qkv_weight: bfloat16 [2, 768, 2304], P(None, 'fsdp'), may hold values from -0.21875 to 0.21875
- query_bias: bfloat16 [2, 768], P(None, 'fsdp'), may hold values from -0.625 to 0.625
- value_bias: bfloat16 [2, 768], P(None, 'fsdp'), may hold values from -0.625 to 0.625
- proj_weight: bfloat16 [2, 768, 768], P(None, 'fsdp'), may hold values from -2.5 to 2.5
- proj_bias: bfloat16 [2, 768], P(None, 'fsdp'), may hold values from -0.625 to 0.625
- first_gain: bfloat16 [2, 768], P(None, 'fsdp'), may hold values from 0.5 to 1.5
- first_shift: bfloat16 [2, 768], P(None, 'fsdp'), may hold values from -0.625 to 0.625
- expand_weight: bfloat16 [2, 768, 3072], P(None, 'fsdp'), may hold values from -0.21875 to 0.21875
- expand_bias: bfloat16 [2, 3072], P(None, 'fsdp'), may hold values from -0.625 to 0.625
- shrink_weight: bfloat16 [2, 3072, 768], P(None, 'fsdp'), may hold values from -0.109375 to 0.109375
- shrink_bias: bfloat16 [2, 768], P(None, 'fsdp'), may hold values from -0.625 to 0.625
- second_gain: bfloat16 [2, 768], P(None, 'fsdp'), may hold values from 0.5 to 1.5
- second_shift: bfloat16 [2, 768], P(None, 'fsdp'), may hold values from -0.625 to 0.625
- key_qkv: float32 [2, 768, 2304], P(None, 'fsdp'), may hold values from -0.21875 to 0.21875
- key_querybias: float32 [2, 768], P(None, 'fsdp'), may hold values from -0.625 to 0.625
- key_valuebias: float32 [2, 768], P(None, 'fsdp'), may hold values from -0.625 to 0.625
- key_proj: float32 [2, 768, 768], P(None, 'fsdp'), may hold values from -2.5 to 2.5
- key_projbias: float32 [2, 768], P(None, 'fsdp'), may hold values from -0.625 to 0.625
- key_firstgain: float32 [2, 768], P(None, 'fsdp'), may hold values from 0.5 to 1.5
- key_firstshift: float32 [2, 768], P(None, 'fsdp'), may hold values from -0.625 to 0.625
- key_expand: float32 [2, 768, 3072], P(None, 'fsdp'), may hold values from -0.21875 to 0.21875
- key_expandbias: float32 [2, 3072], P(None, 'fsdp'), may hold values from -0.625 to 0.625
- key_shrink: float32 [2, 3072, 768], P(None, 'fsdp'), may hold values from -0.109375 to 0.109375
- key_shrinkbias: float32 [2, 768], P(None, 'fsdp'), may hold values from -0.625 to 0.625
- key_secondgain: float32 [2, 768], P(None, 'fsdp'), may hold values from 0.5 to 1.5
- key_secondshift: float32 [2, 768], P(None, 'fsdp'), may hold values from -0.625 to 0.625
Outputs:
- hidden_out: bfloat16 [64, 256, 768], P(('dp', 'fsdp'))
- grad_input: bfloat16 [64, 256, 768], P(('dp', 'fsdp'))
- grad_qkv: float32 [2, 768, 2304], P(None, 'fsdp')
- grad_querybias: float32 [2, 768], P(None, 'fsdp')
- grad_valuebias: float32 [2, 768], P(None, 'fsdp')
- grad_proj: float32 [2, 768, 768], P(None, 'fsdp')
- grad_projbias: float32 [2, 768], P(None, 'fsdp')
- grad_firstgain: float32 [2, 768], P(None, 'fsdp')
- grad_firstshift: float32 [2, 768], P(None, 'fsdp')
- grad_expand: float32 [2, 768, 3072], P(None, 'fsdp')
- grad_expandbias: float32 [2, 3072], P(None, 'fsdp')
- grad_shrink: float32 [2, 3072, 768], P(None, 'fsdp')
- grad_shrinkbias: float32 [2, 768], P(None, 'fsdp')
- grad_secondgain: float32 [2, 768], P(None, 'fsdp')
- grad_secondshift: float32 [2, 768], P(None, 'fsdp')
- crop_loss: float32 [64], P(('dp', 'fsdp'))
Inputs may be any that keep to these rules, and one draw needn't show every extreme that they name: `len_query`: the crops of one device share a domain; the bound of a domain is 256, 192, 128 or 64, and a crop's length lies between three quarters of its bound and the bound, except one crop of 256 tokens. `len_key`: the same law as len_query, with the same domain for each device and lengths drawn afresh.
All inputs are finite; a program needn't handle non-finite values.
Results may differ from a plain program's by a relative error of at most 0.04.
Values may be sent and summed in bfloat16 or wider, within the bound.
A program may use at most 192 MiB of HBM per device.

v0:
```python
import jax
import jax.numpy as jnp
from jax import lax
from jax.sharding import PartitionSpec as P

HEADS = 12
LAYERS = 2


contrast_sharpness = 0.05
objective_factor = 512.0
momentum = 0.9995
norm_eps = 1e-12
unit_eps = 1e-06
masked = -1000000000.0


def layer_norm(residual, gain_vec, shift_vec):
    centered = residual - jnp.mean(residual, -1, keepdims=True)
    spread = jnp.mean(centered * centered, -1, keepdims=True)
    return centered * lax.rsqrt(spread + norm_eps) * gain_vec + shift_vec


def unit_rows(pooled):
    return pooled * lax.rsqrt(jnp.sum(pooled * pooled, -1, keepdims=True) + unit_eps)


def gelu_exact(pre_act):
    return jax.nn.gelu(pre_act, approximate=False)


def pool_rows(final_out, key_valid, lengths):
    num_crops, seq_len = key_valid.shape
    shaped = final_out.reshape(num_crops, seq_len, final_out.shape[-1])
    summed = jnp.sum(jnp.where(key_valid[:, :, None], shaped, 0.0), 1)
    return summed / lengths[:, None].astype(jnp.float32)


def gather_query(
    qkv_mat,
    query_add,
    value_add,
    proj_mat,
    proj_add,
    first_gain,
    first_shift,
    expand_mat,
    expand_add,
    shrink_mat,
    shrink_add,
    second_gain,
    second_shift,
):
    return (
        lax.all_gather(qkv_mat, "fsdp", axis=0, tiled=True),
        lax.all_gather(query_add, "fsdp", axis=0, tiled=True),
        lax.all_gather(value_add, "fsdp", axis=0, tiled=True),
        lax.all_gather(proj_mat, "fsdp", axis=0, tiled=True),
        lax.all_gather(proj_add, "fsdp", axis=0, tiled=True),
        lax.all_gather(first_gain, "fsdp", axis=0, tiled=True),
        lax.all_gather(first_shift, "fsdp", axis=0, tiled=True),
        lax.all_gather(expand_mat, "fsdp", axis=0, tiled=True),
        lax.all_gather(expand_add, "fsdp", axis=0, tiled=True),
        lax.all_gather(shrink_mat, "fsdp", axis=0, tiled=True),
        lax.all_gather(shrink_add, "fsdp", axis=0, tiled=True),
        lax.all_gather(second_gain, "fsdp", axis=0, tiled=True),
        lax.all_gather(second_shift, "fsdp", axis=0, tiled=True),
    )


def gather_mirror(
    qkv_mat,
    query_add,
    value_add,
    proj_mat,
    proj_add,
    first_gain,
    first_shift,
    expand_mat,
    expand_add,
    shrink_mat,
    shrink_add,
    second_gain,
    second_shift,
):
    return (
        lax.all_gather(qkv_mat, "fsdp", axis=0, tiled=True),
        lax.all_gather(query_add, "fsdp", axis=0, tiled=True),
        lax.all_gather(value_add, "fsdp", axis=0, tiled=True),
        lax.all_gather(proj_mat, "fsdp", axis=0, tiled=True),
        lax.all_gather(proj_add, "fsdp", axis=0, tiled=True),
        lax.all_gather(first_gain, "fsdp", axis=0, tiled=True),
        lax.all_gather(first_shift, "fsdp", axis=0, tiled=True),
        lax.all_gather(expand_mat, "fsdp", axis=0, tiled=True),
        lax.all_gather(expand_add, "fsdp", axis=0, tiled=True),
        lax.all_gather(shrink_mat, "fsdp", axis=0, tiled=True),
        lax.all_gather(shrink_add, "fsdp", axis=0, tiled=True),
        lax.all_gather(second_gain, "fsdp", axis=0, tiled=True),
        lax.all_gather(second_shift, "fsdp", axis=0, tiled=True),
    )


def scatter_grads(
    qkv_mat,
    query_add,
    value_add,
    proj_mat,
    proj_add,
    first_gain,
    first_shift,
    expand_mat,
    expand_add,
    shrink_mat,
    shrink_add,
    second_gain,
    second_shift,
):
    return (
        lax.psum_scatter(
            qkv_mat.astype(jnp.bfloat16), "fsdp", scatter_dimension=0, tiled=True
        ).astype(jnp.float32),
        lax.psum_scatter(
            query_add.astype(jnp.bfloat16), "fsdp", scatter_dimension=0, tiled=True
        ).astype(jnp.float32),
        lax.psum_scatter(
            value_add.astype(jnp.bfloat16), "fsdp", scatter_dimension=0, tiled=True
        ).astype(jnp.float32),
        lax.psum_scatter(
            proj_mat.astype(jnp.bfloat16), "fsdp", scatter_dimension=0, tiled=True
        ).astype(jnp.float32),
        lax.psum_scatter(
            proj_add.astype(jnp.bfloat16), "fsdp", scatter_dimension=0, tiled=True
        ).astype(jnp.float32),
        lax.psum_scatter(
            first_gain.astype(jnp.bfloat16), "fsdp", scatter_dimension=0, tiled=True
        ).astype(jnp.float32),
        lax.psum_scatter(
            first_shift.astype(jnp.bfloat16), "fsdp", scatter_dimension=0, tiled=True
        ).astype(jnp.float32),
        lax.psum_scatter(
            expand_mat.astype(jnp.bfloat16), "fsdp", scatter_dimension=0, tiled=True
        ).astype(jnp.float32),
        lax.psum_scatter(
            expand_add.astype(jnp.bfloat16), "fsdp", scatter_dimension=0, tiled=True
        ).astype(jnp.float32),
        lax.psum_scatter(
            shrink_mat.astype(jnp.bfloat16), "fsdp", scatter_dimension=0, tiled=True
        ).astype(jnp.float32),
        lax.psum_scatter(
            shrink_add.astype(jnp.bfloat16), "fsdp", scatter_dimension=0, tiled=True
        ).astype(jnp.float32),
        lax.psum_scatter(
            second_gain.astype(jnp.bfloat16), "fsdp", scatter_dimension=0, tiled=True
        ).astype(jnp.float32),
        lax.psum_scatter(
            second_shift.astype(jnp.bfloat16), "fsdp", scatter_dimension=0, tiled=True
        ).astype(jnp.float32),
    )


def sum_grads(
    qkv_mat,
    query_add,
    value_add,
    proj_mat,
    proj_add,
    first_gain,
    first_shift,
    expand_mat,
    expand_add,
    shrink_mat,
    shrink_add,
    second_gain,
    second_shift,
):
    return (
        lax.psum(qkv_mat.astype(jnp.bfloat16), "dp").astype(jnp.float32),
        lax.psum(query_add.astype(jnp.bfloat16), "dp").astype(jnp.float32),
        lax.psum(value_add.astype(jnp.bfloat16), "dp").astype(jnp.float32),
        lax.psum(proj_mat.astype(jnp.bfloat16), "dp").astype(jnp.float32),
        lax.psum(proj_add.astype(jnp.bfloat16), "dp").astype(jnp.float32),
        lax.psum(first_gain.astype(jnp.bfloat16), "dp").astype(jnp.float32),
        lax.psum(first_shift.astype(jnp.bfloat16), "dp").astype(jnp.float32),
        lax.psum(expand_mat.astype(jnp.bfloat16), "dp").astype(jnp.float32),
        lax.psum(expand_add.astype(jnp.bfloat16), "dp").astype(jnp.float32),
        lax.psum(shrink_mat.astype(jnp.bfloat16), "dp").astype(jnp.float32),
        lax.psum(shrink_add.astype(jnp.bfloat16), "dp").astype(jnp.float32),
        lax.psum(second_gain.astype(jnp.bfloat16), "dp").astype(jnp.float32),
        lax.psum(second_shift.astype(jnp.bfloat16), "dp").astype(jnp.float32),
    )


def attention_scores(queries, key_vecs, key_valid):
    score_scale = queries.shape[-1] ** (-0.5)
    raw_scores = (
        jnp.einsum("cqhe,ckhe->chqk", queries, key_vecs, preferred_element_type=jnp.float32)
        * score_scale
    )
    return jnp.where(key_valid[:, None, None, :], raw_scores, masked)


def layer_forward(inputs, key_valid, weights):
    (
        qkv_mat,
        query_add,
        value_add,
        proj_mat,
        proj_add,
        first_gain,
        first_shift,
        expand_mat,
        expand_add,
        shrink_mat,
        shrink_add,
        second_gain,
        second_shift,
    ) = weights
    num_crops, seq_len, model_width = inputs.shape
    head_shape = (num_crops, seq_len, HEADS, model_width // HEADS)
    in_rows = inputs.reshape(num_crops * seq_len, model_width)
    projected = jnp.dot(in_rows, qkv_mat, preferred_element_type=jnp.float32)
    queries = (projected[:, :model_width] + query_add.astype(jnp.float32)).astype(jnp.bfloat16)
    key_vecs = projected[:, model_width : 2 * model_width].astype(jnp.bfloat16)
    values = (projected[:, 2 * model_width :] + value_add.astype(jnp.float32)).astype(jnp.bfloat16)
    scores = attention_scores(queries.reshape(head_shape), key_vecs.reshape(head_shape), key_valid)
    row_peak = jnp.max(scores, -1, keepdims=True)
    exp_scores = jnp.exp(scores - row_peak)
    exp_total = jnp.sum(exp_scores, -1, keepdims=True)
    log_total = row_peak + jnp.log(exp_total)
    prob_low = (exp_scores / exp_total).astype(jnp.bfloat16)
    context = jnp.einsum(
        "chqk,ckhe->cqhe", prob_low, values.reshape(head_shape), preferred_element_type=jnp.float32
    )
    context = context.astype(jnp.bfloat16).reshape(num_crops * seq_len, model_width)
    attn_out = jnp.dot(context, proj_mat, preferred_element_type=jnp.float32) + proj_add.astype(
        jnp.float32
    )
    residual_a = in_rows.astype(jnp.float32) + attn_out
    hidden_a = layer_norm(
        residual_a, first_gain.astype(jnp.float32), first_shift.astype(jnp.float32)
    )
    hidden_low = hidden_a.astype(jnp.bfloat16)
    ffn_inner = jnp.dot(
        hidden_low, expand_mat, preferred_element_type=jnp.float32
    ) + expand_add.astype(jnp.float32)
    active = gelu_exact(ffn_inner).astype(jnp.bfloat16)
    branch = jnp.dot(active, shrink_mat, preferred_element_type=jnp.float32) + shrink_add.astype(
        jnp.float32
    )
    residual_b = hidden_a + branch
    final_out = layer_norm(
        residual_b, second_gain.astype(jnp.float32), second_shift.astype(jnp.float32)
    )
    saved_state = (
        in_rows,
        queries,
        key_vecs,
        values,
        log_total,
        context,
        residual_a,
        hidden_low,
        ffn_inner,
        active,
        residual_b,
    )
    return (final_out, saved_state)


def layer_backward(grad_out, saved_state, key_valid, weights):
    (
        qkv_mat,
        query_add,
        value_add,
        proj_mat,
        proj_add,
        first_gain,
        first_shift,
        expand_mat,
        expand_add,
        shrink_mat,
        shrink_add,
        second_gain,
        second_shift,
    ) = weights
    (
        in_rows,
        queries,
        key_vecs,
        values,
        log_total,
        context,
        residual_a,
        hidden_low,
        ffn_inner,
        active,
        residual_b,
    ) = saved_state
    num_rows, model_width = in_rows.shape
    num_crops = key_valid.shape[0]
    head_shape = (num_crops, num_rows // num_crops, HEADS, model_width // HEADS)
    score_scale = (model_width // HEADS) ** (-0.5)
    unused, second_back = jax.vjp(
        layer_norm, residual_b, second_gain.astype(jnp.float32), second_shift.astype(jnp.float32)
    )
    grad_resid_b, grad_second_gain, grad_second_shift = second_back(grad_out)
    grad_branch = grad_resid_b.astype(jnp.bfloat16)
    grad_shrink_add = jnp.sum(grad_branch.astype(jnp.float32), 0)
    grad_shrink_mat = jnp.einsum(
        "tf,td->fd", active, grad_branch, preferred_element_type=jnp.float32
    )
    grad_active = jnp.einsum(
        "td,fd->tf", grad_branch, shrink_mat, preferred_element_type=jnp.float32
    )
    unused, gelu_back = jax.vjp(gelu_exact, ffn_inner)
    grad_inner = gelu_back(grad_active)[0].astype(jnp.bfloat16)
    grad_expand_add = jnp.sum(grad_inner.astype(jnp.float32), 0)
    grad_expand_mat = jnp.einsum(
        "td,tf->df", hidden_low, grad_inner, preferred_element_type=jnp.float32
    )
    grad_hidden = grad_resid_b + jnp.einsum(
        "tf,df->td", grad_inner, expand_mat, preferred_element_type=jnp.float32
    )
    unused, first_back = jax.vjp(
        layer_norm, residual_a, first_gain.astype(jnp.float32), first_shift.astype(jnp.float32)
    )
    grad_resid_a, grad_first_gain, grad_first_shift = first_back(grad_hidden)
    grad_attn = grad_resid_a.astype(jnp.bfloat16)
    grad_proj_add = jnp.sum(grad_attn.astype(jnp.float32), 0)
    grad_proj_mat = jnp.einsum("td,te->de", context, grad_attn, preferred_element_type=jnp.float32)
    grad_context = jnp.einsum("te,de->td", grad_attn, proj_mat, preferred_element_type=jnp.float32)
    grad_context = grad_context.astype(jnp.bfloat16).reshape(head_shape)
    query_heads = queries.reshape(head_shape)
    key_heads = key_vecs.reshape(head_shape)
    value_heads = values.reshape(head_shape)
    scores = attention_scores(query_heads, key_heads, key_valid)
    probs = jnp.exp(scores - log_total)
    grad_values = jnp.einsum(
        "chqk,cqhe->ckhe",
        probs.astype(jnp.bfloat16),
        grad_context,
        preferred_element_type=jnp.float32,
    ).astype(jnp.bfloat16)
    grad_probs = jnp.einsum(
        "cqhe,ckhe->chqk", grad_context, value_heads, preferred_element_type=jnp.float32
    )
    row_delta = jnp.sum(probs * grad_probs, -1, keepdims=True)
    grad_scores = (probs * (grad_probs - row_delta)).astype(jnp.bfloat16)
    grad_queries = (
        jnp.einsum("chqk,ckhe->cqhe", grad_scores, key_heads, preferred_element_type=jnp.float32)
        * score_scale
    ).astype(jnp.bfloat16)
    grad_keys = (
        jnp.einsum("chqk,cqhe->ckhe", grad_scores, query_heads, preferred_element_type=jnp.float32)
        * score_scale
    ).astype(jnp.bfloat16)
    grad_mixed = jnp.concatenate(
        [
            grad_queries.reshape(num_rows, model_width),
            grad_keys.reshape(num_rows, model_width),
            grad_values.reshape(num_rows, model_width),
        ],
        1,
    )
    grad_qkv_mat = jnp.einsum("td,te->de", in_rows, grad_mixed, preferred_element_type=jnp.float32)
    grad_query_add = jnp.sum(grad_mixed[:, :model_width].astype(jnp.float32), 0)
    grad_value_add = jnp.sum(grad_mixed[:, 2 * model_width :].astype(jnp.float32), 0)
    grad_rows = grad_resid_a + jnp.einsum(
        "te,de->td", grad_mixed, qkv_mat, preferred_element_type=jnp.float32
    )
    return (
        grad_rows,
        (
            grad_qkv_mat,
            grad_query_add,
            grad_value_add,
            grad_proj_mat,
            grad_proj_add,
            grad_first_gain,
            grad_first_shift,
            grad_expand_mat,
            grad_expand_add,
            grad_shrink_mat,
            grad_shrink_add,
            grad_second_gain,
            grad_second_shift,
        ),
    )


def on_device(
    x_query,
    x_key,
    len_query,
    len_key,
    queue,
    qkv_weight,
    query_bias,
    value_bias,
    proj_weight,
    proj_bias,
    first_gain,
    first_shift,
    expand_weight,
    expand_bias,
    shrink_weight,
    shrink_bias,
    second_gain,
    second_shift,
    key_qkv,
    key_querybias,
    key_valuebias,
    key_proj,
    key_projbias,
    key_firstgain,
    key_firstshift,
    key_expand,
    key_expandbias,
    key_shrink,
    key_shrinkbias,
    key_secondgain,
    key_secondshift,
):
    query_params = (
        qkv_weight,
        query_bias,
        value_bias,
        proj_weight,
        proj_bias,
        first_gain,
        first_shift,
        expand_weight,
        expand_bias,
        shrink_weight,
        shrink_bias,
        second_gain,
        second_shift,
    )
    mirror_params = (
        key_qkv,
        key_querybias,
        key_valuebias,
        key_proj,
        key_projbias,
        key_firstgain,
        key_firstshift,
        key_expand,
        key_expandbias,
        key_shrink,
        key_shrinkbias,
        key_secondgain,
        key_secondshift,
    )
    num_crops, seq_len, model_width = x_query.shape
    positions = lax.broadcasted_iota(jnp.int32, (num_crops, seq_len), 1)
    valid_query = positions < len_query[:, None]
    valid_key = positions < len_key[:, None]
    updated = tuple(
        (
            momentum * mirror_arr + (1.0 - momentum) * source.astype(jnp.float32)
            for mirror_arr, source in zip(mirror_params, query_params)
        )
    )
    key_hidden = x_key
    key_out = None
    for layer_idx in range(LAYERS):
        weights = gather_mirror(*[member[layer_idx].astype(jnp.bfloat16) for member in updated])
        key_out, unused = layer_forward(key_hidden, valid_key, weights)
        key_hidden = key_out.astype(jnp.bfloat16).reshape(num_crops, seq_len, model_width)
    normalized_key = unit_rows(pool_rows(key_out, valid_key, len_key)).astype(jnp.bfloat16)
    hidden = x_query
    final_out = None
    saved = []
    for layer_idx in range(LAYERS):
        weights = gather_query(*[member[layer_idx] for member in query_params])
        final_out, saved_state = layer_forward(hidden, valid_query, weights)
        saved.append((saved_state, weights))
        hidden = final_out.astype(jnp.bfloat16).reshape(num_crops, seq_len, model_width)
    pooled = pool_rows(final_out, valid_query, len_query)
    normalized_query = unit_rows(pooled).astype(jnp.bfloat16)
    matching_similarity = (
        jnp.sum(normalized_query.astype(jnp.float32) * normalized_key.astype(jnp.float32), -1)
        / contrast_sharpness
    )
    logits = (
        jnp.einsum(
            "cd,kd->ck",
            lax.all_gather(normalized_query, ("dp", "fsdp"), axis=0, tiled=True),
            queue,
            preferred_element_type=jnp.float32,
        )
        / contrast_sharpness
    )
    start_own = lax.axis_index(("dp", "fsdp")) * num_crops
    row_peak = jnp.max(logits, 1)
    own_peak = jnp.maximum(
        lax.dynamic_slice_in_dim(row_peak, start_own, num_crops, 0), matching_similarity
    )
    row_peak = lax.dynamic_update_slice_in_dim(row_peak, own_peak, start_own, 0)
    global_peak = lax.pmax(row_peak, ("dp", "fsdp"))
    own_top = lax.dynamic_slice_in_dim(global_peak, start_own, num_crops, 0)
    exp_sums = jnp.sum(jnp.exp(logits - global_peak[:, None]), 1)
    own_sums = lax.dynamic_slice_in_dim(exp_sums, start_own, num_crops, 0) + jnp.exp(
        matching_similarity - own_top
    )
    exp_sums = lax.dynamic_update_slice_in_dim(exp_sums, own_sums, start_own, 0)
    global_sum = lax.psum(exp_sums, ("dp", "fsdp"))
    own_top = lax.dynamic_slice_in_dim(global_peak, start_own, num_crops, 0)
    own_total = lax.dynamic_slice_in_dim(global_sum, start_own, num_crops, 0)
    crop_losses = own_top + jnp.log(own_total) - matching_similarity
    share_sequence = jnp.exp(logits - global_peak[:, None]) / global_sum[:, None]
    sharpened_similarity = (objective_factor * share_sequence / contrast_sharpness).astype(
        jnp.bfloat16
    )
    normalized_gradient = lax.psum_scatter(
        jnp.dot(sharpened_similarity, queue, preferred_element_type=jnp.float32),
        ("dp", "fsdp"),
        scatter_dimension=0,
        tiled=True,
    )
    device_share = jnp.exp(matching_similarity - own_top) / own_total
    normalized_gradient = normalized_gradient + (
        objective_factor * (device_share - 1.0) / contrast_sharpness
    )[:, None] * normalized_key.astype(jnp.float32)
    unused, unit_back = jax.vjp(unit_rows, pooled)
    grad_pooled = unit_back(normalized_gradient)[0]
    spread_back = (grad_pooled / len_query[:, None].astype(jnp.float32))[:, None, :]
    grad_rows = jnp.where(valid_query[:, :, None], spread_back, 0.0).reshape(
        num_crops * seq_len, model_width
    )
    totals = [None] * LAYERS
    for layer_idx in reversed(range(LAYERS)):
        saved_state, weights = saved[layer_idx]
        layer_slices = [member[layer_idx] for member in query_params]
        weights = (
            lax.all_gather(layer_slices[0], "fsdp", axis=0, tiled=True),
            lax.all_gather(layer_slices[1], "fsdp", axis=0, tiled=True),
            lax.all_gather(layer_slices[2], "fsdp", axis=0, tiled=True),
            lax.all_gather(layer_slices[3], "fsdp", axis=0, tiled=True),
            lax.all_gather(layer_slices[4], "fsdp", axis=0, tiled=True),
            lax.all_gather(layer_slices[5], "fsdp", axis=0, tiled=True),
            lax.all_gather(layer_slices[6], "fsdp", axis=0, tiled=True),
            lax.all_gather(layer_slices[7], "fsdp", axis=0, tiled=True),
            lax.all_gather(layer_slices[8], "fsdp", axis=0, tiled=True),
            lax.all_gather(layer_slices[9], "fsdp", axis=0, tiled=True),
            lax.all_gather(layer_slices[10], "fsdp", axis=0, tiled=True),
            lax.all_gather(layer_slices[11], "fsdp", axis=0, tiled=True),
            lax.all_gather(layer_slices[12], "fsdp", axis=0, tiled=True),
        )
        grad_rows, layer_grads = layer_backward(grad_rows, saved_state, valid_query, weights)
        totals[layer_idx] = sum_grads(*scatter_grads(*layer_grads))
    grad_input = grad_rows.astype(jnp.bfloat16).reshape(num_crops, seq_len, model_width)
    stacked = [
        jnp.stack([totals[layer_idx][member] for layer_idx in range(LAYERS)])
        for member in range(13)
    ]
    return (
        hidden,
        grad_input,
        stacked[0],
        stacked[1],
        stacked[2],
        stacked[3],
        stacked[4],
        stacked[5],
        stacked[6],
        stacked[7],
        stacked[8],
        stacked[9],
        stacked[10],
        stacked[11],
        stacked[12],
        crop_losses,
    )


def solution(mesh):
    in_specs = (
        P(("dp", "fsdp"), None, None),
        P(("dp", "fsdp"), None, None),
        P(("dp", "fsdp")),
        P(("dp", "fsdp")),
        P(("dp", "fsdp"), None),
        P(None, "fsdp", None),
        P(None, "fsdp"),
        P(None, "fsdp"),
        P(None, "fsdp", None),
        P(None, "fsdp"),
        P(None, "fsdp"),
        P(None, "fsdp"),
        P(None, "fsdp", None),
        P(None, "fsdp"),
        P(None, "fsdp", None),
        P(None, "fsdp"),
        P(None, "fsdp"),
        P(None, "fsdp"),
        P(None, "fsdp", None),
        P(None, "fsdp"),
        P(None, "fsdp"),
        P(None, "fsdp", None),
        P(None, "fsdp"),
        P(None, "fsdp"),
        P(None, "fsdp"),
        P(None, "fsdp", None),
        P(None, "fsdp"),
        P(None, "fsdp", None),
        P(None, "fsdp"),
        P(None, "fsdp"),
        P(None, "fsdp"),
    )
    out_specs = (
        P(("dp", "fsdp"), None, None),
        P(("dp", "fsdp"), None, None),
        P(None, "fsdp", None),
        P(None, "fsdp"),
        P(None, "fsdp"),
        P(None, "fsdp", None),
        P(None, "fsdp"),
        P(None, "fsdp"),
        P(None, "fsdp"),
        P(None, "fsdp", None),
        P(None, "fsdp"),
        P(None, "fsdp", None),
        P(None, "fsdp"),
        P(None, "fsdp"),
        P(None, "fsdp"),
        P(("dp", "fsdp")),
    )
    return jax.shard_map(
        on_device, mesh=mesh, in_specs=in_specs, out_specs=out_specs, check_vma=False
    )
```

profile of v0, /device:TPU:11, one launch (start us, length us, event | category | flops | bytes accessed | tf_op | source)
XLA Modules:
  0.0 2211.7 jit_solution(13392310861292853000)
XLA Ops:
  38.9 29.8 %all-reduce.52 = (bf16[768]{0:T(1024)(128)(2,1)S(1)}, bf16[768]{0:T(1024)(128)(2,1)S(1)}, bf16[768]{0:T(1024)(128)(2,1)S(1)}, bf16[768]{0:T(1024)(128)(2,1)S(1)}...) all-reduce(bf16[768]{0:T(1024)(128)(2,1)S(1)} %dynamic-update-slice, ...), channel_id=4, replica_groups=mesh['dp'=4,'fsdp'=8] {'fsdp'}, use_global_device_ids=true, to_apply=%add.1 | all-reduce | flops 24576 | bytes 98304
  78.4 23.4 %all-gather.21 = bf16[1,3072]{1,0:T(2,128)(2,1)S(1)} all-gather(bf16[1,384]{1,0:T(2,128)(2,1)S(1)} %get-tuple-element.208), channel_id=23, replica_groups=mesh['dp'=4,'fsdp'=8] {'fsdp'}, dimensions={1}, use_global_device_ids=true | all-gather | bytes 6912 | tf_op jit(solution)/shard_map/all_gather | solution.py:63
  102.4 21.9 all-gather.47
  124.9 22.3 %all-gather.8 = bf16[1,3072]{1,0:T(2,128)(2,1)S(1)} all-gather(bf16[1,384]{1,0:T(2,128)(2,1)S(1)} %get-tuple-element.209), channel_id=10, replica_groups=mesh['dp'=4,'fsdp'=8] {'fsdp'}, dimensions={1}, use_global_device_ids=true | all-gather | bytes 6912 | tf_op jit(solution)/shard_map/all_gather | solution.py:63
  147.2 21.5 all-gather.34
  168.7 4.1 convolution_bitcast_fusion
  176.4 4.3 fusion.74
  211.8 16.5 all-gather.72.cloned.1.call-done
  231.8 76.6 %all-gather.90.cloned.1.call-done = bf16[1,768,3072]{2,1,0:T(8,128)(2,1)} async-done(((bf16[1,96,3072]{2,1,0:T(8,128)(2,1)}), bf16[1,768,3072]{2,1,0:T(8,128)(2,1)}) %all-gather.90.cloned.1.call-update) | async-done | bytes 4718608 | tf_op jit(solution)/shard_map/all_gather | solution.py:94
  308.5 8.2 fusion.46
  316.7 71.9 %all-gather.92.cloned.1.call-done = bf16[1,3072,768]{2,1,0:T(8,128)(2,1)} async-done(((bf16[1,384,768]{2,1,0:T(8,128)(2,1)}), bf16[1,3072,768]{2,1,0:T(8,128)(2,1)}) %all-gather.92.cloned.1.call-update) | async-done | bytes 4718608 | tf_op jit(solution)/shard_map/all_gather | solution.py:96
  388.6 20.1 fusion.312
  410.1 44.5 %all-gather.94.cloned.1.call-done = bf16[1,768,2304]{2,1,0:T(8,128)(2,1)} async-done(((bf16[1,96,2304]{2,1,0:T(8,128)(2,1)}), bf16[1,768,2304]{2,1,0:T(8,128)(2,1)}) %all-gather.94.cloned.1.call-update) | async-done | bytes 3538960 | tf_op jit(solution)/shard_map/all_gather | solution.py:87
  454.5 4.6 fusion.65
  463.6 3.1 reshape.506
  468.9 2.9 reshape.508
  481.8 14.6 all-gather.96.cloned.1.call-done
  500.7 76.6 %all-gather.74.cloned.1.call-done = bf16[1,768,3072]{2,1,0:T(8,128)(2,1)} async-done(((bf16[1,96,3072]{2,1,0:T(8,128)(2,1)}), bf16[1,768,3072]{2,1,0:T(8,128)(2,1)}) %all-gather.74.cloned.1.call-update) | async-done | bytes 4718608 | tf_op jit(solution)/shard_map/all_gather | solution.py:62
  577.3 19.9 multiply_convert_fusion.3
  597.2 60.2 %all-gather.76.cloned.1.call-done = bf16[1,3072,768]{2,1,0:T(8,128)(2,1)} async-done(((bf16[1,384,768]{2,1,0:T(8,128)(2,1)}), bf16[1,3072,768]{2,1,0:T(8,128)(2,1)}) %all-gather.76.cloned.1.call-update) | async-done | bytes 4718608 | tf_op jit(solution)/shard_map/all_gather | solution.py:64
  657.4 6.0 fusion.306
  665.5 72.1 %all-gather.98.cloned.1.call-done = bf16[1,768,3072]{2,1,0:T(8,128)(2,1)} async-done(((bf16[1,96,3072]{2,1,0:T(8,128)(2,1)}), bf16[1,768,3072]{2,1,0:T(8,128)(2,1)}) %all-gather.98.cloned.1.call-update) | async-done | bytes 4718608 | tf_op jit(solution)/shard_map/all_gather | solution.py:94
  737.6 8.2 fusion.42
  745.8 71.9 %all-gather.100.cloned.1.call-done = bf16[1,3072,768]{2,1,0:T(8,128)(2,1)} async-done(((bf16[1,384,768]{2,1,0:T(8,128)(2,1)}), bf16[1,3072,768]{2,1,0:T(8,128)(2,1)}) %all-gather.100.cloned.1.call-update) | async-done | bytes 4718608 | tf_op jit(solution)/shard_map/all_gather | solution.py:96
  817.8 20.9 fusion.315
  838.7 45.0 %all-gather.78.cloned.1.call-done = bf16[1,768,2304]{2,1,0:T(8,128)(2,1)} async-done(((bf16[1,96,2304]{2,1,0:T(8,128)(2,1)}), bf16[1,768,2304]{2,1,0:T(8,128)(2,1)}) %all-gather.78.cloned.1.call-update) | async-done | bytes 3538960 | tf_op jit(solution)/shard_map/all_gather | solution.py:55
  883.7 4.1 fusion.70
  906.9 18.5 all-gather.80.cloned.1.call-done
  928.6 77.0 %all-gather.82.cloned.1.call-done = bf16[1,768,3072]{2,1,0:T(8,128)(2,1)} async-done(((bf16[1,96,3072]{2,1,0:T(8,128)(2,1)}), bf16[1,768,3072]{2,1,0:T(8,128)(2,1)}) %all-gather.82.cloned.1.call-update) | async-done | bytes 4718608 | tf_op jit(solution)/shard_map/all_gather | solution.py:62
  1005.6 19.9 multiply_convert_fusion.2
  1025.5 60.2 %all-gather.84.cloned.1.call-done = bf16[1,3072,768]{2,1,0:T(8,128)(2,1)} async-done(((bf16[1,384,768]{2,1,0:T(8,128)(2,1)}), bf16[1,3072,768]{2,1,0:T(8,128)(2,1)}) %all-gather.84.cloned.1.call-update) | async-done | bytes 4718608 | tf_op jit(solution)/shard_map/all_gather | solution.py:64
  1085.7 6.6 fusion.309
  1095.1 57.3 %all-gather.52 = bf16[32,2,768]{2,1,0:T(2,128)(2,1)S(1)} all-gather(bf16[1,2,768]{2,1,0:T(2,128)(2,1)S(1)} %bitcast.425), channel_id=1, replica_groups=mesh['dp'=4,'fsdp'=8] {'dp','fsdp'}, dimensions={0}, use_global_device_ids=true | all-gather | bytes 101376 | tf_op jit(solution)/shard_map/all_gather | solution.py:488
  1153.2 47.7 %pmax.7 = f32[64]{0:T(128)S(1)} all-reduce(f32[64]{0:T(128)S(1)} %maximum_dynamic-update-slice_fusion), channel_id=1, replica_groups=mesh['dp'=4,'fsdp'=8] {'dp','fsdp'}, use_global_device_ids=true, to_apply=%region_30.31 | all-reduce | flops 64 | bytes 512 | tf_op jit(solution)/shard_map/pmax | solution.py:500
  1201.2 39.3 %psum.189 = f32[64]{0:T(128)S(1)} all-reduce(f32[64]{0:T(128)S(1)} %add_dynamic-update-slice_fusion), channel_id=1, replica_groups=mesh['dp'=4,'fsdp'=8] {'dp','fsdp'}, use_global_device_ids=true, to_apply=%region_32.33 | all-reduce | flops 64 | bytes 512 | tf_op jit(solution)/shard_map/psum | solution.py:507
  1242.2 123.9 %all-reduce.58.cloned.1.call-done = f32[64,768]{1,0:T(8,128)} async-done(((f32[64,768]{1,0:T(8,128)}), f32[64,768]{1,0:T(8,128)}) %all-reduce.58.cloned.1.call-update) | async-done | bytes 196624
  1369.5 9.8 fusion.321
  1379.3 3.2 multiply_reduce_fusion.3
  1389.2 2.9 reshape.511
  1392.1 5.2 fusion.319
  1408.9 4.1 convolution_convert_fusion.4
  1413.0 5.8 multiply_reduce_fusion.2
  1422.2 9.3 fusion.322
  1431.5 6.6 multiply_reduce_fusion.4
  1443.1 3.1 reshape.515
  1446.1 4.4 fusion.320
  1463.0 3.7 fusion.64
  1466.7 5.8 copy.201
  1475.8 3.1 convolution_convert_fusion.7
  1478.9 6.5 convolution_convert_fusion.2
  1486.6 6.8 convolution_convert_fusion
  1494.8 6.4 convolution_convert_fusion.3
  1502.3 6.7 convolution_convert_fusion.1
  1511.0 29.0 %all-reduce.51 = (bf16[768]{0:T(1024)(128)(2,1)S(1)}, bf16[768]{0:T(1024)(128)(2,1)S(1)}, bf16[768]{0:T(1024)(128)(2,1)S(1)}, bf16[768]{0:T(1024)(128)(2,1)S(1)}...) all-reduce(bf16[768]{0:T(1024)(128)(2,1)S(1)} %reduce_sum.677, ...), channel_id=58, replica_groups=mesh['dp'=4,'fsdp'=8] {'fsdp'}, use_global_device_ids=true, to_apply=%region_53.54.clone | all-reduce | flops 18432 | bytes 73728
  1543.4 41.2 %reduce-scatter.25.cloned.1.call-done = bf16[96,2304]{1,0:T(8,128)(2,1)} async-done(((bf16[768,2304]{1,0:T(8,128)(2,1)}), bf16[96,2304]{1,0:T(8,128)(2,1)}) %reduce-scatter.25.cloned.1.call-update) | async-done | bytes 442384
  1586.7 62.7 %reduce-scatter.15.cloned.1.call-done = bf16[96,768]{1,0:T(8,128)(2,1)} async-done(((bf16[768,768]{1,0:T(8,128)(2,1)}), bf16[96,768]{1,0:T(8,128)(2,1)}) %reduce-scatter.15.cloned.1.call-update) | async-done | bytes 147472 | tf_op jit(solution)/shard_map/reduce_scatter | solution.py:128
  1649.4 66.4 %reduce-scatter.13.cloned.1.call-done = bf16[96,768]{1,0:T(8,128)(2,1)} async-done(((bf16[768,768]{1,0:T(8,128)(2,1)}), bf16[96,768]{1,0:T(8,128)(2,1)}) %reduce-scatter.13.cloned.1.call-update) | async-done | bytes 147472 | tf_op jit(solution)/shard_map/reduce_scatter | solution.py:128
  1715.8 100.0 %reduce-scatter.19.cloned.1.call-done = bf16[96,3072]{1,0:T(8,128)(2,1)} async-done(((bf16[768,3072]{1,0:T(8,128)(2,1)}), bf16[96,3072]{1,0:T(8,128)(2,1)}) %reduce-scatter.19.cloned.1.call-update) | async-done | bytes 589840 | tf_op jit(solution)/shard_map/reduce_scatter | solution.py:140
  1815.9 98.9 %reduce-scatter.23.cloned.1.call-done = bf16[384,768]{1,0:T(8,128)(2,1)} async-done(((bf16[3072,768]{1,0:T(8,128)(2,1)}), bf16[384,768]{1,0:T(8,128)(2,1)}) %reduce-scatter.23.cloned.1.call-update) | async-done | bytes 589840 | tf_op jit(solution)/shard_map/reduce_scatter | solution.py:146
  1914.7 98.7 %reduce-scatter.17.cloned.1.call-done = bf16[96,3072]{1,0:T(8,128)(2,1)} async-done(((bf16[768,3072]{1,0:T(8,128)(2,1)}), bf16[96,3072]{1,0:T(8,128)(2,1)}) %reduce-scatter.17.cloned.1.call-update) | async-done | bytes 589840 | tf_op jit(solution)/shard_map/reduce_scatter | solution.py:140
  2013.4 98.8 %reduce-scatter.21.cloned.1.call-done = bf16[384,768]{1,0:T(8,128)(2,1)} async-done(((bf16[3072,768]{1,0:T(8,128)(2,1)}), bf16[384,768]{1,0:T(8,128)(2,1)}) %reduce-scatter.21.cloned.1.call-update) | async-done | bytes 589840 | tf_op jit(solution)/shard_map/reduce_scatter | solution.py:146
  2112.3 9.8 all-reduce.53
  2127.3 5.7 add_convert_fusion.5
  2133.0 63.2 %all-reduce.60.cloned.1.call-done = (bf16[1,96,2304]{1,2,0:T(8,128)(2,1)}, bf16[1,96,2304]{1,2,0:T(8,128)(2,1)}, bf16[1,96,768]{2,1,0:T(8,128)(2,1)}, bf16[1,96,...) async-done(((bf16[1,96,2304]{1,2,0:T(8,128)(2,1)}, ...) | async-done | bytes 3538960 | tf_op jit(solution)/shard_map/psum | solution.py:177
  (648 shorter events, 199.6 us)
Async XLA Ops:
  7.2 1145.4 %copy-start = (bf16[512,768]{1,0:T(8,128)(2,1)S(1)}, bf16[512,768]{1,0:T(8,128)(2,1)}, u32[]{:S(2)}) copy-start(bf16[512,768]{1,0:T(8,128)(2,1)} %param.35) | copy-start | bytes 2359300
  7.2 161.5 %all-gather.86.cloned.1.call-start = ((), (), s32[]{:S(2)}) async-start(), calls=%async_computation.22 | async-start | bytes 3981312 | tf_op jit(solution)/shard_map/all_gather | solution.py:87
  10.4 166.0 %all-gather.70.cloned.1.call-start = ((), (), s32[]{:S(2)}) async-start(), calls=%async_computation.14 | async-start | bytes 3981312 | tf_op jit(solution)/shard_map/all_gather | solution.py:55
  11.5 190.2 %all-gather.88.cloned.1.call-start = ((), (), s32[]{:S(2)}) async-start(), calls=%async_computation.23 | async-start | bytes 1327104 | tf_op jit(solution)/shard_map/all_gather | solution.py:90
  13.5 214.8 %all-gather.72.cloned.1.call-start = ((), (), s32[]{:S(2)}) async-start(), calls=%async_computation.15 | async-start | bytes 1327104 | tf_op jit(solution)/shard_map/all_gather | solution.py:58
  14.3 294.1 %all-gather.90.cloned.1.call-start = ((), (), s32[]{:S(2)}) async-start(), calls=%async_computation.24 | async-start | bytes 5308416 | tf_op jit(solution)/shard_map/all_gather | solution.py:94
  17.6 370.9 %all-gather.92.cloned.1.call-start = ((), (), s32[]{:S(2)}) async-start(), calls=%async_computation.25 | async-start | bytes 5308416 | tf_op jit(solution)/shard_map/all_gather | solution.py:96
  20.9 433.6 %all-gather.94.cloned.1.call-start = ((), (), s32[]{:S(2)}) async-start(), calls=%async_computation.26 | async-start | bytes 3981312 | tf_op jit(solution)/shard_map/all_gather | solution.py:87
  21.7 474.7 %all-gather.96.cloned.1.call-start = ((), (), s32[]{:S(2)}) async-start(), calls=%async_computation.27 | async-start | bytes 1327104 | tf_op jit(solution)/shard_map/all_gather | solution.py:90
  22.4 554.9 %all-gather.74.cloned.1.call-start = ((), (), s32[]{:S(2)}) async-start(), calls=%async_computation.16 | async-start | bytes 5308416 | tf_op jit(solution)/shard_map/all_gather | solution.py:62
  23.8 145.0 %copy-start.119 = (bf16[2,256,768]{2,1,0:T(8,128)(2,1)S(1)}, bf16[2,256,768]{2,1,0:T(8,128)(2,1)}, u32[]{:S(2)}) copy-start(bf16[2,256,768]{2,1,0:T(8,128)(2,1)} %param.32) | copy-start | bytes 2359300
  23.8 633.6 %all-gather.76.cloned.1.call-start = ((), (), s32[]{:S(2)}) async-start(), calls=%async_computation.17 | async-start | bytes 5308416 | tf_op jit(solution)/shard_map/all_gather | solution.py:64
  25.0 712.7 %all-gather.98.cloned.1.call-start = ((), (), s32[]{:S(2)}) async-start(), calls=%async_computation.28 | async-start | bytes 5308416 | tf_op jit(solution)/shard_map/all_gather | solution.py:94
  25.7 792.0 %all-gather.100.cloned.1.call-start = ((), (), s32[]{:S(2)}) async-start(), calls=%async_computation.29 | async-start | bytes 5308416 | tf_op jit(solution)/shard_map/all_gather | solution.py:96
  26.3 857.4 %all-gather.78.cloned.1.call-start = ((), (), s32[]{:S(2)}) async-start(), calls=%async_computation.18 | async-start | bytes 3981312 | tf_op jit(solution)/shard_map/all_gather | solution.py:55
  27.0 898.4 %all-gather.80.cloned.1.call-start = ((), (), s32[]{:S(2)}) async-start(), calls=%async_computation.19 | async-start | bytes 1327104 | tf_op jit(solution)/shard_map/all_gather | solution.py:58
  27.6 978.0 %all-gather.82.cloned.1.call-start = ((), (), s32[]{:S(2)}) async-start(), calls=%async_computation.20 | async-start | bytes 5308416 | tf_op jit(solution)/shard_map/all_gather | solution.py:62
  28.2 1057.5 %all-gather.84.cloned.1.call-start = ((), (), s32[]{:S(2)}) async-start(), calls=%async_computation.21 | async-start | bytes 5308416 | tf_op jit(solution)/shard_map/all_gather | solution.py:64
  28.8 1337.3 %all-reduce.58.cloned.1.call-start = ((), (), s32[]{:S(2)}) async-start(), calls=%async_computation.32 | async-start | bytes 393216
  29.4 176.1 %copy-start.60 = (pred[2,256]{1,0:T(4,128)(4,1)}, pred[2,256]{1,0:T(4,128)(4,1)S(1)}, u32[]{:S(2)}) copy-start(pred[2,256]{1,0:T(4,128)(4,1)S(1)} %iota_compare_fusion.1) | copy-start | bytes 1540
  30.0 447.3 %copy-start.114 = (pred[2,256]{1,0:T(4,128)(4,1)}, pred[2,256]{1,0:T(4,128)(4,1)S(1)}, u32[]{:S(2)}) copy-start(pred[2,256]{1,0:T(4,128)(4,1)S(1)} %iota_compare_fusion) | copy-start | bytes 1540
  68.8 588.6 %copy-start.73 = (f32[768]{0:T(1024)}, f32[768]{0:T(1024)S(1)}, u32[]{:S(2)}) copy-start(f32[768]{0:T(1024)S(1)} %convert_element_type.811) | copy-start | bytes 9220
  70.0 587.4 %copy-start.92 = (f32[768]{0:T(1024)}, f32[768]{0:T(1024)S(1)}, u32[]{:S(2)}) copy-start(f32[768]{0:T(1024)S(1)} %convert_element_type.812) | copy-start | bytes 9220
  147.2 430.1 %copy-start.78 = (f32[1,3072]{1,0:T(1,128)}, f32[1,3072]{1,0:T(1,128)S(1)}, u32[]{:S(2)}) copy-start(f32[1,3072]{1,0:T(1,128)S(1)} %convert_element_type.777) | copy-start | bytes 36868
  185.5 24.1 %copy-start.29 = (bf16[2,256,12,64]{1,0,3,2:T(2,128)(2,1)}, bf16[2,256,12,64]{1,0,3,2:T(2,128)(2,1)S(1)}, u32[]{:S(2)}) copy-start(bf16[2,256,12,64]{1,0,3,2:T(2,128)(2,1)S(1)} %reshape.491) | copy-start | bytes 2359300
  190.3 15.2 copy-start.7
  193.7 11.8 copy-start.3
  211.8 104.9 %copy-start.39 = (bf16[96,8,2,256]{3,1,2,0:T(8,128)(2,1)}, bf16[96,8,2,256]{3,1,2,0:T(8,128)(2,1)S(1)}, u32[]{:S(2)}) copy-start(bf16[96,8,2,256]{3,1,2,0:T(8,128)(2,1)S(1)} %copy.205) | copy-start | bytes 2359300
  230.7 426.7 %copy-start.13 = (f32[512,768]{1,0:T(8,128)}, f32[512,768]{1,0:T(8,128)S(1)}, u32[]{:S(2)}) copy-start(f32[512,768]{1,0:T(8,128)S(1)} %get-tuple-element.247) | copy-start | bytes 4718596
  230.7 426.7 %copy-start.62 = (f32[512]{0:T(512)}, f32[512]{0:T(512)S(1)}, u32[]{:S(2)}) copy-start(f32[512]{0:T(512)S(1)} %broadcast_multiply_fusion.7) | copy-start | bytes 6148
  231.8 425.6 %copy-start.82 = (f32[512]{0:T(512)}, f32[512]{0:T(512)S(1)}, u32[]{:S(2)}) copy-start(f32[512]{0:T(512)S(1)} %fusion.210) | copy-start | bytes 6148
  577.3 80.1 %copy-start.100 = (f32[768]{0:T(1024)S(1)}, f32[768]{0:T(1024)}, u32[]{:S(2)}) copy-start(f32[768]{0:T(1024)} %convert_element_type.813) | copy-start | bytes 9220
  657.4 80.2 %copy-start.98 = (f32[768]{0:T(1024)S(1)}, f32[768]{0:T(1024)}, u32[]{:S(2)}) copy-start(f32[768]{0:T(1024)} %convert_element_type.836) | copy-start | bytes 9220
  657.4 80.2 %copy-start.99 = (f32[768]{0:T(1024)S(1)}, f32[768]{0:T(1024)}, u32[]{:S(2)}) copy-start(f32[768]{0:T(1024)} %convert_element_type.835) | copy-start | bytes 9220
  665.5 152.2 %copy-start.81 = (f32[1,3072]{1,0:T(1,128)S(1)}, f32[1,3072]{1,0:T(1,128)}, u32[]{:S(2)}) copy-start(f32[1,3072]{1,0:T(1,128)} %convert_element_type.804) | copy-start | bytes 36868
  665.5 152.2 %copy-start.101 = (f32[768]{0:T(1024)S(1)}, f32[768]{0:T(1024)}, u32[]{:S(2)}) copy-start(f32[768]{0:T(1024)} %convert_element_type.837) | copy-start | bytes 9220
  817.7 66.0 %copy-start.22 = (f32[512,768]{1,0:T(8,128)S(1)}, f32[512,768]{1,0:T(8,128)}, u32[]{:S(2)}) copy-start(f32[512,768]{1,0:T(8,128)} %copy-done.21) | copy-start | bytes 4718596
  817.7 66.0 %copy-start.76 = (f32[768]{0:T(1024)S(1)}, f32[768]{0:T(1024)}, u32[]{:S(2)}) copy-start(f32[768]{0:T(1024)} %convert_element_type.814) | copy-start | bytes 9220
  817.7 66.0 %copy-start.95 = (f32[768]{0:T(1024)S(1)}, f32[768]{0:T(1024)}, u32[]{:S(2)}) copy-start(f32[768]{0:T(1024)} %convert_element_type.815) | copy-start | bytes 9220
  838.7 50.1 %copy-start.71 = (f32[768]{0:T(1024)S(1)}, f32[768]{0:T(1024)}, u32[]{:S(2)}) copy-start(f32[768]{0:T(1024)} %convert_element_type.817) | copy-start | bytes 9220
  838.7 50.1 %copy-start.72 = (f32[768]{0:T(1024)S(1)}, f32[768]{0:T(1024)}, u32[]{:S(2)}) copy-start(f32[768]{0:T(1024)} %convert_element_type.816) | copy-start | bytes 9220
  892.7 10.9 copy-start.31
  905.2 20.2 copy-start.97
  906.2 22.1 copy-start.41
  925.5 80.2 %copy-start.75 = (f32[768]{0:T(1024)S(1)}, f32[768]{0:T(1024)}, u32[]{:S(2)}) copy-start(f32[768]{0:T(1024)} %convert_element_type.819) | copy-start | bytes 9220
  925.5 80.2 %copy-start.80 = (f32[1,3072]{1,0:T(1,128)S(1)}, f32[1,3072]{1,0:T(1,128)}, u32[]{:S(2)}) copy-start(f32[1,3072]{1,0:T(1,128)} %convert_element_type.786) | copy-start | bytes 36868
  925.5 80.2 %copy-start.94 = (f32[768]{0:T(1024)S(1)}, f32[768]{0:T(1024)}, u32[]{:S(2)}) copy-start(f32[768]{0:T(1024)} %convert_element_type.820) | copy-start | bytes 9220
  928.3 97.2 %copy-start.18 = (f32[512,768]{1,0:T(8,128)}, f32[512,768]{1,0:T(8,128)S(1)}, u32[]{:S(2)}) copy-start(f32[512,768]{1,0:T(8,128)S(1)} %get-tuple-element.254) | copy-start | bytes 4718596
  1005.6 80.1 %copy-start.96 = (f32[768]{0:T(1024)S(1)}, f32[768]{0:T(1024)}, u32[]{:S(2)}) copy-start(f32[768]{0:T(1024)} %convert_element_type.821) | copy-start | bytes 9220
  1092.6 275.2 %copy-start.103 = (pred[512]{0:T(512)(128)(4,1)S(1)}, pred[512]{0:T(512)(128)(4,1)}, u32[]{:S(2)}) copy-start(pred[512]{0:T(512)(128)(4,1)} %lt.47) | copy-start | bytes 1540
  1241.5 299.8 %reduce-scatter.27.cloned.1.call-start = ((), (), s32[]{:S(2)}) async-start(), calls=%async_computation.31 | async-start | bytes 3981312
  1368.5 10.8 slice-start.4
  1369.4 9.9 copy-start.19
  1369.4 9.9 slice-start.5
  1385.2 12.1 slice-start.2
  1420.6 164.0 %reduce-scatter.25.cloned.1.call-start = ((), (), s32[]{:S(2)}) async-start(), calls=%async_computation.30 | async-start | bytes 3981312
  1472.6 176.9 %reduce-scatter.15.cloned.1.call-start = ((), (), s32[]{:S(2)}) async-start(), calls=%async_computation.9 | async-start | bytes 1327104 | tf_op jit(solution)/shard_map/reduce_scatter | solution.py:128
  1475.7 240.1 %reduce-scatter.13.cloned.1.call-start = ((), (), s32[]{:S(2)}) async-start(), calls=%async_computation.8 | async-start | bytes 1327104 | tf_op jit(solution)/shard_map/reduce_scatter | solution.py:128
  1478.9 337.0 %reduce-scatter.19.cloned.1.call-start = ((), (), s32[]{:S(2)}) async-start(), calls=%async_computation.11 | async-start | bytes 5308416 | tf_op jit(solution)/shard_map/reduce_scatter | solution.py:140
  1485.5 429.2 %reduce-scatter.23.cloned.1.call-start = ((), (), s32[]{:S(2)}) async-start(), calls=%async_computation.13 | async-start | bytes 5308416 | tf_op jit(solution)/shard_map/reduce_scatter | solution.py:146
  1493.4 520.0 %reduce-scatter.17.cloned.1.call-start = ((), (), s32[]{:S(2)}) async-start(), calls=%async_computation.10 | async-start | bytes 5308416 | tf_op jit(solution)/shard_map/reduce_scatter | solution.py:140
  1501.2 611.0 %reduce-scatter.21.cloned.1.call-start = ((), (), s32[]{:S(2)}) async-start(), calls=%async_computation.12 | async-start | bytes 5308416 | tf_op jit(solution)/shard_map/reduce_scatter | solution.py:146
  1509.0 618.2 %copy-start.17 = (f32[512,768]{1,0:T(8,128)S(1)}, f32[512,768]{1,0:T(8,128)}, u32[]{:S(2)}) copy-start(f32[512,768]{1,0:T(8,128)} %copy-done.16) | copy-start | bytes 4718596
  1509.1 687.1 %all-reduce.60.cloned.1.call-start = ((), (), s32[]{:S(2)}) async-start(), calls=%async_computation.33 | async-start | bytes 7667712 | tf_op jit(solution)/shard_map/psum | solution.py:177
  (93 other events, 410.4 us)
Sparse Core Ops, SparseCore 0:
  10.8 66.7 all-gather.85
  80.3 64.1 all-gather.69
  146.7 39.6 all-gather.87
  188.4 39.8 all-gather.71
  230.3 78.0 all-gather.89
  310.5 78.0 all-gather.91
  390.7 63.7 all-gather.93
  456.7 39.6 all-gather.95
  499.2 78.0 all-gather.73
  579.3 78.0 all-gather.75
  659.6 78.0 all-gather.97
  739.7 78.0 all-gather.99
  819.9 63.7 all-gather.77
  885.8 39.6 all-gather.79
  927.5 78.0 all-gather.81
  1007.6 78.0 all-gather.83
  1241.6 124.4 all-reduce.57
  1420.7 80.0 reduce-scatter.26
  1504.4 80.1 reduce-scatter.24
  1587.8 61.5 reduce-scatter.14
  1652.8 62.9 reduce-scatter.12
  1719.5 96.3 reduce-scatter.18
  1819.5 95.1 reduce-scatter.22
  1918.2 95.1 reduce-scatter.16
  2017.0 95.1 reduce-scatter.20
  2116.1 80.0 all-reduce.59
where the time goes:
time: 2220 us; the launch traced here: 2210 us
  waiting for transfers between devices  1460 us (66%)
  blocking collectives  302 us (14%)
  matrix products  252 us (11%)
  local copies, waits for them, and re-layouts  114 us (5%)
  other arithmetic  58.7 us (3%)
    reduce_scatter x2, waiting for transfers between devices, scatter_grads(): lax.psum_scatter(expand_mat.astype(jnp.bfloat16), 'fsdp', scatter_dimensi...  199 us
    reduce_scatter x2, waiting for transfers between devices, scatter_grads(): lax.psum_scatter(shrink_mat.astype(jnp.bfloat16), 'fsdp', scatter_dimensi...  198 us
    unnamed x29, waiting for transfers between devices  170 us
    all_gather x2, waiting for transfers between devices, gather_query(): lax.all_gather(expand_mat, 'fsdp', axis=0, tiled=True)  154 us
    all_gather x2, waiting for transfers between devices, gather_mirror(): lax.all_gather(expand_mat, 'fsdp', axis=0, tiled=True)  149 us
    all_gather x2, waiting for transfers between devices, gather_mirror(): lax.all_gather(shrink_mat, 'fsdp', axis=0, tiled=True)  144 us
    reduce_scatter x2, waiting for transfers between devices, scatter_grads(): lax.psum_scatter(proj_mat.astype(jnp.bfloat16), 'fsdp', scatter_dimension...  129 us
    all_gather x2, waiting for transfers between devices, gather_query(): lax.all_gather(shrink_mat, 'fsdp', axis=0, tiled=True)  120 us
  transfers between devices with their start and end apart: 26, of which 22 were waited for; matrix products, arithmetic and copies ran while one was open for 15% of the time, Pallas kernels for 0%

commit v1 on v0

v1 whole, which is shorter than its diff:
```python
import functools

import jax
import jax.numpy as jnp
from jax import lax
from jax.experimental import pallas as pl
from jax.experimental.pallas import tpu as pltpu
from jax.sharding import PartitionSpec as P

MESH=pl.DeviceIdType.MESH

def coords(D,F):
    d=lax.axis_index("dp"); f=lax.axis_index("fsdp")
    B=F//4
    return d,f,f//B,f%B,(d//2)%2,d%2


def ag_kernel(D,F,L,opt,w,vec,g,vg,lsem,vsem,vrsem,zs,zr,ys,yr,xs,xr,cs,cr,csx,crx):
    A=4;B=F//4
    R=w.shape[1]; T=R//16
    half=T//2; nx=(half*opt['nx'])//36; nyz=half-nx
    d,f,a,b,x,c=coords(D,F)
    h=c*half
    xn=nx*16; yzn=nyz*16
    def rows(t0,n): return pl.ds(pl.multiple_of(t0*16,16),n)
    yzr=rows(h+x*nx,yzn); xsr=rows(h+x*nyz,xn); xrr=rows(h+(1-x)*nyz,xn)
    hc=(1-c)*half
    oyz=rows(hc+x*nx,yzn); oxr=rows(hc+(1-x)*nyz,xn)
    xd=d+2-4*x; cd=d+1-2*c
    bar=pltpu.get_barrier_semaphore()
    for s in range(1,F):
        pl.semaphore_signal(bar,inc=1,device_id=(d,(f+s)%F),device_id_type=MESH)
    pl.semaphore_signal(bar,inc=1,device_id=(xd,f),device_id_type=MESH)
    pl.semaphore_signal(bar,inc=1,device_id=(cd,f),device_id_type=MESH)
    pl.semaphore_wait(bar,F+1)
    def rc(src,dst,ss,rs,dev):
        return pltpu.make_async_remote_copy(src,dst,ss,rs,device_id=dev,device_id_type=MESH)
    def vcopy(s):
        return rc(vec,vg.at[f],vsem.at[s],vrsem.at[s],(d,(f+s)%F))
    for s in range(1,F): vcopy(s).start()
    vl=pltpu.make_async_copy(vec,vg.at[f],vsem.at[0]); vl.start()
    def own(l): return pltpu.make_async_copy(w.at[l],g.at[l,f],lsem.at[l])
    def src_a(hd):
        hh,dr=hd
        return a-hh if dr==0 else a+hh
    def has(hd):
        hh,dr=hd
        return (a>=hh) if dr==0 else (a+hh<A)
    def when(cond,fn):
        if cond is True: fn()
        else: pl.when(cond)(fn)
    def zsend(l,src,hd,fs):
        hh,dr=hd
        na=a+1 if dr==0 else a-1
        return rc(src,g.at[l,fs,yzr],zs.at[l,dr,hh],zr.at[l,dr,hh],(d,na*B+b))
    def canpass(dr): return (a+1<A) if dr==0 else (a>0)
    def zrecv(l,hd):
        fs=src_a(hd)*B+b
        return rc(g.at[l,fs,yzr],g.at[l,fs,yzr],zs.at[l,hd[1],hd[0]],zr.at[l,hd[1],hd[0]],(d,f))
    def slot(hd): return hd[0]*2+hd[1]
    def ycopy(l,src,hd,fs,t): return rc(src,g.at[l,fs,yzr],ys.at[l,slot(hd),t],yr.at[l,slot(hd),t],(d,a*B+(b+t)%B))
    def yrecv(l,hd,t):
        fs=src_a(hd)*B+(b-t)%B
        return fs,rc(g.at[l,fs,yzr],g.at[l,fs,yzr],ys.at[l,slot(hd),t],yr.at[l,slot(hd),t],(d,f))
    def xcopy(l,fs,i): return rc(g.at[l,fs,xsr],g.at[l,fs,xsr],xs.at[l,i],xr.at[l,i],(xd,f))
    def xrecv(l,fs,i): return rc(g.at[l,fs,xrr],g.at[l,fs,xrr],xs.at[l,i],xr.at[l,i],(xd,f))
    def ccopy(l,fs,i): return rc(g.at[l,fs,yzr],g.at[l,fs,yzr],cs.at[l,i],cr.at[l,i],(cd,f))
    def cxcopy(l,fs,i): return rc(g.at[l,fs,xrr],g.at[l,fs,xrr],csx.at[l,i],crx.at[l,i],(cd,f))
    def crecv(l,fs,i): return rc(g.at[l,fs,oyz],g.at[l,fs,oyz],cs.at[l,i],cr.at[l,i],(cd,f))
    def cxrecv(l,fs,i): return rc(g.at[l,fs,oxr],g.at[l,fs,oxr],csx.at[l,i],crx.at[l,i],(cd,f))
    OWN=(0,0)
    def start(l):
        for dr in (0,1): when(canpass(dr),lambda dr=dr: zsend(l,w.at[l,yzr],(1,dr),f).start())
        for t in range(1,B): ycopy(l,w.at[l,yzr],OWN,f,t).start()
        own(l).start()
    def handle_z(l,hh):
        for dr in (0,1):
            hd=(hh,dr)
            def go(hd=hd,dr=dr):
                fs=src_a(hd)*B+b
                zrecv(l,hd).wait_recv()
                if hh+1<A:
                    when(canpass(dr),lambda: zsend(l,g.at[l,fs,yzr],(hh+1,dr),fs).start())
                for t in range(1,B): ycopy(l,g.at[l,fs,yzr],hd,fs,t).start()
                xcopy(l,fs,slot(hd)*B).start()
                ccopy(l,fs,slot(hd)*B).start()
            pl.when(has(hd))(go)
    def hds(hh): return [(0,0)] if hh==0 else [(hh,0),(hh,1)]
    def handle_y(l,hh):
        for hd in hds(hh):
            for t in range(1,B):
                def go(hd=hd,t=t):
                    fs,r=yrecv(l,hd,t); r.wait_recv()
                    xcopy(l,fs,slot(hd)*B+t).start()
                    ccopy(l,fs,slot(hd)*B+t).start()
                when(True if hh==0 else has(hd),go)
    def each_foreign(fn):
        for hh in range(A):
            for hd in hds(hh):
                for t in range(B):
                    if hh==0 and t==0: continue
                    def go(hd=hd,t=t): fn(src_a(hd)*B+(b-t)%B,slot(hd)*B+t)
                    when(True if hh==0 else has(hd),go)
    def xphase(l):
        def go(fs,i):
            xrecv(l,fs,i).wait_recv(); cxcopy(l,fs,i).start()
        each_foreign(go)
    start(0)
    for l in range(L):
        for hh in range(1,A):
            if hh==opt['pre'] and l+1<L: start(l+1)
            handle_z(l,hh)
            handle_y(l,hh-1)
            if hh==1 and l: xphase(l-1)
        if opt['pre']==A and l+1<L: start(l+1)
        handle_y(l,A-1)
    xphase(L-1)
    for l in range(L):
        def go(fs,i):
            crecv(l,fs,i).wait_recv(); cxrecv(l,fs,i).wait_recv()
            xcopy(l,fs,i).wait_send(); ccopy(l,fs,i).wait_send(); cxcopy(l,fs,i).wait_send()
        each_foreign(go)
        for dr in (0,1):
            for hh in range(1,A):
                cond=canpass(dr)
                if hh>1: cond=jnp.logical_and(cond,has((hh-1,dr)))
                pl.when(cond)(lambda hh=hh,dr=dr: zsend(l,w.at[l,yzr],(hh,dr),f).wait_send())
        for hh in range(A):
            for hd in hds(hh):
                for t in range(1,B):
                    when(True if hh==0 else has(hd),lambda hd=hd,t=t: ycopy(l,w.at[l,yzr],hd,f,t).wait_send())
        own(l).wait()
    vl.wait()
    for s in range(1,F):
        vcopy(s).wait_send()
        rc(vec,vg.at[f],vsem.at[s],vrsem.at[s],(d,f)).wait_recv()

def all_gather(D,F,w,vec,cid=1,opt=None):
    L,R,C=w.shape
    A=4;B=F//4
    S=pltpu.SemaphoreType.DMA
    N=2*A*B
    return pl.pallas_call(functools.partial(ag_kernel,D,F,L,opt),
        out_shape=(jax.ShapeDtypeStruct((L,F,R,C),w.dtype),jax.ShapeDtypeStruct((F,)+vec.shape,vec.dtype)),
        in_specs=[pl.BlockSpec(memory_space=pl.ANY)]*2,out_specs=[pl.BlockSpec(memory_space=pl.ANY)]*2,
        scratch_shapes=[S((L,)),S((F,)),S((F,)),S((L,2,A)),S((L,2,A)),S((L,2*A,B)),S((L,2*A,B))]+[S((L,N))]*6,
        compiler_params=pltpu.CompilerParams(collective_id=cid,has_side_effects=True),name="gather_weights")(w,vec)
f32=jnp.float32; bf16=jnp.bfloat16
HEADS=12
def dot(a,b): return lax.dot_general(a,b,(((1,),(0,)),((),())),preferred_element_type=f32)
def dot_t(a,b): return lax.dot_general(a,b,(((1,),(1,)),((),())),preferred_element_type=f32)
def tdot(a,b): return lax.dot_general(a,b,(((0,),(0,)),((),())),preferred_element_type=f32)

def phi_parts(u):
    z=jnp.abs(u)*0.7071067811865476
    t=1.0/(1.0+0.3275911*z)
    e=jnp.exp(-z*z)
    poly=t*(0.254829592+t*(-0.284496736+t*(1.421413741+t*(-1.453152027+t*1.061405429))))
    half=0.5*poly*e
    cdf=jnp.where(u>=0,1.0-half,half)
    return cdf,e*0.3989422804014327

def load_weights(l,g,wv,sv,sem):
    F=g.shape[1]; r=768//F; rs=3072//F
    cps=[]
    for j in range(8):
        cps.append(pltpu.make_async_copy(g.at[l,:,pl.ds(j*r,r),:],wv.at[j],sem.at[j]))
    for j in range(4):
        cps.append(pltpu.make_async_copy(g.at[l,pl.ds(j*(F//4),F//4),pl.ds(8*r,rs),:],sv.at[j],sem.at[8+j]))
    return cps

def fwd_kernel(l,save,lens,x,vec,g,*rest):
    if save:
        (y,pooled,qkv_o,pb_o,ctx_o,xh1_o,rs1_o,h1_o,act_o,der_o,xh2_o,rs2_o,
         wv,sv,qkv,pb,ctx,xh1,rs1,h1,act,der,xh2,rs2,acc,sem,osem)=rest
    else:
        (y,pooled,wv,sv,qkv,ctx,xh1,h1,acc,sem)=rest
    cps=load_weights(l,g,wv,sv,sem)
    for c in cps: c.start()
    outs=[]
    def out(i,src,dst):
        if save:
            cp=pltpu.make_async_copy(src,dst,osem.at[i]); cp.start(); outs.append(cp)
    def W(j): return wv[j].reshape(768,768)
    def S(j): return sv[j].reshape(768,768)
    NR=512
    for j in range(3):
        cps[j].wait()
        r=dot(x[...],W(j))
        if j==0: r=r+vec[0:1,:]
        if j==2: r=r+vec[1:2,:]
        qkv[:,j*768:(j+1)*768]=r.astype(bf16)
    if save: out(0,qkv,qkv_o)
    lane=lax.broadcasted_iota(jnp.int32,(256,128),1)
    low_half=lane<64
    kpos=lax.broadcasted_iota(jnp.int32,(256,256),1)
    def pair(i,_):
        c=i//6; p=i-c*6
        rows=pl.ds(pl.multiple_of(c*256,256),256)
        o=pl.multiple_of(p*128,128)
        q2=qkv[rows,pl.ds(o,128)]*jnp.asarray(0.125,bf16)
        k2=qkv[rows,pl.ds(pl.multiple_of(768+o,128),128)]
        v2=qkv[rows,pl.ds(pl.multiple_of(1536+o,128),128)]
        ok=kpos<lens[c]
        res=[]
        for hh in range(2):
            qm=jnp.where(low_half if hh==0 else jnp.logical_not(low_half),q2,jnp.zeros_like(q2))
            s=jnp.where(ok,dot_t(qm,k2),-1e9)
            m=jnp.max(s,-1,keepdims=True)
            e=jnp.exp(s-m)
            pr=(e*(1.0/jnp.sum(e,-1,keepdims=True))).astype(bf16)
            if save: pb[i*2+hh]=pr
            res.append(dot(pr,v2))
        ctx[rows,pl.ds(o,128)]=jnp.where(low_half,res[0],res[1]).astype(bf16)
        return 0
    lax.fori_loop(0,12,pair,0,unroll=3)
    if save: out(1,pb,pb_o); out(2,ctx,ctx_o)
    cps[3].wait()
    def ln(z,gain,shift):
        mu=jnp.mean(z,-1,keepdims=True); cz=z-mu
        rstd=lax.rsqrt(jnp.mean(cz*cz,-1,keepdims=True)+1e-12)
        xh=cz*rstd
        return xh,rstd,xh*gain+shift
    z=dot(ctx[...],W(3))+vec[2:3,:]+x[...].astype(f32)
    xh,rstd,h=ln(z,vec[3:4,:],vec[4:5,:])
    if save:
        xh1[...]=xh; rs1[...]=jnp.broadcast_to(rstd,(NR,128)); out(3,xh1,xh1_o); out(4,rs1,rs1_o)
    h1[...]=h.astype(bf16)
    acc[...]=h+vec[5:6,:]
    if save: out(5,h1,h1_o)
    for j in range(4):
        cps[4+j].wait(); cps[8+j].wait()
        u=dot(h1[...],W(4+j))+vec[8+j:9+j,:]
        cdf,pdf=phi_parts(u)
        gb=(u*cdf).astype(bf16)
        if save:
            act[:,j*768:(j+1)*768]=gb
            der[:,j*768:(j+1)*768]=(cdf+u*pdf).astype(bf16)
        acc[...]+=dot(gb,S(j))
    if save: out(6,act,act_o); out(7,der,der_o)
    xh,rstd,yy=ln(acc[...],vec[6:7,:],vec[7:8,:])
    if save:
        xh2[...]=xh; rs2[...]=jnp.broadcast_to(rstd,(NR,128)); out(8,xh2,xh2_o); out(9,rs2,rs2_o)
    y[...]=yy.astype(bf16)
    tpos=lax.broadcasted_iota(jnp.int32,(256,768),0)
    for c in range(2):
        pooled[c:c+1,:]=jnp.sum(jnp.where(tpos<lens[c],yy[c*256:(c+1)*256],0.0),0,keepdims=True)/lens[c].astype(f32)
    for cp in outs: cp.wait()

def layer_fwd(l,save,lens,x,vec,g):
    F=g.shape[1]
    sd=jax.ShapeDtypeStruct
    V=pl.BlockSpec(memory_space=pltpu.VMEM); ANY=pl.BlockSpec(memory_space=pl.ANY)
    saved=[sd((512,2304),bf16),sd((24,256,256),bf16),sd((512,768),bf16),sd((512,768),f32),sd((512,128),f32),sd((512,768),bf16),sd((512,3072),bf16),sd((512,3072),bf16),sd((512,768),f32),sd((512,128),f32)]
    outs=[sd((512,768),bf16),sd((2,768),f32)]+(saved if save else [])
    wscr=[pltpu.VMEM((8,F,768//F,768),bf16),pltpu.VMEM((4,F//4,3072//F,768),bf16)]
    if save: scr=wscr+[pltpu.VMEM(s.shape,s.dtype) for s in saved]+[pltpu.VMEM((512,768),f32),pltpu.SemaphoreType.DMA((12,)),pltpu.SemaphoreType.DMA((10,))]
    else: scr=wscr+[pltpu.VMEM((512,2304),bf16),pltpu.VMEM((512,768),bf16),pltpu.VMEM((512,768),f32),pltpu.VMEM((512,768),bf16),pltpu.VMEM((512,768),f32),pltpu.SemaphoreType.DMA((12,))]
    return pl.pallas_call(functools.partial(fwd_kernel,l,save),out_shape=outs,
        in_specs=[pl.BlockSpec(memory_space=pltpu.SMEM),V,V,ANY],out_specs=[V,V]+([ANY]*10 if save else []),
        scratch_shapes=scr,compiler_params=pltpu.CompilerParams(vmem_limit_bytes=60<<20),name="layer_fwd")(lens,x,vec,g)
def bwd_kernel(l,first,lens,dyin,x,vec,g,qkv_i,pb_i,ctx_i,xh1_i,rs1_i,h1_i,act_i,der_i,xh2_i,rs2_i,
               dx,dg,vg,wv,sv,qkv,pb,ctx,xh1,rs1,h1,act,der,xh2,rs2,dmix,dacc,dr2,dctx,dv,ds,sem,isem,osem):
    F=g.shape[1]; r=768//F; rs_=3072//F
    cps=load_weights(l,g,wv,sv,sem)
    ins=[pltpu.make_async_copy(s,d,isem.at[i]) for i,(s,d) in enumerate([(qkv_i,qkv),(pb_i,pb),(ctx_i,ctx),(xh1_i,xh1),(rs1_i,rs1),(h1_i,h1),(act_i,act),(der_i,der),(xh2_i,xh2),(rs2_i,rs2)])]
    QKV,PB,CTX,XH1,RS1,H1,ACT,DER,XH2,RS2=range(10)
    for i in (XH2,RS2): ins[i].start()
    for j in range(4):
        cps[8+j].start()
        if j==0: ins[ACT].start(); ins[DER].start(); ins[H1].start()
        cps[4+j].start()
    for i in (XH1,RS1,CTX): ins[i].start()
    cps[3].start(); ins[QKV].start(); ins[PB].start()
    for j in range(3): cps[j].start()
    def W(j): return wv[j].reshape(768,768)
    def S(j): return sv[j].reshape(768,768)
    outs=[]
    def outw(j,val):
        if j<8:
            dv[j]=val.astype(bf16).reshape(F,r,768)
            cp=pltpu.make_async_copy(dv.at[j],dg.at[:,pl.ds(j*r,r),:],osem.at[j])
        else:
            q=j-8
            ds[q]=val.astype(bf16).reshape(F//4,rs_,768)
            cp=pltpu.make_async_copy(ds.at[q],dg.at[pl.ds(q*(F//4),F//4),pl.ds(8*r,rs_),:],osem.at[j])
        cp.start(); outs.append(cp)
    vg[...]=jnp.zeros_like(vg)
    tpos=lax.broadcasted_iota(jnp.int32,(256,768),0)
    if first:
        dy=jnp.concatenate([jnp.where(tpos<lens[c],dyin[c:c+1,:],0.0) for c in range(2)],0)
    else: dy=dyin[...]
    def ln_back(dy,xh,rstd,gain):
        t=dy*gain
        return rstd*(t-jnp.mean(t,-1,keepdims=True)-xh*jnp.mean(t*xh,-1,keepdims=True))
    def colsum(v): return jnp.sum(v,0,keepdims=True)
    ins[XH2].wait(); ins[RS2].wait()
    xh=xh2[...]
    vg[6:7,:]=colsum(dy*xh); vg[7:8,:]=colsum(dy)
    d2=ln_back(dy,xh,rs2[:,0:1],vec[6:7,:])
    dacc[...]=d2
    dfb=d2.astype(bf16)
    dr2[...]=dfb
    vg[5:6,:]=colsum(dfb.astype(f32))
    for i in (ACT,DER,H1): ins[i].wait()
    for j in range(4):
        cps[8+j].wait(); cps[4+j].wait()
        a=act[:,j*768:(j+1)*768]
        outw(8+j,tdot(a,dr2[...]))
        du=(dot_t(dr2[...],S(j))*der[:,j*768:(j+1)*768].astype(f32)).astype(bf16)
        vg[8+j:9+j,:]=colsum(du.astype(f32))
        outw(4+j,tdot(h1[...],du))
        dacc[...]+=dot_t(du,W(4+j))
    for i in (XH1,RS1,CTX): ins[i].wait()
    dh=dacc[...]; xh=xh1[...]
    vg[3:4,:]=colsum(dh*xh); vg[4:5,:]=colsum(dh)
    d1=ln_back(dh,xh,rs1[:,0:1],vec[3:4,:])
    dacc[...]=d1
    dr2[...]=d1.astype(bf16)
    vg[2:3,:]=colsum(dr2[...].astype(f32))
    cps[3].wait()
    outw(3,tdot(ctx[...],dr2[...]))
    dctx[...]=dot_t(dr2[...],W(3)).astype(bf16)
    ins[QKV].wait(); ins[PB].wait()
    lane=lax.broadcasted_iota(jnp.int32,(256,128),1); low_half=lane<64
    def pair(i,_):
        c=i//6; p=i-c*6
        rows=pl.ds(pl.multiple_of(c*256,256),256); o=pl.multiple_of(p*128,128)
        o1=pl.multiple_of(768+o,128); o2=pl.multiple_of(1536+o,128)
        q2=qkv[rows,pl.ds(o,128)]; k2=qkv[rows,pl.ds(o1,128)]; v2=qkv[rows,pl.ds(o2,128)]
        dc=dctx[rows,pl.ds(o,128)]
        res=[]
        for hh in range(2):
            m=low_half if hh==0 else jnp.logical_not(low_half)
            P=pb[i*2+hh]; pf=P.astype(f32)
            dP=dot_t(jnp.where(m,dc,jnp.zeros_like(dc)),v2)
            pd=pf*dP
            dS=(pd-pf*jnp.sum(pd,-1,keepdims=True)).astype(bf16)
            res.append((dot(dS,k2),tdot(dS,q2),tdot(P,dc)))
        sel=lambda t: jnp.where(low_half,res[0][t],res[1][t])
        dmix[rows,pl.ds(o,128)]=(sel(0)*0.125).astype(bf16)
        dmix[rows,pl.ds(o1,128)]=(sel(1)*0.125).astype(bf16)
        dmix[rows,pl.ds(o2,128)]=sel(2).astype(bf16)
        return 0
    lax.fori_loop(0,12,pair,0,unroll=3)
    for j in range(3):
        cps[j].wait()
        dm=dmix[:,j*768:(j+1)*768]
        if j==0: vg[0:1,:]=colsum(dm.astype(f32))
        if j==2: vg[1:2,:]=colsum(dm.astype(f32))
        outw(j,tdot(x[...],dm))
        dacc[...]+=dot_t(dm,W(j))
    dx[...]=dacc[...].astype(dx.dtype)
    for c in outs: c.wait()

def layer_bwd(l,first,lens,dy,x,vec,g,saved,dxt):
    F=g.shape[1]; sd=jax.ShapeDtypeStruct
    V=pl.BlockSpec(memory_space=pltpu.VMEM); ANY=pl.BlockSpec(memory_space=pl.ANY)
    S=pltpu.SemaphoreType.DMA
    w=[pltpu.VMEM((8,F,768//F,768),bf16),pltpu.VMEM((4,F//4,3072//F,768),bf16)]
    scr=w+[pltpu.VMEM(s.shape,s.dtype) for s in saved]+[pltpu.VMEM((512,2304),bf16),pltpu.VMEM((512,768),f32),pltpu.VMEM((512,768),bf16),pltpu.VMEM((512,768),bf16)]+w+[S((12,)),S((10,)),S((12,))]
    return pl.pallas_call(functools.partial(bwd_kernel,l,first),out_shape=[sd((512,768),dxt),sd((F,12*768//F,768),bf16),sd((16,768),f32)],
        in_specs=[pl.BlockSpec(memory_space=pltpu.SMEM),V,V,V]+[ANY]*11,out_specs=[V,ANY,V],scratch_shapes=scr,
        compiler_params=pltpu.CompilerParams(vmem_limit_bytes=61<<20),name="layer_bwd")(lens,dy,x,vec,g,*saved)

def sizes(F):
    n=4*(768//F); np_=n//3; nq=n-np_
    return n,np_,nq
def rs_scratch(D,F,NP):
    A=4;B=F//4;O=D//4; n,np_,nq=sizes(F); nh=n//2; Sm=pltpu.SemaphoreType.DMA
    V=pltpu.VMEM
    return dict(T=V((NP,F,n,384),bf16),RC=V((NP,F,n,384),bf16),RPX=V((NP,F,np_//2,384),bf16),RPY=V((NP,B-1,A,np_//2,384),bf16),
      RQY=V((NP,B-1,A,nq,384),bf16),RQX=V((NP,A,nq//2,384),bf16),T3=V((NP,A,nh,384),bf16),RZ=V((NP,A-1,nh,384),bf16),
      **(dict(RO=V((NP,O-1,nh,384),bf16),TO=V((NP,nh,384),bf16)) if O>1 else {}),
      VS=V((5,32,768),f32),VRC=V((1,32,768),f32),VRX=V((1,32,768),f32),VRY=V((B-1,32,768),f32),VRZ=V((A-1,32,768),f32),
      **(dict(VRO=V((O-1,32,768),f32)) if O>1 else {}),
      LS=Sm((NP,)),SS=Sm((NP,8+B+A+B+A+O,)),RS=Sm((NP,8+B+A+B+A+O)),VSS=Sm((8+B+A+O,)),VRS=Sm((8+B+A+O,)))
class Reduce:
    def __init__(self,D,F,src,fin,vin,vout,buf):
        self.D,self.F=D,F; self.A=4; self.B=F//4; self.O=D//4
        d=lax.axis_index("dp"); f=lax.axis_index("fsdp")
        self.d,self.f=d,f; self.a=f//self.B; self.b=f%self.B; self.x=(d//2)%2; self.c=d%2; self.o=d//4
        self.xd=d+2-4*self.x; self.cd=d+1-2*self.c
        self.src,self.fin,self.vin,self.vout=src,fin,vin,vout
        self.__dict__.update(buf); self.n,self.np,self.nq=sizes(F)
        self.hp=self.np//2; self.hq=self.nq//2
        self.pending=[]
        m=pl.multiple_of
        self.mycols=pl.ds(m(self.c*384,128),384); self.ocols=pl.ds(m((1-self.c)*384,128),384)
        self.Pown=pl.ds(m(self.x*self.hp,16),self.hp); self.Poth=pl.ds(m((1-self.x)*self.hp,16),self.hp)
        self.Qown=pl.ds(m(self.np+self.x*self.hq,16),self.hq); self.Qoth=pl.ds(m(self.np+(1-self.x)*self.hq,16),self.hq)
        self.Qall=pl.ds(self.np,self.nq)
    def peers(self):
        out=[(self.d,(self.f+s)%self.F) for s in range(1,self.F)]
        out+=[(self.xd,self.f),(self.cd,self.f)]+[((self.d+4*s)%self.D,self.f) for s in range(1,self.O)]
        return out
    def rc(self,i,k,src,dst,dev):
        cp=pltpu.make_async_remote_copy(src,dst,self.SS.at[i,k],self.RS.at[i,k],device_id=dev,device_id_type=MESH)
        return cp
    def go(self,cp): cp.start(); self.pending.append(cp)
    def kPy(self,t): return 8+t
    def kQy(self,t): return 8+self.B+t
    def kZ(self,s): return 8+2*self.B+s
    def kO(self,s): return 8+2*self.B+self.A+s
    def Yd(self,t): return (self.d,self.a*self.B+(self.b+t)%self.B)
    def Zd(self,s): return (self.d,((self.a+s)%self.A)*self.B+self.b)
    def s0(self,i):
        s=self.src(i)
        self.cC=lambda i: self.rc(i,0,self.src(i).at[:,:,self.ocols],self.RC.at[i],(self.cd,self.f))
        self.go(self.cC(i))
        self.lc=lambda i: pltpu.make_async_copy(self.src(i).at[:,:,self.mycols],self.T.at[i],self.LS.at[i])
        self.lc(i).start()
    def s1(self,i):
        self.lc(i).wait(); self.cC(i).wait_recv()
        T,RC=self.T,self.RC
        def body(f,_):
            T[i,f]=(T[i,f].astype(f32)+RC[i,f].astype(f32)).astype(bf16); return 0
        lax.fori_loop(0,self.F,body,0)
        self.go(self.cPx(i))
        for t in range(1,self.B):
            for a in range(self.A): pass
        for t in range(1,self.B):
            fb=(self.b+t)%self.B
            for a in range(self.A):
                pass
        self.startQy(i)
    def cPx(self,i): return self.rc(i,1,self.T.at[i,:,self.Poth],self.RPX.at[i],(self.xd,self.f))
    def Tab(self,i):
        return self.T.at[i].reshape(self.A,self.B,self.n,384)
    def cQy(self,i,t): return self.rc(i,self.kQy(t),self.Tab(i).at[:,(self.b+t)%self.B,self.Qall],self.RQY.at[i,t-1],self.Yd(t))
    def cPy(self,i,t): return self.rc(i,self.kPy(t),self.Tab(i).at[:,(self.b+t)%self.B,self.Pown],self.RPY.at[i,t-1],self.Yd(t))
    def startQy(self,i):
        for t in range(1,self.B): self.go(self.cQy(i,t))
    def s2(self,i):
        T=self.T
        self.cPx(i).wait_recv()
        def body(f,_):
            T[i,f,self.Pown]=(T[i,f,self.Pown].astype(f32)+self.RPX[i,f].astype(f32)).astype(bf16); return 0
        lax.fori_loop(0,self.F,body,0)
        for t in range(1,self.B): self.go(self.cPy(i,t))
        for t in range(1,self.B): self.cQy(i,t).wait_recv()
        def bodyq(a,_):
            fo=a*self.B+self.b
            v=T[i,fo,self.Qall].astype(f32)
            for t in range(1,self.B): v=v+self.RQY[i,t-1,a].astype(f32)
            T[i,fo,self.Qall]=v.astype(bf16); return 0
        lax.fori_loop(0,self.A,bodyq,0)
        self.go(self.cQx(i))
    def cQx(self,i): return self.rc(i,2,self.Tab(i).at[:,self.b,self.Qoth],self.RQX.at[i],(self.xd,self.f))
    def s3(self,i):
        for t in range(1,self.B): self.cPy(i,t).wait_recv()
        self.cQx(i).wait_recv()
        def body(a,_):
            fo=a*self.B+self.b
            v=self.T[i,fo,self.Pown].astype(f32)
            for t in range(1,self.B): v=v+self.RPY[i,t-1,a].astype(f32)
            self.T3[i,a,0:self.hp]=v.astype(bf16)
            self.T3[i,a,self.hp:self.hp+self.hq]=(self.T[i,fo,self.Qown].astype(f32)+self.RQX[i,a].astype(f32)).astype(bf16)
            return 0
        lax.fori_loop(0,self.A,body,0)
        for s in range(1,self.A): self.go(self.cZ(i,s))
    def cZ(self,i,s): return self.rc(i,self.kZ(s),self.T3.at[i,(self.a+s)%self.A],self.RZ.at[i,s-1],self.Zd(s))
    def cO(self,i,s): return self.rc(i,self.kO(s),self.TO.at[i],self.RO.at[i,s-1],((self.d+4*s)%self.D,self.f))
    def put(self,i,v):
        v=v.astype(bf16)
        self.fin[i,self.Pown,self.mycols]=v[:self.hp]; self.fin[i,self.Qown,self.mycols]=v[self.hp:]
        self.go(self.cFX(i,0)); self.go(self.cFX(i,1))
    def cFX(self,i,w):
        r=(self.Pown,self.Qown)[w]; v=self.fin.at[i,r,self.mycols]
        return self.rc(i,3+w,v,v,(self.xd,self.f))
    def rFX(self,i,w):
        r=(self.Poth,self.Qoth)[w]; v=self.fin.at[i,r,self.mycols]
        return self.rc(i,3+w,v,v,(self.xd,self.f))
    def s4(self,i):
        v=self.T3[i,self.a].astype(f32)
        for s in range(1,self.A):
            self.cZ(i,s).wait_recv()
            v=v+self.RZ[i,s-1].astype(f32)
        if self.O>1:
            self.TO[i]=v.astype(bf16)
            for s in range(1,self.O): self.go(self.cO(i,s))
            for s in range(1,self.O):
                self.cO(i,s).wait_recv(); v=v+self.RO[i,s-1].astype(f32)
        self.put(i,v)
    def s5(self,i):
        for w in (0,1): self.rFX(i,w).wait_recv()
        v=self.fin.at[i,:,self.mycols]; self.go(self.rc(i,5,v,v,(self.cd,self.f)))
    def s6(self,i):
        v=self.fin.at[i,:,self.ocols]; self.rc(i,5,v,v,(self.cd,self.f)).wait_recv()
    def vstage(self,k):
        st=[(self.VRC,[(self.cd,self.f)],0),(self.VRX,[(self.xd,self.f)],1),(self.VRY,[self.Yd(t) for t in range(1,self.B)],8),(self.VRZ,[self.Zd(s) for s in range(1,self.A)],8+self.B)]
        if self.O>1: st.append((self.VRO,[((self.d+4*s)%self.D,self.f) for s in range(1,self.O)],8+self.B+self.A))
        def cps(k):
            buf,devs,k0=st[k]
            return [pltpu.make_async_remote_copy(self.VS.at[k],buf.at[q],self.VSS.at[k0+q],self.VRS.at[k0+q],device_id=dv,device_id_type=MESH) for q,dv in enumerate(devs)]
        if k==0: self.VS[0]=self.vin[...]
        elif k<=len(st):
            v=self.VS[k-1]
            for q,cp in enumerate(cps(k-1)):
                cp.wait_recv(); v=v+st[k-1][0][q]
            if k<len(st): self.VS[k]=v
            else: self.vout[...]=v
        if k<len(st):
            for cp in cps(k): self.go(cp)
    def finish(self):
        for cp in self.pending: cp.wait_send()

def rs_kernel(D,F,names,dgs,vin,fin,vout,*scr):
    buf=dict(zip(names,scr))
    n=4*(768//F)
    NP=3*len(dgs)
    src=lambda i: dgs[i//3].at[:,pl.ds((2-i%3)*n,n),:]
    R=Reduce(D,F,src,fin,vin,vout,buf)
    bar=pltpu.get_barrier_semaphore(); ps=R.peers()
    for p in ps: pl.semaphore_signal(bar,inc=1,device_id=p,device_id_type=MESH)
    pl.semaphore_wait(bar,len(ps))
    stages=[R.s0,R.s1,R.s2,R.s3,R.s4,R.s5,R.s6]
    for t in range(NP+6):
        if t<6: R.vstage(t)
        for i in range(NP):
            if 0<=t-i<=6: stages[t-i](i)
    R.finish()

def reduce_grads(D,F,dgs,vin,cid):
    n,np_,nq=sizes(F); NP=3*len(dgs)
    buf=rs_scratch(D,F,NP); sd=jax.ShapeDtypeStruct
    V=pl.BlockSpec(memory_space=pltpu.VMEM); ANY=pl.BlockSpec(memory_space=pl.ANY)
    def k(*refs):
        nd=len(dgs)
        rs_kernel(D,F,list(buf),refs[:nd],refs[nd],refs[nd+1],refs[nd+2],*refs[nd+3:])
    return pl.pallas_call(k,out_shape=[sd((NP,n,768),bf16),sd((32,768),f32)],in_specs=[ANY]*len(dgs)+[V],out_specs=[V,V],
        scratch_shapes=list(buf.values()),compiler_params=pltpu.CompilerParams(collective_id=cid,has_side_effects=True,vmem_limit_bytes=61<<20),name="reduce_grads")(*dgs,vin)

contrast_sharpness = 0.05
objective_factor = 512.0
momentum = 0.9995
unit_eps = 1e-06


def unit_rows(pooled):
    return pooled * lax.rsqrt(jnp.sum(pooled * pooled, -1, keepdims=True) + unit_eps)


def pack_mats(qkv, proj, expand, shrink):
    w = proj.shape[-1]
    return jnp.concatenate(
        [qkv[:, :, i * w : (i + 1) * w] for i in range(3)]
        + [proj]
        + [expand[:, :, i * w : (i + 1) * w] for i in range(4)]
        + [shrink],
        1,
    )


def on_device(dp, fsdp, x_query, x_key, len_query, len_key, queue, *params):
    query_params, key_params = params[:13], params[13:]
    num_crops, seq_len, width = x_query.shape
    mirror = tuple(
        (momentum * k + (1.0 - momentum) * q.astype(f32)).astype(bf16)
        for k, q in zip(key_params, query_params)
    )
    both = [jnp.concatenate([q, m], 0) for q, m in zip(query_params, mirror)]
    qkv, qb, vb, proj, pb, g1, b1, expand, eb, shrink, sb, g2, b2 = both
    mats = pack_mats(qkv, proj, expand, shrink)
    small = jnp.concatenate([qb, vb, pb, g1, b1, sb, g2, b2, eb], 1)
    small_len = small.shape[1]
    vec = jnp.pad(small.reshape(-1), (0, 16 * width - 4 * small_len)).reshape(16, width)
    gathered, vec_all = all_gather(dp, fsdp, mats, vec, cid=1, opt=dict(nx=13, pre=2))
    vec_all = vec_all.reshape(fsdp, 16 * width)[:, : 4 * small_len].reshape(fsdp, 4, small_len)
    r = width // fsdp
    rows8 = vec_all[:, :, : 8 * r].reshape(fsdp, 4, 8, r).transpose(1, 2, 0, 3).reshape(4, 8, width)
    rows4 = vec_all[:, :, 8 * r :].transpose(1, 0, 2).reshape(4, 4, width)
    vecs = jnp.concatenate([rows8, rows4, jnp.zeros((4, 4, width), bf16)], 1).astype(f32)
    x0 = x_query.reshape(num_crops * seq_len, width)
    y0, _, *saved0 = layer_fwd(0, True, len_query, x0, vecs[0], gathered)
    y1, pooled, *saved1 = layer_fwd(1, True, len_query, y0, vecs[1], gathered)
    xk = x_key.reshape(num_crops * seq_len, width)
    k0, _ = layer_fwd(2, False, len_key, xk, vecs[2], gathered)
    _, pooled_key = layer_fwd(3, False, len_key, k0, vecs[3], gathered)
    key_unit = unit_rows(pooled_key).astype(bf16)
    query_unit = unit_rows(pooled).astype(bf16)
    pos = jnp.sum(query_unit.astype(f32) * key_unit.astype(f32), -1) / contrast_sharpness
    everyone = ("dp", "fsdp")
    logits = (
        jnp.einsum("cd,kd->ck", lax.all_gather(query_unit, everyone, axis=0, tiled=True), queue, preferred_element_type=f32)
        / contrast_sharpness
    )
    start_own = lax.axis_index(everyone) * num_crops
    own = lambda v: lax.dynamic_slice_in_dim(v, start_own, num_crops, 0)
    peak = jnp.max(logits, 1)
    peak = lax.dynamic_update_slice_in_dim(peak, jnp.maximum(own(peak), pos), start_own, 0)
    peak = lax.pmax(peak, everyone)
    shifted = jnp.exp(logits - peak[:, None])
    part = jnp.dot(shifted.astype(bf16), queue, preferred_element_type=f32)
    sums = jnp.sum(shifted, 1)
    payload = jnp.concatenate([part, jnp.broadcast_to(sums[:, None], (sums.shape[0], 128))], 1)
    payload = lax.psum_scatter(payload, everyone, scatter_dimension=0, tiled=True)
    own_peak = own(peak)
    pos_exp = jnp.exp(pos - own_peak)
    total = payload[:, width] + pos_exp
    crop_losses = own_peak + jnp.log(total) - pos
    scale = objective_factor / contrast_sharpness
    grad_unit = payload[:, :width] * (scale / total)[:, None]
    grad_unit = grad_unit + (scale * (pos_exp / total - 1.0))[:, None] * key_unit.astype(f32)
    _, unit_back = jax.vjp(unit_rows, pooled)
    grad_pooled = unit_back(grad_unit)[0] / len_query[:, None].astype(f32)
    dx1, d1, v1 = layer_bwd(1, True, len_query, grad_pooled, y0, vecs[1], gathered, saved1, f32)
    dx0, d0, v0 = layer_bwd(0, False, len_query, dx1, x0, vecs[0], gathered, saved0, bf16)
    fin, vsum = reduce_grads(dp, fsdp, [d1, d0], jnp.concatenate([v1, v0], 0), 2)
    me = lax.axis_index("fsdp")
    n = fin.shape[1]
    fin = fin.astype(f32).reshape(2, 3, n, width)[::-1]
    sh_g, ex_g, at_g = fin[:, 0], fin[:, 1], fin[:, 2]
    grad_qkv = jnp.concatenate([at_g[:, i * r : (i + 1) * r] for i in range(3)], 2)
    grad_proj = at_g[:, 3 * r :]
    grad_expand = jnp.concatenate([ex_g[:, i * r : (i + 1) * r] for i in range(4)], 2)
    vsum = vsum.reshape(2, 16, width)[::-1]
    mine = lax.dynamic_slice_in_dim(vsum[:, :8], me * r, r, 2)
    ebg = lax.dynamic_slice_in_dim(vsum[:, 8:12].reshape(2, 4 * width), me * 4 * r, 4 * r, 1)
    qb, vb, pb, g1, b1, sb, g2, b2 = [mine[:, i] for i in range(8)]
    hidden = y1.reshape(num_crops, seq_len, width)
    grad_input = dx0.reshape(num_crops, seq_len, width)
    return (hidden, grad_input, grad_qkv, qb, vb, grad_proj, pb, g1, b1, grad_expand, ebg, sh_g, sb, g2, b2, crop_losses)


def solution(mesh):
    in_specs = (
        P(("dp", "fsdp"), None, None),
        P(("dp", "fsdp"), None, None),
        P(("dp", "fsdp")),
        P(("dp", "fsdp")),
        P(("dp", "fsdp"), None),
        P(None, "fsdp", None),
        P(None, "fsdp"),
        P(None, "fsdp"),
        P(None, "fsdp", None),
        P(None, "fsdp"),
        P(None, "fsdp"),
        P(None, "fsdp"),
        P(None, "fsdp", None),
        P(None, "fsdp"),
        P(None, "fsdp", None),
        P(None, "fsdp"),
        P(None, "fsdp"),
        P(None, "fsdp"),
        P(None, "fsdp", None),
        P(None, "fsdp"),
        P(None, "fsdp"),
        P(None, "fsdp", None),
        P(None, "fsdp"),
        P(None, "fsdp"),
        P(None, "fsdp"),
        P(None, "fsdp", None),
        P(None, "fsdp"),
        P(None, "fsdp", None),
        P(None, "fsdp"),
        P(None, "fsdp"),
        P(None, "fsdp"),
    )
    out_specs = (
        P(("dp", "fsdp"), None, None),
        P(("dp", "fsdp"), None, None),
        P(None, "fsdp", None),
        P(None, "fsdp"),
        P(None, "fsdp"),
        P(None, "fsdp", None),
        P(None, "fsdp"),
        P(None, "fsdp"),
        P(None, "fsdp"),
        P(None, "fsdp", None),
        P(None, "fsdp"),
        P(None, "fsdp", None),
        P(None, "fsdp"),
        P(None, "fsdp"),
        P(None, "fsdp"),
        P(("dp", "fsdp")),
    )
    return jax.shard_map(
        functools.partial(on_device, mesh.shape["dp"], mesh.shape["fsdp"]), mesh=mesh, in_specs=in_specs, out_specs=out_specs, check_vma=False
    )
```

time: 2220 us -> 865 us (0.39)
  waiting for transfers between devices: 1460 us -> 123 us
  Pallas kernels: 0 us -> 572 us
  matrix products: 252 us -> 0.77 us
  blocking collectives: 302 us -> 108 us
  local copies, waits for them, and re-layouts: 114 us -> 18.9 us
  other arithmetic: 58.7 us -> 19.8 us
    all_gather x16 -> x0, waiting for transfers between devices: 706 us -> none  [the longest x2 154 us: gather_query(): lax.all_gather(expand_mat, 'fsdp', axis=0, tiled=True)]
    pallas_call x0 -> x8, Pallas kernels: none -> 572 us  [the longest x1 230 us: all_gather(): pl.pallas_call(functools.partial(ag_kernel, D, F, L, opt), out_shape=(jax...]
    reduce_scatter x6 -> x0, waiting for transfers between devices: 526 us -> none  [the longest x2 199 us: scatter_grads(): lax.psum_scatter(expand_mat.astype(jnp.bfloat16), 'fsdp', scatter_dimensi...]
    dot_general x50 -> x2, matrix products: 252 us -> 0.77 us  [the longest x1 0.46 us: on_device(): jnp.einsum('cd,kd->ck', lax.all_gather(query_unit, everyone, axis=0, tile...]
    all_gather x5 -> x1, blocking collectives: 146 us -> 57.6 us  [on_device(): lax.all_gather(query_unit, everyone, axis=0, tiled=True)]
    psum x1 -> x0, waiting for transfers between devices: 63.2 us -> none  [sum_grads(): lax.psum(qkv_mat.astype(jnp.bfloat16), 'dp').astype(jnp.float32)]
    unnamed x2 -> x0, blocking collectives: 58.8 us -> none
    psum x2 -> x0, blocking collectives: 49.1 us -> none  [the longest x1 39.3 us: on_device(): global_sum = lax.psum(exp_sums, ('dp', 'fsdp'))]
  transfers between devices with their start and end apart: 26 -> 1, of which waited for: 22 -> 1; matrix products, arithmetic and copies ran while one was open for 15% -> 0% of each run, Pallas kernels for 0% -> 0%
where the time goes in v1:
time: 865 us; the launch traced here: 857 us
  Pallas kernels  572 us (66%)
  waiting for transfers between devices  123 us (14%)
  blocking collectives  108 us (12%)
  other arithmetic  19.8 us (2%)
  local copies, waits for them, and re-layouts  18.9 us (2%)
  between operations  15.1 us (2%)
    pallas_call x1, Pallas kernels, all_gather(): pl.pallas_call(functools.partial(ag_kernel, D, F, L, opt), out_shape=(jax...  230 us
    pallas_call x1, Pallas kernels, reduce_grads(): pl.pallas_call(k, out_shape=[sd((NP, n, 768), bf16), sd((32, 768), f32)],...  171 us
    unnamed x2, waiting for transfers between devices  123 us
    pallas_call x4, Pallas kernels, layer_fwd(): pl.pallas_call(functools.partial(fwd_kernel, l, save), out_shape=outs, in...  98.1 us
    pallas_call x2, Pallas kernels, layer_bwd(): pl.pallas_call(functools.partial(bwd_kernel, l, first), out_shape=[sd((51...  73 us
    all_gather x1, blocking collectives, on_device(): lax.all_gather(query_unit, everyone, axis=0, tiled=True)  57.6 us
    pmax x1, blocking collectives, on_device(): peak = lax.pmax(peak, everyone)  50.1 us
  transfers between devices with their start and end apart: 1, of which 1 were waited for; matrix products, arithmetic and copies ran while one was open for 0% of the time, Pallas kernels for 0%

profile of v1, /device:TPU:11, one launch (start us, length us, event | category | flops | bytes accessed | tf_op | source)
XLA Modules:
  0.0 857.0 jit_solution(1030484899414263805)
XLA Ops:
  7.2 0.0 copy-start
  7.2 0.0 all-reduce.4.cloned.1.call-start
  7.3 2.1 add_convert_fusion.2
  9.6 0.8 copy-done.9
  10.4 0.2 copy-done.10
  10.6 0.1 add_convert_fusion.3
  10.7 0.2 copy-done.2
  11.0 0.8 copy-done.8
  11.8 0.4 add_convert_fusion.1
  12.1 0.1 fusion.7
  12.2 0.1 fusion.9
  12.5 0.1 fusion.5
  12.5 0.1 fusion.10
  12.6 2.9 copy-done.4
  15.9 0.1 concatenate.74
  16.1 0.7 reshape.104.vec
  16.7 2.0 add_convert_fusion
  18.7 1.6 maximum_dynamic-update-slice_fusion.w
  20.4 229.7 %gather_weights.1 = (bf16[4,8,1152,768]{3,2,1,0:T(8,128)(2,1)}, bf16[8,16,768]{2,1,0:T(8,128)(2,1)}) custom-call(bf16[4,1152,768]{2,1,0:T(8,128)(2,1)} %maximum_dynamic-update-slice_fusion.w, bf16[16,768]{1,0:T(8,128)(2,1)} %reshape.104.vec), custom_call_target="tpu_custom_call" | custom-call | tf_op jit(solution)/shard_map/gather_weights/pallas_call | solution.py:143
  250.1 1.0 copy.66
  251.2 0.1 reshape.107
  251.3 0.1 reshape.108
  251.4 0.1 pad.18.clone
  251.5 0.1 maximum_convert_fusion
  251.6 0.7 slice_bitcast_fusion.3
  252.3 26.0 %layer_fwd.4 = (bf16[512,768]{1,0:T(8,128)(2,1)}, f32[2,768]{1,0:T(2,128)}, bf16[512,2304]{1,0:T(8,128)(2,1)}, bf16[24,256,256]{2,1,0:T(8,128)(2,1)}, bf16[512,7...) custom-call(s32[2]{0:T(128)} %lens.11, ...), custom_call_target="tpu_custom_call" | custom-call | tf_op jit(solution)/shard_map/layer_fwd/pallas_call | solution.py:259
  278.3 26.2 %layer_fwd.5 = (bf16[512,768]{1,0:T(8,128)(2,1)}, f32[2,768]{1,0:T(2,128)}, bf16[512,2304]{1,0:T(8,128)(2,1)}, bf16[24,256,256]{2,1,0:T(8,128)(2,1)}, bf16[512,7...) custom-call(s32[2]{0:T(128)} %lens.11, ...), custom_call_target="tpu_custom_call" | custom-call | tf_op jit(solution)/shard_map/layer_fwd/pallas_call | solution.py:259
  304.5 0.8 multiply_reduce_fusion.2
  305.3 22.8 %layer_fwd.6 = (bf16[512,768]{1,0:T(8,128)(2,1)}, f32[2,768]{1,0:T(2,128)}) custom-call(s32[2]{0:T(128)} %lens.9, bf16[512,768]{1,0:T(8,128)(2,1)} %bitcast.65, f32[16,768]{1,0:T(8,128)} %get-tuple-element.105.vec, bf16[4,8,1152,768]{3,2,1,0:T(8,128)(2,1)} %get-tuple-element.52.g), custom_call_target="tpu_custom_call" | custom-call | tf_op jit(solution)/shard_map/layer_fwd/pallas_call | solution.py:259
  328.2 23.0 %layer_fwd.7 = (bf16[512,768]{1,0:T(8,128)(2,1)}, f32[2,768]{1,0:T(2,128)}) custom-call(s32[2]{0:T(128)} %lens.9, bf16[512,768]{1,0:T(8,128)(2,1)} %get-tuple-element.56.x, f32[16,768]{1,0:T(8,128)} %get-tuple-element.104.vec, bf16[4,8,1152,768]{3,2,1,0:T(8,128)(2,1)} %get-tuple-element.52.g), custom_call_target="tpu_custom_call" | custom-call | tf_op jit(solution)/shard_map/layer_fwd/pallas_call | solution.py:259
  351.2 0.8 multiply_reduce_fusion.1
  352.1 0.9 fusion.17
  353.0 57.6 %all-gather = bf16[32,2,768]{2,1,0:T(2,128)(2,1)S(1)} all-gather(bf16[1,2,768]{2,1,0:T(2,128)(2,1)S(1)} %bitcast.74), channel_id=1, replica_groups=mesh['dp'=4,'fsdp'=8] {'dp','fsdp'}, dimensions={0}, use_global_device_ids=true | all-gather | bytes 101376 | tf_op jit(solution)/shard_map/all_gather | solution.py:585
  410.6 0.5 fusion.31
  411.1 0.2 maximum_dynamic-update-slice_fusion.2
  411.2 50.1 %pmax.7 = f32[64]{0:T(128)S(1)} all-reduce(f32[64]{0:T(128)S(1)} %maximum_dynamic-update-slice_fusion.2), channel_id=1, replica_groups=mesh['dp'=4,'fsdp'=8] {'dp','fsdp'}, use_global_device_ids=true, to_apply=%region_4.5 | all-reduce | flops 64 | bytes 512 | tf_op jit(solution)/shard_map/pmax | solution.py:592
  461.4 0.2 fusion.12
  461.6 0.3 fusion.14
  461.9 0.1 broadcast_in_dim.7
  462.0 0.7 pad_maximum_fusion.4
  462.7 0.0 all-reduce.4.cloned.1.call-update
  462.8 123.0 %all-reduce.4.cloned.1.call-done = f32[64,896]{1,0:T(8,128)} async-done(((f32[64,896]{1,0:T(8,128)}), f32[64,896]{1,0:T(8,128)}) %all-reduce.4.cloned.1.call-update) | async-done | bytes 229392
  585.8 0.9 dynamic-slice_reduce_fusion
  586.6 0.6 add_subtract_fusion
  587.2 0.9 multiply_reduce_fusion
  588.2 0.7 fusion.19.dyin
  588.9 36.6 %layer_bwd.2 = (f32[512,768]{1,0:T(8,128)}, bf16[8,1152,768]{2,1,0:T(8,128)(2,1)}, f32[16,768]{1,0:T(8,128)}) custom-call(s32[2]{0:T(128)} %lens.11, f32[2,768]{1,0:T(2,128)} %fusion.19.dyin, bf16[512,768]{1,0:T(8,128)(2,1)} %get-tuple-element.53.x, f32[16,768]{1,0:T(8,128)} %get-tuple-element.106.vec, bf16[4,8,1152,768]{3,2,1,0:T(8,128)(2,1)} %get-tuple-element.52.g, ...), custom_call_target="tpu_custom_call" | custom-call | tf_op jit(solution)/shard_map/layer_bwd/pallas_call | solution.py:362
  625.4 36.4 %layer_bwd.3 = (bf16[512,768]{1,0:T(8,128)(2,1)}, bf16[8,1152,768]{2,1,0:T(8,128)(2,1)}, f32[16,768]{1,0:T(8,128)}) custom-call(s32[2]{0:T(128)} %lens.11, f32[512,768]{1,0:T(8,128)} %get-tuple-element.68.dyin, bf16[512,768]{1,0:T(8,128)(2,1)} %bitcast.64, f32[16,768]{1,0:T(8,128)} %get-tuple-element.107.vec, bf16[4,8,1152,768]{3,2,1,0:T(8,128)(2,1)} %get-tuple-element.52.g, ...), custom_call_target="tpu_custom_call" | custom-call | tf_op jit(solution)/shard_map/layer_bwd/pallas_call | solution.py:362
  661.9 1.4 pad_maximum_fusion.5.refs_2_
  663.3 170.9 %reduce_grads.1 = (bf16[6,384,768]{2,1,0:T(8,128)(2,1)}, f32[32,768]{1,0:T(8,128)}) custom-call(bf16[8,1152,768]{2,1,0:T(8,128)(2,1)} %get-tuple-element.80.refs_0_, bf16[8,1152,768]{2,1,0:T(8,128)(2,1)} %get-tuple-element.81.refs_1_, f32[32,768]{1,0:T(8,128)} %pad_maximum_fusion.5.refs_2_), custom_call_target="tpu_custom_call" | custom-call | tf_op jit(solution)/shard_map/reduce_grads/pallas_call | solution.py:531
  834.2 0.8 slice.191
  835.0 0.8 slice.198
  835.8 2.6 convert.1
  838.5 1.9 slice_bitcast_fusion
  840.3 0.2 reverse_bitcast_fusion.2
  840.5 1.2 fusion.30
  841.8 0.3 slice.150
  842.1 1.8 reverse_bitcast_fusion.1
  843.9 0.2 fusion.29
  844.1 1.6 reverse_bitcast_fusion
  845.7 0.6 constant_dynamic-slice_fusion.7
  846.3 1.3 pad_maximum_fusion.1
  847.6 1.7 pad_maximum_fusion
  849.3 0.7 fusion.20
  (93 shorter events, 0.7 us)
Async XLA Ops:
  7.2 403.4 %copy-start = (bf16[512,768]{1,0:T(8,128)(2,1)S(1)}, bf16[512,768]{1,0:T(8,128)(2,1)}, u32[]{:S(2)}) copy-start(bf16[512,768]{1,0:T(8,128)(2,1)} %param.35) | copy-start | bytes 2359300
  7.2 2.2 copy-start.3
  7.2 578.6 %all-reduce.4.cloned.1.call-start = ((), (), s32[]{:S(2)}) async-start(), calls=%async_computation | async-start | bytes 458752
  9.4 1.0 copy-start.9
  9.4 1.1 copy-start.10
  9.5 1.5 copy-start.2
  9.5 2.2 copy-start.8
  12.3 3.3 copy-start.14
  12.3 3.3 copy-start.15
  12.3 3.3 copy-start.16
  12.3 3.3 copy-start.24
  12.3 3.3 copy-start.17
  12.3 3.3 copy-start.25
  12.3 3.3 copy-start.18
  12.3 3.3 copy-start.26
  12.3 3.4 copy-start.19
  12.4 3.4 copy-start.27
  12.4 3.4 copy-start.20
  12.4 3.4 copy-start.28
  12.4 3.4 copy-start.21
  12.4 3.4 copy-start.29
  12.4 3.4 copy-start.22
  12.4 3.4 copy-start.30
  12.4 3.4 copy-start.23
  12.5 3.4 copy-start.31
  12.5 4.2 copy-start.5
  12.6 2.9 copy-start.4
  328.2 23.9 %copy-start.11 = (f32[2,768]{1,0:T(2,128)S(1)}, f32[2,768]{1,0:T(2,128)}, u32[]{:S(2)}) copy-start(f32[2,768]{1,0:T(2,128)} %get-tuple-element.55) | copy-start | bytes 18436
  351.2 111.5 %copy-start.13 = (s32[2]{0:T(128)S(1)}, s32[2]{0:T(128)}, u32[]{:S(2)}) copy-start(s32[2]{0:T(128)} %lens.11) | copy-start | bytes 28
  625.4 36.5 %copy-start.12 = (f32[16,768]{1,0:T(8,128)S(1)}, f32[16,768]{1,0:T(8,128)}, u32[]{:S(2)}) copy-start(f32[16,768]{1,0:T(8,128)} %get-tuple-element.82) | copy-start | bytes 147460
  844.1 2.2 copy-start.6
  844.1 2.2 copy-start.7
  847.6 2.4 copy-start.1
Sparse Core Ops, SparseCore 0:
  462.8 122.8 all-reduce.3

commit v2 on v1

--- a/solution.py
+++ b/solution.py
@@ -7,144 +7,6 @@
 from jax.experimental.pallas import tpu as pltpu
 from jax.sharding import PartitionSpec as P
 
-MESH=pl.DeviceIdType.MESH
-
-def coords(D,F):
-    d=lax.axis_index("dp"); f=lax.axis_index("fsdp")
-    B=F//4
-    return d,f,f//B,f%B,(d//2)%2,d%2
-
-
-def ag_kernel(D,F,L,opt,w,vec,g,vg,lsem,vsem,vrsem,zs,zr,ys,yr,xs,xr,cs,cr,csx,crx):
-    A=4;B=F//4
-    R=w.shape[1]; T=R//16
-    half=T//2; nx=(half*opt['nx'])//36; nyz=half-nx
-    d,f,a,b,x,c=coords(D,F)
-    h=c*half
-    xn=nx*16; yzn=nyz*16
-    def rows(t0,n): return pl.ds(pl.multiple_of(t0*16,16),n)
-    yzr=rows(h+x*nx,yzn); xsr=rows(h+x*nyz,xn); xrr=rows(h+(1-x)*nyz,xn)
-    hc=(1-c)*half
-    oyz=rows(hc+x*nx,yzn); oxr=rows(hc+(1-x)*nyz,xn)
-    xd=d+2-4*x; cd=d+1-2*c
-    bar=pltpu.get_barrier_semaphore()
-    for s in range(1,F):
-        pl.semaphore_signal(bar,inc=1,device_id=(d,(f+s)%F),device_id_type=MESH)
-    pl.semaphore_signal(bar,inc=1,device_id=(xd,f),device_id_type=MESH)
-    pl.semaphore_signal(bar,inc=1,device_id=(cd,f),device_id_type=MESH)
-    pl.semaphore_wait(bar,F+1)
-    def rc(src,dst,ss,rs,dev):
-        return pltpu.make_async_remote_copy(src,dst,ss,rs,device_id=dev,device_id_type=MESH)
-    def vcopy(s):
-        return rc(vec,vg.at[f],vsem.at[s],vrsem.at[s],(d,(f+s)%F))
-    for s in range(1,F): vcopy(s).start()
-    vl=pltpu.make_async_copy(vec,vg.at[f],vsem.at[0]); vl.start()
-    def own(l): return pltpu.make_async_copy(w.at[l],g.at[l,f],lsem.at[l])
-    def src_a(hd):
-        hh,dr=hd
-        return a-hh if dr==0 else a+hh
-    def has(hd):
-        hh,dr=hd
-        return (a>=hh) if dr==0 else (a+hh<A)
-    def when(cond,fn):
-        if cond is True: fn()
-        else: pl.when(cond)(fn)
-    def zsend(l,src,hd,fs):
-        hh,dr=hd
-        na=a+1 if dr==0 else a-1
-        return rc(src,g.at[l,fs,yzr],zs.at[l,dr,hh],zr.at[l,dr,hh],(d,na*B+b))
-    def canpass(dr): return (a+1<A) if dr==0 else (a>0)
-    def zrecv(l,hd):
-        fs=src_a(hd)*B+b
-        return rc(g.at[l,fs,yzr],g.at[l,fs,yzr],zs.at[l,hd[1],hd[0]],zr.at[l,hd[1],hd[0]],(d,f))
-    def slot(hd): return hd[0]*2+hd[1]
-    def ycopy(l,src,hd,fs,t): return rc(src,g.at[l,fs,yzr],ys.at[l,slot(hd),t],yr.at[l,slot(hd),t],(d,a*B+(b+t)%B))
-    def yrecv(l,hd,t):
-        fs=src_a(hd)*B+(b-t)%B
-        return fs,rc(g.at[l,fs,yzr],g.at[l,fs,yzr],ys.at[l,slot(hd),t],yr.at[l,slot(hd),t],(d,f))
-    def xcopy(l,fs,i): return rc(g.at[l,fs,xsr],g.at[l,fs,xsr],xs.at[l,i],xr.at[l,i],(xd,f))
-    def xrecv(l,fs,i): return rc(g.at[l,fs,xrr],g.at[l,fs,xrr],xs.at[l,i],xr.at[l,i],(xd,f))
-    def ccopy(l,fs,i): return rc(g.at[l,fs,yzr],g.at[l,fs,yzr],cs.at[l,i],cr.at[l,i],(cd,f))
-    def cxcopy(l,fs,i): return rc(g.at[l,fs,xrr],g.at[l,fs,xrr],csx.at[l,i],crx.at[l,i],(cd,f))
-    def crecv(l,fs,i): return rc(g.at[l,fs,oyz],g.at[l,fs,oyz],cs.at[l,i],cr.at[l,i],(cd,f))
-    def cxrecv(l,fs,i): return rc(g.at[l,fs,oxr],g.at[l,fs,oxr],csx.at[l,i],crx.at[l,i],(cd,f))
-    OWN=(0,0)
-    def start(l):
-        for dr in (0,1): when(canpass(dr),lambda dr=dr: zsend(l,w.at[l,yzr],(1,dr),f).start())
-        for t in range(1,B): ycopy(l,w.at[l,yzr],OWN,f,t).start()
-        own(l).start()
-    def handle_z(l,hh):
-        for dr in (0,1):
-            hd=(hh,dr)
-            def go(hd=hd,dr=dr):
-                fs=src_a(hd)*B+b
-                zrecv(l,hd).wait_recv()
-                if hh+1<A:
-                    when(canpass(dr),lambda: zsend(l,g.at[l,fs,yzr],(hh+1,dr),fs).start())
-                for t in range(1,B): ycopy(l,g.at[l,fs,yzr],hd,fs,t).start()
-                xcopy(l,fs,slot(hd)*B).start()
-                ccopy(l,fs,slot(hd)*B).start()
-            pl.when(has(hd))(go)
-    def hds(hh): return [(0,0)] if hh==0 else [(hh,0),(hh,1)]
-    def handle_y(l,hh):
-        for hd in hds(hh):
-            for t in range(1,B):
-                def go(hd=hd,t=t):
-                    fs,r=yrecv(l,hd,t); r.wait_recv()
-                    xcopy(l,fs,slot(hd)*B+t).start()
-                    ccopy(l,fs,slot(hd)*B+t).start()
-                when(True if hh==0 else has(hd),go)
-    def each_foreign(fn):
-        for hh in range(A):
-            for hd in hds(hh):
-                for t in range(B):
-                    if hh==0 and t==0: continue
-                    def go(hd=hd,t=t): fn(src_a(hd)*B+(b-t)%B,slot(hd)*B+t)
-                    when(True if hh==0 else has(hd),go)
-    def xphase(l):
-        def go(fs,i):
-            xrecv(l,fs,i).wait_recv(); cxcopy(l,fs,i).start()
-        each_foreign(go)
-    start(0)
-    for l in range(L):
-        for hh in range(1,A):
-            if hh==opt['pre'] and l+1<L: start(l+1)
-            handle_z(l,hh)
-            handle_y(l,hh-1)
-            if hh==1 and l: xphase(l-1)
-        if opt['pre']==A and l+1<L: start(l+1)
-        handle_y(l,A-1)
-    xphase(L-1)
-    for l in range(L):
-        def go(fs,i):
-            crecv(l,fs,i).wait_recv(); cxrecv(l,fs,i).wait_recv()
-            xcopy(l,fs,i).wait_send(); ccopy(l,fs,i).wait_send(); cxcopy(l,fs,i).wait_send()
-        each_foreign(go)
-        for dr in (0,1):
-            for hh in range(1,A):
-                cond=canpass(dr)
-                if hh>1: cond=jnp.logical_and(cond,has((hh-1,dr)))
-                pl.when(cond)(lambda hh=hh,dr=dr: zsend(l,w.at[l,yzr],(hh,dr),f).wait_send())
-        for hh in range(A):
-            for hd in hds(hh):
-                for t in range(1,B):
-                    when(True if hh==0 else has(hd),lambda hd=hd,t=t: ycopy(l,w.at[l,yzr],hd,f,t).wait_send())
-        own(l).wait()
-    vl.wait()
-    for s in range(1,F):
-        vcopy(s).wait_send()
-        rc(vec,vg.at[f],vsem.at[s],vrsem.at[s],(d,f)).wait_recv()
-
-def all_gather(D,F,w,vec,cid=1,opt=None):
-    L,R,C=w.shape
-    A=4;B=F//4
-    S=pltpu.SemaphoreType.DMA
-    N=2*A*B
-    return pl.pallas_call(functools.partial(ag_kernel,D,F,L,opt),
-        out_shape=(jax.ShapeDtypeStruct((L,F,R,C),w.dtype),jax.ShapeDtypeStruct((F,)+vec.shape,vec.dtype)),
-        in_specs=[pl.BlockSpec(memory_space=pl.ANY)]*2,out_specs=[pl.BlockSpec(memory_space=pl.ANY)]*2,
-        scratch_shapes=[S((L,)),S((F,)),S((F,)),S((L,2,A)),S((L,2,A)),S((L,2*A,B)),S((L,2*A,B))]+[S((L,N))]*6,
-        compiler_params=pltpu.CompilerParams(collective_id=cid,has_side_effects=True),name="gather_weights")(w,vec)
 f32=jnp.float32; bf16=jnp.bfloat16
 HEADS=12
 def dot(a,b): return lax.dot_general(a,b,(((1,),(0,)),((),())),preferred_element_type=f32)
@@ -169,96 +31,383 @@
         cps.append(pltpu.make_async_copy(g.at[l,pl.ds(j*(F//4),F//4),pl.ds(8*r,rs),:],sv.at[j],sem.at[8+j]))
     return cps
 
-def fwd_kernel(l,save,lens,x,vec,g,*rest):
-    if save:
-        (y,pooled,qkv_o,pb_o,ctx_o,xh1_o,rs1_o,h1_o,act_o,der_o,xh2_o,rs2_o,
-         wv,sv,qkv,pb,ctx,xh1,rs1,h1,act,der,xh2,rs2,acc,sem,osem)=rest
-    else:
-        (y,pooled,wv,sv,qkv,ctx,xh1,h1,acc,sem)=rest
-    cps=load_weights(l,g,wv,sv,sem)
-    for c in cps: c.start()
-    outs=[]
-    def out(i,src,dst):
-        if save:
-            cp=pltpu.make_async_copy(src,dst,osem.at[i]); cp.start(); outs.append(cp)
-    def W(j): return wv[j].reshape(768,768)
-    def S(j): return sv[j].reshape(768,768)
-    NR=512
-    for j in range(3):
-        cps[j].wait()
-        r=dot(x[...],W(j))
-        if j==0: r=r+vec[0:1,:]
-        if j==2: r=r+vec[1:2,:]
-        qkv[:,j*768:(j+1)*768]=r.astype(bf16)
-    if save: out(0,qkv,qkv_o)
-    lane=lax.broadcasted_iota(jnp.int32,(256,128),1)
-    low_half=lane<64
-    kpos=lax.broadcasted_iota(jnp.int32,(256,256),1)
-    def pair(i,_):
-        c=i//6; p=i-c*6
-        rows=pl.ds(pl.multiple_of(c*256,256),256)
-        o=pl.multiple_of(p*128,128)
-        q2=qkv[rows,pl.ds(o,128)]*jnp.asarray(0.125,bf16)
-        k2=qkv[rows,pl.ds(pl.multiple_of(768+o,128),128)]
-        v2=qkv[rows,pl.ds(pl.multiple_of(1536+o,128),128)]
-        ok=kpos<lens[c]
-        res=[]
-        for hh in range(2):
-            qm=jnp.where(low_half if hh==0 else jnp.logical_not(low_half),q2,jnp.zeros_like(q2))
-            s=jnp.where(ok,dot_t(qm,k2),-1e9)
-            m=jnp.max(s,-1,keepdims=True)
-            e=jnp.exp(s-m)
-            pr=(e*(1.0/jnp.sum(e,-1,keepdims=True))).astype(bf16)
-            if save: pb[i*2+hh]=pr
-            res.append(dot(pr,v2))
-        ctx[rows,pl.ds(o,128)]=jnp.where(low_half,res[0],res[1]).astype(bf16)
-        return 0
-    lax.fori_loop(0,12,pair,0,unroll=3)
-    if save: out(1,pb,pb_o); out(2,ctx,ctx_o)
-    cps[3].wait()
-    def ln(z,gain,shift):
+MESH=pl.DeviceIdType.MESH
+SHARP=0.05
+FACTOR=512.0
+MOM=0.9995
+
+def remote(src,dst,ss,rs,dev):
+    return pltpu.make_async_remote_copy(src,dst,ss,rs,device_id=dev,device_id_type=MESH)
+
+def when(cond,fn):
+    if cond is True: fn()
+    else: pl.when(cond)(fn)
+
+class Place:
+    def __init__(self,D,F):
+        self.D,self.F=D,F; self.A=4; self.B=F//4; self.O=D//4
+        d=self.d=lax.axis_index("dp"); f=self.f=lax.axis_index("fsdp")
+        self.a=f//self.B; self.b=f%self.B; self.o=d//4; self.x=(d//2)%2; self.c=d%2
+        self.xd=d+2-4*self.x; self.cd=d+1-2*self.c
+        self.N=D*F; self.me=d*F+f
+    def peer(self,s):
+        p=(self.me+s)%self.N
+        return p,(p//self.F,p%self.F)
+
+class Gather:
+    def __init__(self,pos,g,chunks,ready,sems):
+        self.p,self.g,self.chunks,self.ready=pos,g,chunks,ready
+        self.zs,self.zr,self.ys,self.yr,self.xs,self.xr,self.cs,self.cr,self.ks,self.kr=sems
+    def rows(self,q,t0,n):
+        return pl.ds(pl.multiple_of(self.chunks[q][1]+t0*16,16),n*16)
+    def parts(self,q):
+        p=self.p; half=self.chunks[q][2]//32; nx=(half*13+18)//36; nyz=half-nx
+        h=p.c*half; hc=(1-p.c)*half
+        R=lambda t0,n: self.rows(q,t0,n)
+        return dict(yz=R(h+p.x*nx,nyz),xs=R(h+p.x*nyz,nx),xr=R(h+(1-p.x)*nyz,nx),oyz=R(hc+p.x*nx,nyz),oxr=R(hc+(1-p.x)*nyz,nx))
+    def at(self,q,fs,part): return self.g.at[self.chunks[q][0],fs,self.parts(q)[part]]
+    def src_a(self,hd): return self.p.a-hd[0] if hd[1]==0 else self.p.a+hd[0]
+    def has(self,hd):
+        if hd[0]==0: return True
+        return (self.p.a>=hd[0]) if hd[1]==0 else (self.p.a+hd[0]<self.p.A)
+    def canpass(self,dr): return (self.p.a+1<self.p.A) if dr==0 else (self.p.a>0)
+    def z(self,q,hd,fs):
+        na=self.p.a+1 if hd[1]==0 else self.p.a-1
+        r=self.at(q,fs,"yz")
+        return remote(r,r,self.zs.at[q,hd[1],hd[0]],self.zr.at[q,hd[1],hd[0]],(self.p.d,na*self.p.B+self.p.b))
+    def slot(self,hd): return hd[0]*2+hd[1]
+    def y(self,q,hd,fs,t):
+        r=self.at(q,fs,"yz"); s=self.slot(hd)
+        return remote(r,r,self.ys.at[q,s,t],self.yr.at[q,s,t],(self.p.d,self.p.a*self.p.B+(self.p.b+t)%self.p.B))
+    def xc(self,q,fs,i,part="xs"):
+        r=self.at(q,fs,part); return remote(r,r,self.xs.at[q,i],self.xr.at[q,i],(self.p.xd,self.p.f))
+    def cc(self,q,fs,i,part="yz"):
+        r=self.at(q,fs,part); return remote(r,r,self.cs.at[q,i],self.cr.at[q,i],(self.p.cd,self.p.f))
+    def kc(self,q,fs,i,part="xr"):
+        r=self.at(q,fs,part); return remote(r,r,self.ks.at[q,i],self.kr.at[q,i],(self.p.cd,self.p.f))
+    def shard(self,hd,t=0): return self.src_a(hd)*self.p.B+(self.p.b-t)%self.p.B
+    def hds(self,hh): return [(0,0)] if hh==0 else [(hh,0),(hh,1)]
+    def start(self,q):
+        self.ready(q)
+        f=self.p.f
+        for dr in (0,1): when(self.canpass(dr),lambda dr=dr: self.z(q,(1,dr),f).start())
+        for t in range(1,self.p.B): self.y(q,(0,0),f,t).start()
+    def on_z(self,q,hh):
+        for hd in self.hds(hh):
+            def go(hd=hd):
+                fs=self.shard(hd); dr=hd[1]
+                self.z(q,hd,fs).wait_recv()
+                if hh+1<self.p.A: when(self.canpass(dr),lambda: self.z(q,(hh+1,dr),fs).start())
+                for t in range(1,self.p.B): self.y(q,hd,fs,t).start()
+                i=self.slot(hd)*self.p.B
+                self.xc(q,fs,i).start(); self.cc(q,fs,i).start()
+            when(self.has(hd),go)
+    def on_y(self,q,hh):
+        for hd in self.hds(hh):
+            for t in range(1,self.p.B):
+                def go(hd=hd,t=t):
+                    fs=self.shard(hd,t); i=self.slot(hd)*self.p.B+t
+                    self.y(q,hd,fs,t).wait_recv()
+                    self.xc(q,fs,i).start(); self.cc(q,fs,i).start()
+                when(self.has(hd),go)
+    def each(self,hh,fn):
+        for hd in self.hds(hh):
+            for t in range(self.p.B):
+                if hh==0 and t==0: continue
+                when(self.has(hd),lambda hd=hd,t=t: fn(self.shard(hd,t),self.slot(hd)*self.p.B+t))
+    def on_x(self,q,hh):
+        def go(fs,i):
+            self.xc(q,fs,i,"xr").wait_recv(); self.kc(q,fs,i).start()
+        self.each(hh,go)
+    def on_c(self,q):
+        def go(fs,i):
+            self.cc(q,fs,i,"oyz").wait_recv(); self.kc(q,fs,i,"oxr").wait_recv()
+        for hh in range(self.p.A): self.each(hh,go)
+    def handlers(self,q,pre):
+        hs=[]; A=self.p.A
+        for hh in range(1,A):
+            if hh==pre and q+1<len(self.chunks): hs.append(lambda: self.start(q+1))
+            hs.append(lambda hh=hh: self.on_z(q,hh))
+            hs.append(lambda hh=hh: self.on_y(q,hh-1))
+            if hh>=2: hs.append(lambda hh=hh: self.on_x(q,hh-2))
+        hs.append(lambda: self.on_y(q,A-1))
+        hs.append(lambda: self.on_x(q,A-2)); hs.append(lambda: self.on_x(q,A-1))
+        hs.append(lambda: self.on_c(q))
+        return hs
+    def finish(self):
+        f=self.p.f
+        for q in range(len(self.chunks)):
+            def go(fs,i):
+                self.xc(q,fs,i).wait_send(); self.cc(q,fs,i).wait_send(); self.kc(q,fs,i).wait_send()
+            for hh in range(self.p.A):
+                self.each(hh,go)
+                for hd in self.hds(hh):
+                    for t in range(1,self.p.B): when(self.has(hd),lambda hd=hd,t=t: self.y(q,hd,f,t).wait_send())
+            for dr in (0,1):
+                for hh in range(1,self.p.A):
+                    cond=self.canpass(dr)
+                    if hh>1: cond=jnp.logical_and(cond,self.has((hh-1,dr)))
+                    pl.when(cond)(lambda hh=hh,dr=dr: self.z(q,(hh,dr),f).wait_send())
+
+def interleave(handlers,steps):
+    done=0; n=max(len(steps),1)
+    for k,s in enumerate(steps):
+        s()
+        upto=(k+1)*len(handlers)//n
+        for h in handlers[done:upto]: h()
+        done=upto
+    for h in handlers[done:]: h()
+
+SAVED=("qkv","pb","ctx","xh1","rs1","h1","act","der","xh2","rs2")
+def saved_shapes():
+    sd=jax.ShapeDtypeStruct
+    return [sd((512,2304),bf16),sd((24,256,256),bf16),sd((512,768),bf16),sd((512,768),f32),sd((512,128),f32),sd((512,768),bf16),sd((512,3072),bf16),sd((512,3072),bf16),sd((512,768),f32),sd((512,128),f32)]
+
+class Forward:
+    def __init__(self,g,vecs,lens,R):
+        self.g,self.vecs,self.lens=g,vecs,lens
+        self.__dict__.update(R)
+    def W(self,j): return self.wv[j].reshape(768,768)
+    def S(self,j): return self.sv[j].reshape(768,768)
+    def load(self,l,js):
+        for j in js: self.wcp(l,j).start()
+    def wcp(self,l,j):
+        F=self.g.shape[1]; r=768//F; rs=3072//F
+        if j<8: return pltpu.make_async_copy(self.g.at[l,:,pl.ds(j*r,r),:],self.wv.at[j],self.wsem.at[j])
+        j-=8
+        return pltpu.make_async_copy(self.g.at[l,pl.ds(j*(F//4),F//4),pl.ds(8*r,rs),:],self.sv.at[j],self.wsem.at[8+j])
+    def ocp(self,l,i): return pltpu.make_async_copy(self.__dict__[SAVED[i]],self.outs[l][i],self.osem.at[l,i])
+    def out(self,l,*names):
+        for n in names: self.ocp(l,SAVED.index(n)).start()
+    def drain(self,l):
+        for i in range(len(SAVED)): self.ocp(l,i).wait()
+    def ln(self,z,gain,shift):
         mu=jnp.mean(z,-1,keepdims=True); cz=z-mu
         rstd=lax.rsqrt(jnp.mean(cz*cz,-1,keepdims=True)+1e-12)
         xh=cz*rstd
         return xh,rstd,xh*gain+shift
-    z=dot(ctx[...],W(3))+vec[2:3,:]+x[...].astype(f32)
-    xh,rstd,h=ln(z,vec[3:4,:],vec[4:5,:])
-    if save:
-        xh1[...]=xh; rs1[...]=jnp.broadcast_to(rstd,(NR,128)); out(3,xh1,xh1_o); out(4,rs1,rs1_o)
-    h1[...]=h.astype(bf16)
-    acc[...]=h+vec[5:6,:]
-    if save: out(5,h1,h1_o)
-    for j in range(4):
-        cps[4+j].wait(); cps[8+j].wait()
-        u=dot(h1[...],W(4+j))+vec[8+j:9+j,:]
-        cdf,pdf=phi_parts(u)
-        gb=(u*cdf).astype(bf16)
-        if save:
-            act[:,j*768:(j+1)*768]=gb
-            der[:,j*768:(j+1)*768]=(cdf+u*pdf).astype(bf16)
-        acc[...]+=dot(gb,S(j))
-    if save: out(6,act,act_o); out(7,der,der_o)
-    xh,rstd,yy=ln(acc[...],vec[6:7,:],vec[7:8,:])
-    if save:
-        xh2[...]=xh; rs2[...]=jnp.broadcast_to(rstd,(NR,128)); out(8,xh2,xh2_o); out(9,rs2,rs2_o)
-    y[...]=yy.astype(bf16)
-    tpos=lax.broadcasted_iota(jnp.int32,(256,768),0)
-    for c in range(2):
-        pooled[c:c+1,:]=jnp.sum(jnp.where(tpos<lens[c],yy[c*256:(c+1)*256],0.0),0,keepdims=True)/lens[c].astype(f32)
-    for cp in outs: cp.wait()
-
-def layer_fwd(l,save,lens,x,vec,g):
-    F=g.shape[1]
-    sd=jax.ShapeDtypeStruct
-    V=pl.BlockSpec(memory_space=pltpu.VMEM); ANY=pl.BlockSpec(memory_space=pl.ANY)
-    saved=[sd((512,2304),bf16),sd((24,256,256),bf16),sd((512,768),bf16),sd((512,768),f32),sd((512,128),f32),sd((512,768),bf16),sd((512,3072),bf16),sd((512,3072),bf16),sd((512,768),f32),sd((512,128),f32)]
-    outs=[sd((512,768),bf16),sd((2,768),f32)]+(saved if save else [])
-    wscr=[pltpu.VMEM((8,F,768//F,768),bf16),pltpu.VMEM((4,F//4,3072//F,768),bf16)]
-    if save: scr=wscr+[pltpu.VMEM(s.shape,s.dtype) for s in saved]+[pltpu.VMEM((512,768),f32),pltpu.SemaphoreType.DMA((12,)),pltpu.SemaphoreType.DMA((10,))]
-    else: scr=wscr+[pltpu.VMEM((512,2304),bf16),pltpu.VMEM((512,768),bf16),pltpu.VMEM((512,768),f32),pltpu.VMEM((512,768),bf16),pltpu.VMEM((512,768),f32),pltpu.SemaphoreType.DMA((12,))]
-    return pl.pallas_call(functools.partial(fwd_kernel,l,save),out_shape=outs,
-        in_specs=[pl.BlockSpec(memory_space=pltpu.SMEM),V,V,ANY],out_specs=[V,V]+([ANY]*10 if save else []),
-        scratch_shapes=scr,compiler_params=pltpu.CompilerParams(vmem_limit_bytes=60<<20),name="layer_fwd")(lens,x,vec,g)
+    def attn_steps(self,l,save,x,lens,before=None):
+        V=lambda i: self.vecs[l,i:i+1,:]
+        def proj_in(j):
+            if j==0 and before: before()
+            if j==0: self.load(l,range(4))
+            self.wcp(l,j).wait()
+            r=dot(x[...],self.W(j))
+            if j==0: r=r+V(0)
+            if j==2: r=r+V(1)
+            self.qkv[:,j*768:(j+1)*768]=r.astype(bf16)
+            if save and j==2: self.out(l,"qkv")
+        lane=lax.broadcasted_iota(jnp.int32,(256,128),1); low_half=lane<64
+        kpos=lax.broadcasted_iota(jnp.int32,(256,256),1)
+        def pair(i,_):
+            c=i//6; p=i-c*6
+            rows=pl.ds(pl.multiple_of(c*256,256),256); o=pl.multiple_of(p*128,128)
+            q2=self.qkv[rows,pl.ds(o,128)]*jnp.asarray(0.125,bf16)
+            k2=self.qkv[rows,pl.ds(pl.multiple_of(768+o,128),128)]; v2=self.qkv[rows,pl.ds(pl.multiple_of(1536+o,128),128)]
+            ok=kpos<lens[c]
+            res=[]
+            for hh in range(2):
+                qm=jnp.where(low_half if hh==0 else jnp.logical_not(low_half),q2,jnp.zeros_like(q2))
+                s=jnp.where(ok,dot_t(qm,k2),-1e9)
+                e=jnp.exp(s-jnp.max(s,-1,keepdims=True))
+                pr=(e*(1.0/jnp.sum(e,-1,keepdims=True))).astype(bf16)
+                if save: self.pb[i*2+hh]=pr
+                res.append(dot(pr,v2))
+            self.ctx[rows,pl.ds(o,128)]=jnp.where(low_half,res[0],res[1]).astype(bf16)
+            return 0
+        def attend(s):
+            lax.fori_loop(6*s,6*s+6,pair,0,unroll=3)
+            if save and s==1: self.out(l,"pb","ctx")
+        def proj_out():
+            self.wcp(l,3).wait()
+            z=dot(self.ctx[...],self.W(3))+V(2)+x[...].astype(f32)
+            xh,rstd,h=self.ln(z,V(3),V(4))
+            if save: self.xh1[...]=xh; self.rs1[...]=jnp.broadcast_to(rstd,(512,128))
+            self.h1[...]=h.astype(bf16)
+            self.acc[...]=h+V(5)
+            if save: self.out(l,"xh1","rs1","h1")
+        return [functools.partial(proj_in,j) for j in range(3)]+[functools.partial(attend,s) for s in range(2)]+[proj_out]
+    def ffn_steps(self,l,save,y,lens,pooled):
+        V=lambda i: self.vecs[l,i:i+1,:]
+        def part(j):
+            if j==0: self.load(l,[4,8,5,9,6,10,7,11])
+            self.wcp(l,4+j).wait(); self.wcp(l,8+j).wait()
+            u=dot(self.h1[...],self.W(4+j))+V(8+j)
+            cdf,pdf=phi_parts(u)
+            gb=(u*cdf).astype(bf16)
+            if save:
+                self.act[:,j*768:(j+1)*768]=gb
+                self.der[:,j*768:(j+1)*768]=(cdf+u*pdf).astype(bf16)
+            self.acc[...]+=dot(gb,self.S(j))
+            if save and j==3: self.out(l,"act","der")
+        def end():
+            xh,rstd,yy=self.ln(self.acc[...],V(6),V(7))
+            if save:
+                self.xh2[...]=xh; self.rs2[...]=jnp.broadcast_to(rstd,(512,128)); self.out(l,"xh2","rs2")
+            y[...]=yy.astype(bf16)
+            if pooled is not None:
+                tpos=lax.broadcasted_iota(jnp.int32,(256,768),0)
+                for c in range(2):
+                    pooled[c:c+1,:]=jnp.sum(jnp.where(tpos<lens[c],yy[c*256:(c+1)*256],0.0),0,keepdims=True)/lens[c].astype(f32)
+        return [functools.partial(part,j) for j in range(4)]+[end]
+
+def unit_scale(p): return lax.rsqrt(jnp.sum(p*p,-1,keepdims=True)+1e-6)
+
+class Contrast:
+    def __init__(self,pos,queue,lens,R):
+        self.p,self.queue,self.lens=pos,queue,lens
+        self.__dict__.update(R)
+    def ucp(self,s):
+        _,dev=self.p.peer(s)
+        return remote(self.units.at[self.p.me],self.units.at[self.p.me],self.us.at[s],self.ur.at[s],dev)
+    def gcp(self,s):
+        j,dev=self.p.peer(s)
+        return remote(self.sends.at[j],self.gets.at[self.p.me],self.gs.at[s],self.gr.at[s],dev)
+    def loop(self,fn): lax.fori_loop(1,self.p.N,lambda s,_: (fn(s),0)[1],0)
+    def send_units(self):
+        p=self.pool_q[...]
+        self.units[self.p.me]=(p*unit_scale(p)).astype(bf16).astype(f32)
+        self.loop(lambda s: self.ucp(s).start())
+    def share(self):
+        self.loop(lambda s: self.ucp(s).wait_recv())
+        N=self.p.N
+        for i in range(N): self.q_all[2*i:2*i+2,:]=self.units[i]
+        lg=dot_t(self.q_all[...].astype(bf16),self.queue[...])*(1.0/SHARP)
+        m=jnp.max(lg,-1,keepdims=True)
+        e=jnp.exp(lg-m)
+        self.part[:,0:768]=dot(e.astype(bf16),self.queue[...])
+        self.part[:,768:896]=jnp.broadcast_to(m,(2*N,128))
+        self.part[:,896:1024]=jnp.broadcast_to(jnp.sum(e,-1,keepdims=True),(2*N,128))
+        for i in range(N): self.sends[i]=self.part[2*i:2*i+2,:]
+        self.gets[self.p.me]=self.sends[self.p.me]
+        self.loop(lambda s: self.gcp(s).start())
+    def end(self,loss,grad):
+        pk=self.pool_k[...]; pq=self.pool_q[...]
+        ku=(pk*unit_scale(pk)).astype(bf16).astype(f32)
+        rs=unit_scale(pq)
+        qu=(pq*rs).astype(bf16).astype(f32)
+        pos=jnp.sum(qu*ku,-1,keepdims=True)/SHARP
+        self.loop(lambda s: self.gcp(s).wait_recv())
+        mi=self.gets[:,:,768:896]
+        top=jnp.maximum(jnp.max(mi,0),pos)
+        w=jnp.exp(mi-top[None])
+        pe=jnp.exp(pos-top)
+        total=jnp.sum(w*self.gets[:,:,896:1024],0)+pe
+        loss[...]=top+jnp.log(total)-pos
+        scale=FACTOR/SHARP
+        inv=scale/total
+        cp=scale*(pe/total-1.0)
+        for k in range(6):
+            cols=slice(k*128,(k+1)*128)
+            grad[:,cols]=jnp.sum(w*self.gets[:,:,cols],0)*inv+cp*ku[:,cols]
+        g=grad[...]
+        d=rs*g-pq*(rs*rs*rs)*jnp.sum(pq*g,-1,keepdims=True)
+        for c in range(2): grad[c:c+1,:]=d[c:c+1]/self.lens[c].astype(f32)
+    def finish(self):
+        self.loop(lambda s: self.ucp(s).wait_send())
+        self.loop(lambda s: self.gcp(s).wait_send())
+
+def forward_kernel(D,F,pre,names,lenq,lenk,xq,xk,queue,msg,qw,pw,ew,sw,kqw,kpw,kew,ksw,
+                   g,vecs,y0,y1,loss,gp,*rest):
+    outs=(rest[:10],rest[10:20]); R=dict(zip(names,rest[20:]))
+    pos=Place(D,F); r=768//F; rs=3072//F; f=pos.f
+    bar=pltpu.get_barrier_semaphore()
+    def hello(s,_):
+        _,dev=pos.peer(s)
+        pl.semaphore_signal(bar,inc=1,device_id=dev,device_id_type=MESH); return 0
+    lax.fori_loop(1,pos.N,hello,0)
+    def own(l,j):
+        dst=lambda j,n: g.at[l,f,pl.ds(j*r,n)]
+        if j<3: s,d=qw.at[l,:,pl.ds(j*768,768)],dst(j,r)
+        elif j==3: s,d=pw.at[l],dst(3,r)
+        elif j<8: s,d=ew.at[l,:,pl.ds((j-4)*768,768)],dst(j,r)
+        else: s,d=sw.at[l],dst(8,rs)
+        return pltpu.make_async_copy(s,d,R["lsem"].at[l,j])
+    groups={0:range(4),1:range(4,9)}
+    for l in range(2):
+        for j in range(9): own(l,j).start()
+    def kload(l):
+        pairs=[(kqw,"kq"),(kpw,"kp"),(kew,"ke"),(ksw,"ks"),(qw,"qq"),(pw,"qp"),(ew,"qe"),(sw,"qs")]
+        return [pltpu.make_async_copy(a.at[l],R[b],R["ksem"].at[i]) for i,(a,b) in enumerate(pairs)]
+    def mcp(l): return pltpu.make_async_copy(R["mo"].at[l],g.at[2+l,f],R["msem"].at[l])
+    for c in kload(0): c.start()
+    def mirror(l):
+        for c in kload(l): c.wait()
+        mo=R["mo"]
+        mix=lambda k,q: (MOM*k+(1.0-MOM)*q.astype(f32)).astype(bf16)
+        for j in range(3):
+            cols=slice(j*768,(j+1)*768); mo[l,j*r:(j+1)*r,:]=mix(R["kq"][:,cols],R["qq"][:,cols])
+        mo[l,3*r:4*r,:]=mix(R["kp"][...],R["qp"][...])
+        for j in range(4):
+            cols=slice(j*768,(j+1)*768); mo[l,(4+j)*r:(5+j)*r,:]=mix(R["ke"][:,cols],R["qe"][:,cols])
+        mo[l,8*r:8*r+rs,:]=mix(R["ks"][...],R["qs"][...])
+        mcp(l).start()
+        if l==0:
+            for c in kload(1): c.start()
+    waited=set()
+    def ready(q):
+        l=q//2
+        if l<2:
+            for j in groups[q%2]: own(l,j).wait()
+        elif l not in waited:
+            waited.add(l); mcp(l-2).wait()
+    chunks=[(l,r0,n) for l in range(4) for r0,n in ((0,4*r),(4*r,8*r))]
+    G=Gather(pos,g,chunks,ready,[R[k] for k in ("zs","zr","ys","yr","xs","xr","cs","cr","ks_","kr_")])
+    vmsg=R["vmsg"]
+    def vcp(s): return remote(msg,vmsg.at[f],R["vs"].at[s],R["vr"].at[s],(pos.d,(f+s)%F))
+    vmsg[f]=msg[...]
+    pl.semaphore_wait(bar,pos.N-1)
+    G.start(0)
+    for s in range(1,F): vcp(s).start()
+    def vectors():
+        for s in range(1,F): vcp(s).wait_recv()
+        row=lax.broadcasted_iota(jnp.int32,(128,768),0); col=lax.broadcasted_iota(jnp.int32,(128,768),1)
+        v=jnp.zeros((32,768),f32)
+        for i in range(F):
+            hot=jnp.logical_and(col==row+i*r,row<r)
+            v=v+dot(vmsg[i,:,0:128],jnp.where(hot,1.0,0.0).astype(bf16))
+        row=lax.broadcasted_iota(jnp.int32,(384,768),0); col=lax.broadcasted_iota(jnp.int32,(384,768),1)
+        for l in range(4): vecs[l,0:8,:]=v[8*l:8*l+8]; vecs[l,8:16,:]=jnp.zeros((8,768),f32)
+        for j in range(4):
+            e=jnp.zeros((32,768),f32)
+            for i in range(F//4):
+                hot=jnp.logical_and(col==row+i*rs,row<rs)
+                e=e+dot(vmsg[j*(F//4)+i,:,128:512],jnp.where(hot,1.0,0.0).astype(bf16))
+            for l in range(4): vecs[l,8+j:9+j,:]=e[8*l:8*l+1]
+    Fw=Forward(g,vecs,None,R); Fw.outs=outs
+    Ct=Contrast(pos,queue,lenq,R)
+    yk=R["yk"]
+    work=[]
+    for l,(save,x,y,lens,pool) in enumerate([(True,xq,y0,lenq,None),(True,y0,y1,lenq,R["pool_q"]),(False,xk,yk,lenk,None),(False,yk,R["yl"],lenk,R["pool_k"])]):
+        work.append(Fw.attn_steps(l,save,x,lens,(lambda k=l-1: Fw.drain(k)) if l in (1,2) else None))
+        work.append(Fw.ffn_steps(l,save,y,lens,pool))
+    work[3].append(Ct.send_units)
+    work[4].append(Ct.share)
+    interleave(G.handlers(0,pre),[vectors,lambda: mirror(0),lambda: mirror(1)])
+    for q in range(1,8): interleave(G.handlers(q,pre),work[q-1])
+    for s in work[7]: s()
+    Ct.end(loss,gp)
+    G.finish(); Ct.finish()
+    for s in range(1,F): vcp(s).wait_send()
+
+def forward(D,F,lenq,lenk,xq,xk,queue,msg,mats,kmats,cid,pre=2):
+    sd=jax.ShapeDtypeStruct; S=pltpu.SemaphoreType.DMA; VM=pltpu.VMEM
+    V=pl.BlockSpec(memory_space=pltpu.VMEM); ANY=pl.BlockSpec(memory_space=pl.ANY); SM=pl.BlockSpec(memory_space=pltpu.SMEM)
+    A=4;B=F//4;Q=8;N=D*F; r=768//F; rs=3072//F; M=2*A*B
+    buf=dict(zip(SAVED,[VM(s.shape,s.dtype) for s in saved_shapes()]))
+    buf.update(acc=VM((512,768),f32),yk=VM((512,768),bf16),yl=VM((512,768),bf16),wv=VM((8,F,r,768),bf16),sv=VM((4,F//4,rs,768),bf16),
+        pool_q=VM((2,768),f32),pool_k=VM((2,768),f32),units=VM((N,2,768),f32),q_all=VM((2*N,768),f32),part=VM((2*N,1024),f32),
+        sends=VM((N,2,1024),f32),gets=VM((N,2,1024),f32),vmsg=VM((F,32,512),bf16),
+        kq=VM((r,2304),f32),kp=VM((r,768),f32),ke=VM((r,3072),f32),ks=VM((rs,768),f32),qq=VM((r,2304),bf16),qp=VM((r,768),bf16),qe=VM((r,3072),bf16),qs=VM((rs,768),bf16),
+        mo=VM((2,12*r,768),bf16),
+        wsem=S((12,)),osem=S((2,10)),lsem=S((2,9)),ksem=S((8,)),msem=S((2,)),us=S((N,)),ur=S((N,)),gs=S((N,)),gr=S((N,)),vs=S((F,)),vr=S((F,)),
+        zs=S((Q,2,A)),zr=S((Q,2,A)),ys=S((Q,2*A,B)),yr=S((Q,2*A,B)),xs=S((Q,M)),xr=S((Q,M)),cs=S((Q,M)),cr=S((Q,M)),ks_=S((Q,M)),kr_=S((Q,M)))
+    saved=saved_shapes()
+    outs=[sd((4,F,12*r,768),bf16),sd((4,16,768),f32),sd((512,768),bf16),sd((512,768),bf16),sd((2,128),f32),sd((2,768),f32)]+saved*2
+    res=pl.pallas_call(functools.partial(forward_kernel,D,F,pre,list(buf)),out_shape=outs,
+        in_specs=[SM,SM,V,V,V,V]+[ANY]*8,out_specs=[ANY,V,V,V,V,V]+[ANY]*20,scratch_shapes=list(buf.values()),
+        compiler_params=pltpu.CompilerParams(collective_id=cid,has_side_effects=True,vmem_limit_bytes=61<<20),name="forward")(lenq,lenk,xq,xk,queue,msg,*mats,*kmats)
+    return res[:6],res[6:16],res[16:26]
 def bwd_kernel(l,first,lens,dyin,x,vec,g,qkv_i,pb_i,ctx_i,xh1_i,rs1_i,h1_i,act_i,der_i,xh2_i,rs2_i,
                dx,dg,vg,wv,sv,qkv,pb,ctx,xh1,rs1,h1,act,der,xh2,rs2,dmix,dacc,dr2,dctx,dv,ds,sem,isem,osem):
     F=g.shape[1]; r=768//F; rs_=3072//F
@@ -531,79 +680,26 @@
     return pl.pallas_call(k,out_shape=[sd((NP,n,768),bf16),sd((32,768),f32)],in_specs=[ANY]*len(dgs)+[V],out_specs=[V,V],
         scratch_shapes=list(buf.values()),compiler_params=pltpu.CompilerParams(collective_id=cid,has_side_effects=True,vmem_limit_bytes=61<<20),name="reduce_grads")(*dgs,vin)
 
-contrast_sharpness = 0.05
-objective_factor = 512.0
-momentum = 0.9995
-unit_eps = 1e-06
-
-
-def unit_rows(pooled):
-    return pooled * lax.rsqrt(jnp.sum(pooled * pooled, -1, keepdims=True) + unit_eps)
-
-
-def pack_mats(qkv, proj, expand, shrink):
-    w = proj.shape[-1]
-    return jnp.concatenate(
-        [qkv[:, :, i * w : (i + 1) * w] for i in range(3)]
-        + [proj]
-        + [expand[:, :, i * w : (i + 1) * w] for i in range(4)]
-        + [shrink],
-        1,
-    )
-
 
 def on_device(dp, fsdp, x_query, x_key, len_query, len_key, queue, *params):
     query_params, key_params = params[:13], params[13:]
     num_crops, seq_len, width = x_query.shape
-    mirror = tuple(
-        (momentum * k + (1.0 - momentum) * q.astype(f32)).astype(bf16)
-        for k, q in zip(key_params, query_params)
-    )
-    both = [jnp.concatenate([q, m], 0) for q, m in zip(query_params, mirror)]
-    qkv, qb, vb, proj, pb, g1, b1, expand, eb, shrink, sb, g2, b2 = both
-    mats = pack_mats(qkv, proj, expand, shrink)
-    small = jnp.concatenate([qb, vb, pb, g1, b1, sb, g2, b2, eb], 1)
-    small_len = small.shape[1]
-    vec = jnp.pad(small.reshape(-1), (0, 16 * width - 4 * small_len)).reshape(16, width)
-    gathered, vec_all = all_gather(dp, fsdp, mats, vec, cid=1, opt=dict(nx=13, pre=2))
-    vec_all = vec_all.reshape(fsdp, 16 * width)[:, : 4 * small_len].reshape(fsdp, 4, small_len)
     r = width // fsdp
-    rows8 = vec_all[:, :, : 8 * r].reshape(fsdp, 4, 8, r).transpose(1, 2, 0, 3).reshape(4, 8, width)
-    rows4 = vec_all[:, :, 8 * r :].transpose(1, 0, 2).reshape(4, 4, width)
-    vecs = jnp.concatenate([rows8, rows4, jnp.zeros((4, 4, width), bf16)], 1).astype(f32)
+    order = (1, 2, 4, 5, 6, 10, 11, 12)
+    small_q = jnp.stack([query_params[i] for i in order], 1)
+    small_k = jnp.stack([key_params[i] for i in order], 1)
+    bias_q, bias_k = query_params[8], key_params[8]
+    mix = lambda k, q: (MOM * k + (1.0 - MOM) * q.astype(f32)).astype(bf16)
+    small = jnp.concatenate([small_q, mix(small_k, small_q)], 0).reshape(32, r)
+    wide = jnp.concatenate([bias_q, mix(bias_k, bias_q)], 0)
+    wide = jnp.pad(wide[:, None, :], ((0, 0), (0, 7), (0, 384 - wide.shape[1]))).reshape(32, 384)
+    msg = jnp.concatenate([jnp.pad(small, ((0, 0), (0, 128 - r))), wide], 1)
+    big = (0, 3, 7, 9)
     x0 = x_query.reshape(num_crops * seq_len, width)
-    y0, _, *saved0 = layer_fwd(0, True, len_query, x0, vecs[0], gathered)
-    y1, pooled, *saved1 = layer_fwd(1, True, len_query, y0, vecs[1], gathered)
     xk = x_key.reshape(num_crops * seq_len, width)
-    k0, _ = layer_fwd(2, False, len_key, xk, vecs[2], gathered)
-    _, pooled_key = layer_fwd(3, False, len_key, k0, vecs[3], gathered)
-    key_unit = unit_rows(pooled_key).astype(bf16)
-    query_unit = unit_rows(pooled).astype(bf16)
-    pos = jnp.sum(query_unit.astype(f32) * key_unit.astype(f32), -1) / contrast_sharpness
-    everyone = ("dp", "fsdp")
-    logits = (
-        jnp.einsum("cd,kd->ck", lax.all_gather(query_unit, everyone, axis=0, tiled=True), queue, preferred_element_type=f32)
-        / contrast_sharpness
-    )
-    start_own = lax.axis_index(everyone) * num_crops
-    own = lambda v: lax.dynamic_slice_in_dim(v, start_own, num_crops, 0)
-    peak = jnp.max(logits, 1)
-    peak = lax.dynamic_update_slice_in_dim(peak, jnp.maximum(own(peak), pos), start_own, 0)
-    peak = lax.pmax(peak, everyone)
-    shifted = jnp.exp(logits - peak[:, None])
-    part = jnp.dot(shifted.astype(bf16), queue, preferred_element_type=f32)
-    sums = jnp.sum(shifted, 1)
-    payload = jnp.concatenate([part, jnp.broadcast_to(sums[:, None], (sums.shape[0], 128))], 1)
-    payload = lax.psum_scatter(payload, everyone, scatter_dimension=0, tiled=True)
-    own_peak = own(peak)
-    pos_exp = jnp.exp(pos - own_peak)
-    total = payload[:, width] + pos_exp
-    crop_losses = own_peak + jnp.log(total) - pos
-    scale = objective_factor / contrast_sharpness
-    grad_unit = payload[:, :width] * (scale / total)[:, None]
-    grad_unit = grad_unit + (scale * (pos_exp / total - 1.0))[:, None] * key_unit.astype(f32)
-    _, unit_back = jax.vjp(unit_rows, pooled)
-    grad_pooled = unit_back(grad_unit)[0] / len_query[:, None].astype(f32)
+    (gathered, vecs, y0, y1, loss, grad_pooled), saved0, saved1 = forward(
+        dp, fsdp, len_query, len_key, x0, xk, queue, msg,
+        [query_params[i] for i in big], [key_params[i] for i in big], 1)
     dx1, d1, v1 = layer_bwd(1, True, len_query, grad_pooled, y0, vecs[1], gathered, saved1, f32)
     dx0, d0, v0 = layer_bwd(0, False, len_query, dx1, x0, vecs[0], gathered, saved0, bf16)
     fin, vsum = reduce_grads(dp, fsdp, [d1, d0], jnp.concatenate([v1, v0], 0), 2)
@@ -620,7 +716,7 @@
     qb, vb, pb, g1, b1, sb, g2, b2 = [mine[:, i] for i in range(8)]
     hidden = y1.reshape(num_crops, seq_len, width)
     grad_input = dx0.reshape(num_crops, seq_len, width)
-    return (hidden, grad_input, grad_qkv, qb, vb, grad_proj, pb, g1, b1, grad_expand, ebg, sh_g, sb, g2, b2, crop_losses)
+    return (hidden, grad_input, grad_qkv, qb, vb, grad_proj, pb, g1, b1, grad_expand, ebg, sh_g, sb, g2, b2, loss[:, 0])
 
 
 def solution(mesh):

time: 865 us -> 649 us (0.75)
  waiting for transfers between devices: 123 us -> 0 us
  blocking collectives: 108 us -> 0 us
  Pallas kernels: 572 us -> 613 us
  between operations: 15.1 us -> 1.02 us
  other arithmetic: 19.8 us -> 9.14 us
    unnamed x2 -> x0, waiting for transfers between devices: 123 us -> none
    all_gather x1 -> x0, blocking collectives: 57.6 us -> none  [on_device(): lax.all_gather(query_unit, everyone, axis=0, tiled=True)]
    pmax x1 -> x0, blocking collectives: 50.1 us -> none  [on_device(): peak = lax.pmax(peak, everyone)]
    pallas_call x5 -> x1, Pallas kernels: 328 us -> 362 us  [forward(): pl.pallas_call(functools.partial(forward_kernel, D, F, pre, list(buf)), o...]
  transfers between devices with their start and end apart: 1 -> 0, of which waited for: 1 -> 0; matrix products, arithmetic and copies ran while one was open for 0% -> 0% of each run, Pallas kernels for 0% -> 0%
where the time goes in v2:
time: 649 us; the launch traced here: 642 us
  Pallas kernels  613 us (94%)
  local copies, waits for them, and re-layouts  19.3 us (3%)
  other arithmetic  9.14 us (1%)
    pallas_call x1, Pallas kernels, forward(): pl.pallas_call(functools.partial(forward_kernel, D, F, pre, list(buf)), o...  362 us
    pallas_call x1, Pallas kernels, reduce_grads(): pl.pallas_call(k, out_shape=[sd((NP, n, 768), bf16), sd((32, 768), f32)],...  178 us
    pallas_call x2, Pallas kernels, layer_bwd(): pl.pallas_call(functools.partial(bwd_kernel, l, first), out_shape=[sd((51...  73 us

profile of v2, /device:TPU:11, one launch (start us, length us, event | category | flops | bytes accessed | tf_op | source)
XLA Modules:
  0.0 642.4 jit_solution(12129696680281668869)
XLA Ops:
  0.6 0.7 constant_dynamic-update-slice_fusion.7
  1.3 0.7 constant_dynamic-update-slice_fusion.6
  2.0 0.7 constant_dynamic-update-slice_fusion.5
  2.6 0.7 constant_dynamic-update-slice_fusion.4
  3.3 0.7 constant_dynamic-update-slice_fusion.3
  4.0 0.7 constant_dynamic-update-slice_fusion.2
  4.6 0.7 constant_dynamic-update-slice_fusion.1
  5.3 0.7 constant_dynamic-update-slice_fusion
  5.9 0.7 constant_dynamic-update-slice_fusion.15
  6.6 0.7 constant_dynamic-update-slice_fusion.14
  7.3 0.7 constant_dynamic-update-slice_fusion.13
  8.0 0.7 constant_dynamic-update-slice_fusion.12
  8.7 0.7 constant_dynamic-update-slice_fusion.11
  9.4 0.7 constant_dynamic-update-slice_fusion.10
  10.0 0.7 constant_dynamic-update-slice_fusion.9
  10.7 0.7 constant_dynamic-update-slice_fusion.8
  11.5 0.7 add_convert_fusion.1
  12.2 0.7 maximum_bitcast_fusion
  12.9 0.6 fusion.1.msg
  13.5 362.1 %forward.1 = (bf16[4,8,1152,768]{3,2,1,0:T(8,128)(2,1)}, f32[4,16,768]{2,1,0:T(8,128)}, bf16[512,768]{1,0:T(8,128)(2,1)}, bf16[512,768]{1,0:T(8,128)(2,1)}, f32[...) custom-call(s32[2]{0:T(128)} %lens.3, s32[2]{0:T(128)} %lenk.1, ...), custom_call_target="tpu_custom_call" | custom-call | tf_op jit(solution)/shard_map/forward/pallas_call | solution.py:407
  375.6 1.5 slice_bitcast_fusion.3
  377.1 36.5 %layer_bwd.2 = (f32[512,768]{1,0:T(8,128)}, bf16[8,1152,768]{2,1,0:T(8,128)(2,1)}, f32[16,768]{1,0:T(8,128)}) custom-call(s32[2]{0:T(128)} %lens.3, f32[2,768]{1,0:T(2,128)} %get-tuple-element.51.dyin, bf16[512,768]{1,0:T(8,128)(2,1)} %get-tuple-element.52.x, f32[16,768]{1,0:T(8,128)} %get-tuple-element.96.vec, ...), custom_call_target="tpu_custom_call" | custom-call | tf_op jit(solution)/shard_map/layer_bwd/pallas_call | solution.py:511
  413.5 0.0 copy-start.2
  413.6 36.6 %layer_bwd.3 = (bf16[512,768]{1,0:T(8,128)(2,1)}, bf16[8,1152,768]{2,1,0:T(8,128)(2,1)}, f32[16,768]{1,0:T(8,128)}) custom-call(s32[2]{0:T(128)} %lens.3, f32[512,768]{1,0:T(8,128)} %get-tuple-element.65.dyin, bf16[512,768]{1,0:T(8,128)(2,1)} %bitcast.83, f32[16,768]{1,0:T(8,128)} %get-tuple-element.95.vec, bf16[4,8,1152,768]{3,2,1,0:T(8,128)(2,1)} %get-tuple-element.54.g, ...), custom_call_target="tpu_custom_call" | custom-call | tf_op jit(solution)/shard_map/layer_bwd/pallas_call | solution.py:511
  450.1 0.0 copy-done.2
  450.2 1.4 pad_maximum_fusion.2.refs_2_
  451.6 177.8 %reduce_grads.1 = (bf16[6,384,768]{2,1,0:T(8,128)(2,1)}, f32[32,768]{1,0:T(8,128)}) custom-call(bf16[8,1152,768]{2,1,0:T(8,128)(2,1)} %get-tuple-element.77.refs_0_, bf16[8,1152,768]{2,1,0:T(8,128)(2,1)} %get-tuple-element.78.refs_1_, f32[32,768]{1,0:T(8,128)} %pad_maximum_fusion.2.refs_2_), custom_call_target="tpu_custom_call" | custom-call | tf_op jit(solution)/shard_map/reduce_grads/pallas_call | solution.py:680
  629.4 2.6 convert.1
  632.1 0.8 slice_bitcast_fusion
  632.9 1.7 reverse_bitcast_fusion
  634.6 0.2 fusion.10
  634.8 1.7 pad_maximum_fusion
  636.5 0.2 reverse_bitcast_fusion.2
  636.7 1.0 fusion.11
  637.7 0.0 copy-start.1
  637.7 0.0 copy-start.3
  637.7 0.0 copy-start
  637.7 1.3 pad_maximum_fusion.1
  639.0 0.0 copy-done.1
  639.0 0.3 slice.95
  639.3 0.7 fusion.2
  640.0 0.6 constant_dynamic-slice_fusion.7
  640.6 0.0 copy-done.3
  640.6 0.6 slice_reduce_fusion
  641.3 0.0 copy-done
  641.3 0.9 copy.82
  (10 shorter events, 0.1 us)
Async XLA Ops:
  413.5 36.6 %copy-start.2 = (f32[16,768]{1,0:T(8,128)S(1)}, f32[16,768]{1,0:T(8,128)}, u32[]{:S(2)}) copy-start(f32[16,768]{1,0:T(8,128)} %get-tuple-element.79) | copy-start | bytes 147460
  637.7 1.3 copy-start.1
  637.7 3.0 copy-start.3
  637.7 3.6 copy-start

commit v3 on v2

--- a/solution.py
+++ b/solution.py
@@ -123,17 +123,6 @@
         def go(fs,i):
             self.cc(q,fs,i,"oyz").wait_recv(); self.kc(q,fs,i,"oxr").wait_recv()
         for hh in range(self.p.A): self.each(hh,go)
-    def handlers(self,q,pre):
-        hs=[]; A=self.p.A
-        for hh in range(1,A):
-            if hh==pre and q+1<len(self.chunks): hs.append(lambda: self.start(q+1))
-            hs.append(lambda hh=hh: self.on_z(q,hh))
-            hs.append(lambda hh=hh: self.on_y(q,hh-1))
-            if hh>=2: hs.append(lambda hh=hh: self.on_x(q,hh-2))
-        hs.append(lambda: self.on_y(q,A-1))
-        hs.append(lambda: self.on_x(q,A-2)); hs.append(lambda: self.on_x(q,A-1))
-        hs.append(lambda: self.on_c(q))
-        return hs
     def finish(self):
         f=self.p.f
         for q in range(len(self.chunks)):
@@ -148,15 +137,6 @@
                     cond=self.canpass(dr)
                     if hh>1: cond=jnp.logical_and(cond,self.has((hh-1,dr)))
                     pl.when(cond)(lambda hh=hh,dr=dr: self.z(q,(hh,dr),f).wait_send())
-
-def interleave(handlers,steps):
-    done=0; n=max(len(steps),1)
-    for k,s in enumerate(steps):
-        s()
-        upto=(k+1)*len(handlers)//n
-        for h in handlers[done:upto]: h()
-        done=upto
-    for h in handlers[done:]: h()
 
 SAVED=("qkv","pb","ctx","xh1","rs1","h1","act","der","xh2","rs2")
 def saved_shapes():
@@ -307,7 +287,7 @@
         self.loop(lambda s: self.ucp(s).wait_send())
         self.loop(lambda s: self.gcp(s).wait_send())
 
-def forward_kernel(D,F,pre,names,lenq,lenk,xq,xk,queue,msg,qw,pw,ew,sw,kqw,kpw,kew,ksw,
+def forward_kernel(D,F,order,names,lenq,lenk,xq,xk,queue,msg,qw,pw,ew,sw,kqw,kpw,kew,ksw,
                    g,vecs,y0,y1,loss,gp,*rest):
     outs=(rest[:10],rest[10:20]); R=dict(zip(names,rest[20:]))
     pos=Place(D,F); r=768//F; rs=3072//F; f=pos.f
@@ -317,7 +297,7 @@
         pl.semaphore_signal(bar,inc=1,device_id=dev,device_id_type=MESH); return 0
     lax.fori_loop(1,pos.N,hello,0)
     def own(l,j):
-        dst=lambda j,n: g.at[l,f,pl.ds(j*r,n)]
+        dst=lambda j,n: R["pk"].at[l,pl.ds(j*r,n)]
         if j<3: s,d=qw.at[l,:,pl.ds(j*768,768)],dst(j,r)
         elif j==3: s,d=pw.at[l],dst(3,r)
         elif j<8: s,d=ew.at[l,:,pl.ds((j-4)*768,768)],dst(j,r)
@@ -344,11 +324,15 @@
         mcp(l).start()
         if l==0:
             for c in kload(1): c.start()
+    def packed(q):
+        l,r0,n=chunks[q]
+        return pltpu.make_async_copy(R["pk"].at[l,pl.ds(r0,n)],g.at[l,f,pl.ds(r0,n)],R["psem"].at[q])
     waited=set()
     def ready(q):
         l=q//2
         if l<2:
             for j in groups[q%2]: own(l,j).wait()
+            cp=packed(q); cp.start(); cp.wait()
         elif l not in waited:
             waited.add(l); mcp(l-2).wait()
     chunks=[(l,r0,n) for l in range(4) for r0,n in ((0,4*r),(4*r,8*r))]
@@ -357,7 +341,6 @@
     def vcp(s): return remote(msg,vmsg.at[f],R["vs"].at[s],R["vr"].at[s],(pos.d,(f+s)%F))
     vmsg[f]=msg[...]
     pl.semaphore_wait(bar,pos.N-1)
-    G.start(0)
     for s in range(1,F): vcp(s).start()
     def vectors():
         for s in range(1,F): vcp(s).wait_recv()
@@ -383,14 +366,16 @@
         work.append(Fw.ffn_steps(l,save,y,lens,pool))
     work[3].append(Ct.send_units)
     work[4].append(Ct.share)
-    interleave(G.handlers(0,pre),[vectors,lambda: mirror(0),lambda: mirror(1)])
-    for q in range(1,8): interleave(G.handlers(q,pre),work[q-1])
-    for s in work[7]: s()
+    pre=[vectors,lambda: mirror(0),lambda: mirror(1)]
+    act=[G.start,G.on_z,G.on_y,G.on_x,G.on_c,lambda q,i: work[q][i](),lambda q,i: pre[i]()]
+    for kind,q,i in order:
+        if kind in (0,4): act[kind](q)
+        else: act[kind](q,i)
     Ct.end(loss,gp)
     G.finish(); Ct.finish()
     for s in range(1,F): vcp(s).wait_send()
 
-def forward(D,F,lenq,lenk,xq,xk,queue,msg,mats,kmats,cid,pre=2):
+def forward(D,F,lenq,lenk,xq,xk,queue,msg,mats,kmats,cid,order=None):
     sd=jax.ShapeDtypeStruct; S=pltpu.SemaphoreType.DMA; VM=pltpu.VMEM
     V=pl.BlockSpec(memory_space=pltpu.VMEM); ANY=pl.BlockSpec(memory_space=pl.ANY); SM=pl.BlockSpec(memory_space=pltpu.SMEM)
     A=4;B=F//4;Q=8;N=D*F; r=768//F; rs=3072//F; M=2*A*B
@@ -399,15 +384,33 @@
         pool_q=VM((2,768),f32),pool_k=VM((2,768),f32),units=VM((N,2,768),f32),q_all=VM((2*N,768),f32),part=VM((2*N,1024),f32),
         sends=VM((N,2,1024),f32),gets=VM((N,2,1024),f32),vmsg=VM((F,32,512),bf16),
         kq=VM((r,2304),f32),kp=VM((r,768),f32),ke=VM((r,3072),f32),ks=VM((rs,768),f32),qq=VM((r,2304),bf16),qp=VM((r,768),bf16),qe=VM((r,3072),bf16),qs=VM((rs,768),bf16),
-        mo=VM((2,12*r,768),bf16),
+        mo=VM((2,12*r,768),bf16),pk=VM((2,12*r,768),bf16),psem=S((4,)),
         wsem=S((12,)),osem=S((2,10)),lsem=S((2,9)),ksem=S((8,)),msem=S((2,)),us=S((N,)),ur=S((N,)),gs=S((N,)),gr=S((N,)),vs=S((F,)),vr=S((F,)),
         zs=S((Q,2,A)),zr=S((Q,2,A)),ys=S((Q,2*A,B)),yr=S((Q,2*A,B)),xs=S((Q,M)),xr=S((Q,M)),cs=S((Q,M)),cr=S((Q,M)),ks_=S((Q,M)),kr_=S((Q,M)))
     saved=saved_shapes()
     outs=[sd((4,F,12*r,768),bf16),sd((4,16,768),f32),sd((512,768),bf16),sd((512,768),bf16),sd((2,128),f32),sd((2,768),f32)]+saved*2
-    res=pl.pallas_call(functools.partial(forward_kernel,D,F,pre,list(buf)),out_shape=outs,
+    res=pl.pallas_call(functools.partial(forward_kernel,D,F,ORDER if order is None else order,list(buf)),out_shape=outs,
         in_specs=[SM,SM,V,V,V,V]+[ANY]*8,out_specs=[ANY,V,V,V,V,V]+[ANY]*20,scratch_shapes=list(buf.values()),
         compiler_params=pltpu.CompilerParams(collective_id=cid,has_side_effects=True,vmem_limit_bytes=61<<20),name="forward")(lenq,lenk,xq,xk,queue,msg,*mats,*kmats)
     return res[:6],res[6:16],res[16:26]
+ORDER = (
+    (0, 0, 0), (1, 0, 1), (6, 0, 0), (1, 0, 2), (2, 0, 0), (6, 0, 1), (0, 1, 0), (6, 0, 2), (1, 0, 3), (2, 0, 1),
+    (3, 0, 0), (2, 0, 2), (1, 1, 1), (2, 0, 3), (3, 0, 1), (2, 1, 0), (3, 0, 2), (1, 1, 2), (3, 0, 3), (4, 0, 0),
+    (5, 0, 0), (5, 0, 1), (1, 1, 3), (5, 0, 2), (5, 0, 3), (3, 1, 0), (2, 1, 1), (0, 2, 0), (5, 0, 4), (2, 1, 2),
+    (1, 2, 1), (5, 0, 5), (1, 2, 2), (2, 2, 0), (0, 3, 0), (2, 1, 3), (1, 2, 3), (3, 1, 1), (2, 2, 1), (3, 1, 2),
+    (3, 2, 0), (2, 2, 2), (1, 3, 1), (3, 1, 3), (4, 1, 0), (5, 1, 0), (2, 2, 3), (3, 2, 1), (2, 3, 0), (3, 2, 2),
+    (1, 3, 2), (5, 1, 1), (3, 2, 3), (5, 1, 2), (4, 2, 0), (5, 1, 3), (1, 3, 3), (5, 1, 4), (3, 3, 0), (2, 3, 1),
+    (5, 2, 0), (0, 4, 0), (5, 2, 1), (2, 3, 2), (1, 4, 1), (5, 2, 2), (5, 2, 3), (1, 4, 2), (2, 4, 0), (0, 5, 0),
+    (5, 2, 4), (2, 3, 3), (1, 4, 3), (3, 3, 1), (2, 4, 1), (3, 3, 2), (5, 2, 5), (3, 4, 0), (2, 4, 2), (1, 5, 1),
+    (3, 3, 3), (4, 3, 0), (5, 3, 0), (2, 4, 3), (3, 4, 1), (2, 5, 0), (3, 4, 2), (1, 5, 2), (5, 3, 1), (3, 4, 3),
+    (5, 3, 2), (4, 4, 0), (5, 3, 3), (1, 5, 3), (5, 3, 4), (3, 5, 0), (2, 5, 1), (5, 3, 5), (0, 6, 0), (5, 4, 0),
+    (2, 5, 2), (5, 4, 1), (1, 6, 1), (5, 4, 2), (5, 4, 3), (1, 6, 2), (2, 6, 0), (0, 7, 0), (2, 5, 3), (5, 4, 4),
+    (1, 6, 3), (3, 5, 1), (2, 6, 1), (3, 5, 2), (3, 6, 0), (5, 4, 5), (2, 6, 2), (1, 7, 1), (3, 5, 3), (4, 5, 0),
+    (5, 4, 6), (2, 6, 3), (3, 6, 1), (2, 7, 0), (3, 6, 2), (1, 7, 2), (3, 6, 3), (4, 6, 0), (5, 5, 0), (1, 7, 3),
+    (5, 5, 1), (3, 7, 0), (2, 7, 1), (5, 5, 2), (5, 5, 3), (2, 7, 2), (5, 5, 4), (5, 6, 0), (5, 6, 1), (2, 7, 3),
+    (5, 6, 2), (3, 7, 1), (5, 6, 3), (3, 7, 2), (5, 6, 4), (3, 7, 3), (4, 7, 0), (5, 6, 5), (5, 7, 0), (5, 7, 1),
+    (5, 7, 2), (5, 7, 3), (5, 7, 4),
+)
 def bwd_kernel(l,first,lens,dyin,x,vec,g,qkv_i,pb_i,ctx_i,xh1_i,rs1_i,h1_i,act_i,der_i,xh2_i,rs2_i,
                dx,dg,vg,wv,sv,qkv,pb,ctx,xh1,rs1,h1,act,der,xh2,rs2,dmix,dacc,dr2,dctx,dv,ds,sem,isem,osem):
     F=g.shape[1]; r=768//F; rs_=3072//F

time: 649 us -> 532 us (0.82)
  Pallas kernels: 613 us -> 493 us
    pallas_call x1, Pallas kernels: 362 us -> 249 us  [forward(): pl.pallas_call(functools.partial(forward_kernel, D, F, ORDER if order is...]
    pallas_call x1, Pallas kernels: 178 us -> 171 us  [reduce_grads(): pl.pallas_call(k, out_shape=[sd((NP, n, 768), bf16), sd((32, 768), f32)],...]
where the time goes in v3:
time: 532 us; the launch traced here: 522 us
  Pallas kernels  493 us (93%)
  local copies, waits for them, and re-layouts  19.3 us (4%)
  other arithmetic  9.14 us (2%)
    pallas_call x1, Pallas kernels, forward(): pl.pallas_call(functools.partial(forward_kernel, D, F, ORDER if order is...  249 us
    pallas_call x1, Pallas kernels, reduce_grads(): pl.pallas_call(k, out_shape=[sd((NP, n, 768), bf16), sd((32, 768), f32)],...  171 us
    pallas_call x2, Pallas kernels, layer_bwd(): pl.pallas_call(functools.partial(bwd_kernel, l, first), out_shape=[sd((51...  73.1 us
    unnamed x28, local copies, waits for them, and re-layouts  11.2 us

profile of v3, /device:TPU:11, one launch (start us, length us, event | category | flops | bytes accessed | tf_op | source)
XLA Modules:
  0.0 522.1 jit_solution(16619424843663129359)
XLA Ops:
  0.6 0.7 constant_dynamic-update-slice_fusion.7
  1.3 0.7 constant_dynamic-update-slice_fusion.6
  2.0 0.7 constant_dynamic-update-slice_fusion.5
  2.6 0.7 constant_dynamic-update-slice_fusion.4
  3.3 0.7 constant_dynamic-update-slice_fusion.3
  4.0 0.7 constant_dynamic-update-slice_fusion.2
  4.6 0.7 constant_dynamic-update-slice_fusion.1
  5.3 0.7 constant_dynamic-update-slice_fusion
  5.9 0.7 constant_dynamic-update-slice_fusion.15
  6.6 0.7 constant_dynamic-update-slice_fusion.14
  7.3 0.7 constant_dynamic-update-slice_fusion.13
  8.0 0.7 constant_dynamic-update-slice_fusion.12
  8.7 0.7 constant_dynamic-update-slice_fusion.11
  9.4 0.7 constant_dynamic-update-slice_fusion.10
  10.0 0.7 constant_dynamic-update-slice_fusion.9
  10.7 0.7 constant_dynamic-update-slice_fusion.8
  11.5 0.7 add_convert_fusion.1
  12.2 0.7 maximum_bitcast_fusion
  12.9 0.6 fusion.1.msg
  13.5 249.0 %forward.1 = (bf16[4,8,1152,768]{3,2,1,0:T(8,128)(2,1)}, f32[4,16,768]{2,1,0:T(8,128)}, bf16[512,768]{1,0:T(8,128)(2,1)}, bf16[512,768]{1,0:T(8,128)(2,1)}, f32[...) custom-call(s32[2]{0:T(128)} %lens.3, s32[2]{0:T(128)} %lenk.1, ...), custom_call_target="tpu_custom_call" | custom-call | tf_op jit(solution)/shard_map/forward/pallas_call | solution.py:392
  262.5 1.5 slice_bitcast_fusion.3
  264.0 36.5 %layer_bwd.2 = (f32[512,768]{1,0:T(8,128)}, bf16[8,1152,768]{2,1,0:T(8,128)(2,1)}, f32[16,768]{1,0:T(8,128)}) custom-call(s32[2]{0:T(128)} %lens.3, f32[2,768]{1,0:T(2,128)} %get-tuple-element.51.dyin, bf16[512,768]{1,0:T(8,128)(2,1)} %get-tuple-element.52.x, f32[16,768]{1,0:T(8,128)} %get-tuple-element.96.vec, ...), custom_call_target="tpu_custom_call" | custom-call | tf_op jit(solution)/shard_map/layer_bwd/pallas_call | solution.py:514
  300.5 0.0 copy-start.2
  300.5 36.6 %layer_bwd.3 = (bf16[512,768]{1,0:T(8,128)(2,1)}, bf16[8,1152,768]{2,1,0:T(8,128)(2,1)}, f32[16,768]{1,0:T(8,128)}) custom-call(s32[2]{0:T(128)} %lens.3, f32[512,768]{1,0:T(8,128)} %get-tuple-element.65.dyin, bf16[512,768]{1,0:T(8,128)(2,1)} %bitcast.83, f32[16,768]{1,0:T(8,128)} %get-tuple-element.95.vec, bf16[4,8,1152,768]{3,2,1,0:T(8,128)(2,1)} %get-tuple-element.54.g, ...), custom_call_target="tpu_custom_call" | custom-call | tf_op jit(solution)/shard_map/layer_bwd/pallas_call | solution.py:514
  337.1 0.0 copy-done.2
  337.1 1.4 pad_maximum_fusion.2.refs_2_
  338.5 170.6 %reduce_grads.1 = (bf16[6,384,768]{2,1,0:T(8,128)(2,1)}, f32[32,768]{1,0:T(8,128)}) custom-call(bf16[8,1152,768]{2,1,0:T(8,128)(2,1)} %get-tuple-element.77.refs_0_, bf16[8,1152,768]{2,1,0:T(8,128)(2,1)} %get-tuple-element.78.refs_1_, f32[32,768]{1,0:T(8,128)} %pad_maximum_fusion.2.refs_2_), custom_call_target="tpu_custom_call" | custom-call | tf_op jit(solution)/shard_map/reduce_grads/pallas_call | solution.py:683
  509.1 2.6 convert.1
  511.8 0.8 slice_bitcast_fusion
  512.6 1.7 reverse_bitcast_fusion
  514.3 0.2 fusion.10
  514.5 1.7 pad_maximum_fusion
  516.2 0.2 reverse_bitcast_fusion.2
  516.4 1.0 fusion.11
  517.3 0.0 copy-start.1
  517.4 0.0 copy-start.3
  517.4 0.0 copy-start
  517.4 1.3 pad_maximum_fusion.1
  518.7 0.0 copy-done.1
  518.7 0.3 slice.95
  519.0 0.7 fusion.2
  519.7 0.6 constant_dynamic-slice_fusion.7
  520.3 0.0 copy-done.3
  520.3 0.6 slice_reduce_fusion
  521.0 0.0 copy-done
  521.0 0.9 copy.82
  (10 shorter events, 0.1 us)
Async XLA Ops:
  300.5 36.6 %copy-start.2 = (f32[16,768]{1,0:T(8,128)S(1)}, f32[16,768]{1,0:T(8,128)}, u32[]{:S(2)}) copy-start(f32[16,768]{1,0:T(8,128)} %get-tuple-element.79) | copy-start | bytes 147460
  517.3 1.3 copy-start.1
  517.4 3.0 copy-start.3
  517.4 3.6 copy-start

commit v4 on v3

--- a/solution.py
+++ b/solution.py
@@ -411,242 +411,135 @@
     (5, 6, 2), (3, 7, 1), (5, 6, 3), (3, 7, 2), (5, 6, 4), (3, 7, 3), (4, 7, 0), (5, 6, 5), (5, 7, 0), (5, 7, 1),
     (5, 7, 2), (5, 7, 3), (5, 7, 4),
 )
-def bwd_kernel(l,first,lens,dyin,x,vec,g,qkv_i,pb_i,ctx_i,xh1_i,rs1_i,h1_i,act_i,der_i,xh2_i,rs2_i,
-               dx,dg,vg,wv,sv,qkv,pb,ctx,xh1,rs1,h1,act,der,xh2,rs2,dmix,dacc,dr2,dctx,dv,ds,sem,isem,osem):
-    F=g.shape[1]; r=768//F; rs_=3072//F
-    cps=load_weights(l,g,wv,sv,sem)
-    ins=[pltpu.make_async_copy(s,d,isem.at[i]) for i,(s,d) in enumerate([(qkv_i,qkv),(pb_i,pb),(ctx_i,ctx),(xh1_i,xh1),(rs1_i,rs1),(h1_i,h1),(act_i,act),(der_i,der),(xh2_i,xh2),(rs2_i,rs2)])]
-    QKV,PB,CTX,XH1,RS1,H1,ACT,DER,XH2,RS2=range(10)
-    for i in (XH2,RS2): ins[i].start()
-    for j in range(4):
-        cps[8+j].start()
-        if j==0: ins[ACT].start(); ins[DER].start(); ins[H1].start()
-        cps[4+j].start()
-    for i in (XH1,RS1,CTX): ins[i].start()
-    cps[3].start(); ins[QKV].start(); ins[PB].start()
-    for j in range(3): cps[j].start()
-    def W(j): return wv[j].reshape(768,768)
-    def S(j): return sv[j].reshape(768,768)
-    outs=[]
-    def outw(j,val):
-        if j<8:
-            dv[j]=val.astype(bf16).reshape(F,r,768)
-            cp=pltpu.make_async_copy(dv.at[j],dg.at[:,pl.ds(j*r,r),:],osem.at[j])
-        else:
-            q=j-8
-            ds[q]=val.astype(bf16).reshape(F//4,rs_,768)
-            cp=pltpu.make_async_copy(ds.at[q],dg.at[pl.ds(q*(F//4),F//4),pl.ds(8*r,rs_),:],osem.at[j])
-        cp.start(); outs.append(cp)
-    vg[...]=jnp.zeros_like(vg)
-    tpos=lax.broadcasted_iota(jnp.int32,(256,768),0)
-    if first:
-        dy=jnp.concatenate([jnp.where(tpos<lens[c],dyin[c:c+1,:],0.0) for c in range(2)],0)
-    else: dy=dyin[...]
-    def ln_back(dy,xh,rstd,gain):
-        t=dy*gain
-        return rstd*(t-jnp.mean(t,-1,keepdims=True)-xh*jnp.mean(t*xh,-1,keepdims=True))
-    def colsum(v): return jnp.sum(v,0,keepdims=True)
-    ins[XH2].wait(); ins[RS2].wait()
-    xh=xh2[...]
-    vg[6:7,:]=colsum(dy*xh); vg[7:8,:]=colsum(dy)
-    d2=ln_back(dy,xh,rs2[:,0:1],vec[6:7,:])
-    dacc[...]=d2
-    dfb=d2.astype(bf16)
-    dr2[...]=dfb
-    vg[5:6,:]=colsum(dfb.astype(f32))
-    for i in (ACT,DER,H1): ins[i].wait()
-    for j in range(4):
-        cps[8+j].wait(); cps[4+j].wait()
-        a=act[:,j*768:(j+1)*768]
-        outw(8+j,tdot(a,dr2[...]))
-        du=(dot_t(dr2[...],S(j))*der[:,j*768:(j+1)*768].astype(f32)).astype(bf16)
-        vg[8+j:9+j,:]=colsum(du.astype(f32))
-        outw(4+j,tdot(h1[...],du))
-        dacc[...]+=dot_t(du,W(4+j))
-    for i in (XH1,RS1,CTX): ins[i].wait()
-    dh=dacc[...]; xh=xh1[...]
-    vg[3:4,:]=colsum(dh*xh); vg[4:5,:]=colsum(dh)
-    d1=ln_back(dh,xh,rs1[:,0:1],vec[3:4,:])
-    dacc[...]=d1
-    dr2[...]=d1.astype(bf16)
-    vg[2:3,:]=colsum(dr2[...].astype(f32))
-    cps[3].wait()
-    outw(3,tdot(ctx[...],dr2[...]))
-    dctx[...]=dot_t(dr2[...],W(3)).astype(bf16)
-    ins[QKV].wait(); ins[PB].wait()
-    lane=lax.broadcasted_iota(jnp.int32,(256,128),1); low_half=lane<64
-    def pair(i,_):
-        c=i//6; p=i-c*6
-        rows=pl.ds(pl.multiple_of(c*256,256),256); o=pl.multiple_of(p*128,128)
-        o1=pl.multiple_of(768+o,128); o2=pl.multiple_of(1536+o,128)
-        q2=qkv[rows,pl.ds(o,128)]; k2=qkv[rows,pl.ds(o1,128)]; v2=qkv[rows,pl.ds(o2,128)]
-        dc=dctx[rows,pl.ds(o,128)]
-        res=[]
-        for hh in range(2):
-            m=low_half if hh==0 else jnp.logical_not(low_half)
-            P=pb[i*2+hh]; pf=P.astype(f32)
-            dP=dot_t(jnp.where(m,dc,jnp.zeros_like(dc)),v2)
-            pd=pf*dP
-            dS=(pd-pf*jnp.sum(pd,-1,keepdims=True)).astype(bf16)
-            res.append((dot(dS,k2),tdot(dS,q2),tdot(P,dc)))
-        sel=lambda t: jnp.where(low_half,res[0][t],res[1][t])
-        dmix[rows,pl.ds(o,128)]=(sel(0)*0.125).astype(bf16)
-        dmix[rows,pl.ds(o1,128)]=(sel(1)*0.125).astype(bf16)
-        dmix[rows,pl.ds(o2,128)]=sel(2).astype(bf16)
-        return 0
-    lax.fori_loop(0,12,pair,0,unroll=3)
-    for j in range(3):
-        cps[j].wait()
-        dm=dmix[:,j*768:(j+1)*768]
-        if j==0: vg[0:1,:]=colsum(dm.astype(f32))
-        if j==2: vg[1:2,:]=colsum(dm.astype(f32))
-        outw(j,tdot(x[...],dm))
-        dacc[...]+=dot_t(dm,W(j))
-    dx[...]=dacc[...].astype(dx.dtype)
-    for c in outs: c.wait()
-
-def layer_bwd(l,first,lens,dy,x,vec,g,saved,dxt):
-    F=g.shape[1]; sd=jax.ShapeDtypeStruct
-    V=pl.BlockSpec(memory_space=pltpu.VMEM); ANY=pl.BlockSpec(memory_space=pl.ANY)
-    S=pltpu.SemaphoreType.DMA
-    w=[pltpu.VMEM((8,F,768//F,768),bf16),pltpu.VMEM((4,F//4,3072//F,768),bf16)]
-    scr=w+[pltpu.VMEM(s.shape,s.dtype) for s in saved]+[pltpu.VMEM((512,2304),bf16),pltpu.VMEM((512,768),f32),pltpu.VMEM((512,768),bf16),pltpu.VMEM((512,768),bf16)]+w+[S((12,)),S((10,)),S((12,))]
-    return pl.pallas_call(functools.partial(bwd_kernel,l,first),out_shape=[sd((512,768),dxt),sd((F,12*768//F,768),bf16),sd((16,768),f32)],
-        in_specs=[pl.BlockSpec(memory_space=pltpu.SMEM),V,V,V]+[ANY]*11,out_specs=[V,ANY,V],scratch_shapes=scr,
-        compiler_params=pltpu.CompilerParams(vmem_limit_bytes=61<<20),name="layer_bwd")(lens,dy,x,vec,g,*saved)
-
-def sizes(F):
-    n=4*(768//F); np_=n//3; nq=n-np_
-    return n,np_,nq
-def rs_scratch(D,F,NP):
-    A=4;B=F//4;O=D//4; n,np_,nq=sizes(F); nh=n//2; Sm=pltpu.SemaphoreType.DMA
-    V=pltpu.VMEM
-    return dict(T=V((NP,F,n,384),bf16),RC=V((NP,F,n,384),bf16),RPX=V((NP,F,np_//2,384),bf16),RPY=V((NP,B-1,A,np_//2,384),bf16),
-      RQY=V((NP,B-1,A,nq,384),bf16),RQX=V((NP,A,nq//2,384),bf16),T3=V((NP,A,nh,384),bf16),RZ=V((NP,A-1,nh,384),bf16),
-      **(dict(RO=V((NP,O-1,nh,384),bf16),TO=V((NP,nh,384),bf16)) if O>1 else {}),
-      VS=V((5,32,768),f32),VRC=V((1,32,768),f32),VRX=V((1,32,768),f32),VRY=V((B-1,32,768),f32),VRZ=V((A-1,32,768),f32),
-      **(dict(VRO=V((O-1,32,768),f32)) if O>1 else {}),
-      LS=Sm((NP,)),SS=Sm((NP,8+B+A+B+A+O,)),RS=Sm((NP,8+B+A+B+A+O)),VSS=Sm((8+B+A+O,)),VRS=Sm((8+B+A+O,)))
+
+def piece_sizes(F):
+    n=4*(768//F); np_=n//3
+    return n,np_,n-np_
+
 class Reduce:
-    def __init__(self,D,F,src,fin,vin,vout,buf):
-        self.D,self.F=D,F; self.A=4; self.B=F//4; self.O=D//4
-        d=lax.axis_index("dp"); f=lax.axis_index("fsdp")
-        self.d,self.f=d,f; self.a=f//self.B; self.b=f%self.B; self.x=(d//2)%2; self.c=d%2; self.o=d//4
-        self.xd=d+2-4*self.x; self.cd=d+1-2*self.c
-        self.src,self.fin,self.vin,self.vout=src,fin,vin,vout
-        self.__dict__.update(buf); self.n,self.np,self.nq=sizes(F)
-        self.hp=self.np//2; self.hq=self.nq//2
-        self.pending=[]
-        m=pl.multiple_of
-        self.mycols=pl.ds(m(self.c*384,128),384); self.ocols=pl.ds(m((1-self.c)*384,128),384)
-        self.Pown=pl.ds(m(self.x*self.hp,16),self.hp); self.Poth=pl.ds(m((1-self.x)*self.hp,16),self.hp)
-        self.Qown=pl.ds(m(self.np+self.x*self.hq,16),self.hq); self.Qoth=pl.ds(m(self.np+(1-self.x)*self.hq,16),self.hq)
+    def __init__(self,pos,src,flush,R,outs,r):
+        self.p,self.src,self.flush,self.outs,self.r=pos,src,flush,outs,r
+        self.__dict__.update(R)
+        self.n,self.np,self.nq=piece_sizes(pos.F); self.hp=self.np//2; self.hq=self.nq//2
+        m=pl.multiple_of; c,x=pos.c,pos.x
+        self.mycols=pl.ds(m(c*384,128),384); self.ocols=pl.ds(m((1-c)*384,128),384)
+        self.Pown=pl.ds(m(x*self.hp,16),self.hp); self.Poth=pl.ds(m((1-x)*self.hp,16),self.hp)
+        self.Qown=pl.ds(m(self.np+x*self.hq,16),self.hq); self.Qoth=pl.ds(m(self.np+(1-x)*self.hq,16),self.hq)
         self.Qall=pl.ds(self.np,self.nq)
-    def peers(self):
-        out=[(self.d,(self.f+s)%self.F) for s in range(1,self.F)]
-        out+=[(self.xd,self.f),(self.cd,self.f)]+[((self.d+4*s)%self.D,self.f) for s in range(1,self.O)]
-        return out
-    def rc(self,i,k,src,dst,dev):
-        cp=pltpu.make_async_remote_copy(src,dst,self.SS.at[i,k],self.RS.at[i,k],device_id=dev,device_id_type=MESH)
-        return cp
-    def go(self,cp): cp.start(); self.pending.append(cp)
-    def kPy(self,t): return 8+t
-    def kQy(self,t): return 8+self.B+t
-    def kZ(self,s): return 8+2*self.B+s
-    def kO(self,s): return 8+2*self.B+self.A+s
-    def Yd(self,t): return (self.d,self.a*self.B+(self.b+t)%self.B)
-    def Zd(self,s): return (self.d,((self.a+s)%self.A)*self.B+self.b)
+        self.X=(pos.xd,pos.f); self.C=(pos.cd,pos.f)
+        self.busy={}
+        self.rest=[]
+    def Y(self,t): return (self.p.d,self.p.a*self.p.B+(self.p.b+t)%self.p.B)
+    def Z(self,s): return (self.p.d,((self.p.a+s)%self.p.A)*self.p.B+self.p.b)
+    def Oo(self,s): return ((self.p.d+4*s)%self.p.D,self.p.f)
+    def rc(self,i,k,src,dst,dev): return remote(src,dst,self.SS.at[i,k],self.RS.at[i,k],dev)
+    def go(self,cp,key=None):
+        cp.start()
+        if key is None: self.rest.append(cp)
+        else: self.busy.setdefault(key,[]).append(cp)
+    def free(self,key):
+        for cp in self.busy.pop(key,[]): cp.wait_send()
+    def ky(self,t): return 5+t
+    def kq(self,t): return 5+self.p.B+t
+    def kz(self,s): return 5+2*self.p.B+s
+    def ko(self,s): return 5+2*self.p.B+self.p.A+s
+    def Tv(self,i): return self.T.at[i%3].reshape(self.p.A,self.p.B,self.n,384)
+    def cC(self,i): return self.rc(i,0,self.src(i).at[:,:,self.ocols],self.RC.at[i],self.C)
+    def cPx(self,i): return self.rc(i,1,self.T.at[i%3,:,self.Poth],self.RPX.at[i],self.X)
+    def cPy(self,i,t): return self.rc(i,self.ky(t),self.Tv(i).at[:,(self.p.b+t)%self.p.B,self.Pown],self.RPY.at[i,t-1],self.Y(t))
+    def cQy(self,i,t): return self.rc(i,self.kq(t),self.Tv(i).at[:,(self.p.b+t)%self.p.B,self.Qall],self.RQY.at[i,t-1],self.Y(t))
+    def cQx(self,i): return self.rc(i,2,self.Tv(i).at[:,self.p.b,self.Qoth],self.RQX.at[i],self.X)
+    def cZ(self,i,s): return self.rc(i,self.kz(s),self.T3.at[i%3,(self.p.a+s)%self.p.A],self.RZ.at[i,s-1],self.Z(s))
+    def cO(self,i,s): return self.rc(i,self.ko(s),self.TO.at[i],self.RO.at[i,s-1],self.Oo(s))
+    def cFX(self,i,w,mine=True):
+        r=((self.Pown,self.Qown) if mine else (self.Poth,self.Qoth))[w]; v=self.FIN.at[i,r,self.mycols]
+        return self.rc(i,3+w,v,v,self.X)
+    def cFC(self,i,mine=True):
+        v=self.FIN.at[i,:,self.mycols if mine else self.ocols]
+        return self.rc(i,5,v,v,self.C)
     def s0(self,i):
-        s=self.src(i)
-        self.cC=lambda i: self.rc(i,0,self.src(i).at[:,:,self.ocols],self.RC.at[i],(self.cd,self.f))
+        self.flush(i)
         self.go(self.cC(i))
-        self.lc=lambda i: pltpu.make_async_copy(self.src(i).at[:,:,self.mycols],self.T.at[i],self.LS.at[i])
-        self.lc(i).start()
+    def loads(self,i):
+        return [pltpu.make_async_copy(self.src(i).at[:,:,self.mycols],self.T.at[i%3],self.LS.at[i,0]),
+                pltpu.make_async_copy(self.RC.at[i],self.RCV,self.LS.at[i,1])]
     def s1(self,i):
-        self.lc(i).wait(); self.cC(i).wait_recv()
-        T,RC=self.T,self.RC
+        self.free(("T",i%3))
+        self.cC(i).wait_recv()
+        for cp in self.loads(i): cp.start()
+    def s2(self,i):
+        T,k=self.T,i%3
+        for cp in self.loads(i): cp.wait()
         def body(f,_):
-            T[i,f]=(T[i,f].astype(f32)+RC[i,f].astype(f32)).astype(bf16); return 0
-        lax.fori_loop(0,self.F,body,0)
-        self.go(self.cPx(i))
-        for t in range(1,self.B):
-            for a in range(self.A): pass
-        for t in range(1,self.B):
-            fb=(self.b+t)%self.B
-            for a in range(self.A):
-                pass
-        self.startQy(i)
-    def cPx(self,i): return self.rc(i,1,self.T.at[i,:,self.Poth],self.RPX.at[i],(self.xd,self.f))
-    def Tab(self,i):
-        return self.T.at[i].reshape(self.A,self.B,self.n,384)
-    def cQy(self,i,t): return self.rc(i,self.kQy(t),self.Tab(i).at[:,(self.b+t)%self.B,self.Qall],self.RQY.at[i,t-1],self.Yd(t))
-    def cPy(self,i,t): return self.rc(i,self.kPy(t),self.Tab(i).at[:,(self.b+t)%self.B,self.Pown],self.RPY.at[i,t-1],self.Yd(t))
-    def startQy(self,i):
-        for t in range(1,self.B): self.go(self.cQy(i,t))
-    def s2(self,i):
-        T=self.T
+            T[k,f]=(T[k,f].astype(f32)+self.RCV[f].astype(f32)).astype(bf16); return 0
+        lax.fori_loop(0,self.p.F,body,0)
+        self.go(self.cPx(i),("T",k))
+        for t in range(1,self.p.B): self.go(self.cQy(i,t),("T",k))
+    def s3(self,i):
+        T,k=self.T,i%3
         self.cPx(i).wait_recv()
         def body(f,_):
-            T[i,f,self.Pown]=(T[i,f,self.Pown].astype(f32)+self.RPX[i,f].astype(f32)).astype(bf16); return 0
-        lax.fori_loop(0,self.F,body,0)
-        for t in range(1,self.B): self.go(self.cPy(i,t))
-        for t in range(1,self.B): self.cQy(i,t).wait_recv()
-        def bodyq(a,_):
-            fo=a*self.B+self.b
-            v=T[i,fo,self.Qall].astype(f32)
-            for t in range(1,self.B): v=v+self.RQY[i,t-1,a].astype(f32)
-            T[i,fo,self.Qall]=v.astype(bf16); return 0
-        lax.fori_loop(0,self.A,bodyq,0)
-        self.go(self.cQx(i))
-    def cQx(self,i): return self.rc(i,2,self.Tab(i).at[:,self.b,self.Qoth],self.RQX.at[i],(self.xd,self.f))
-    def s3(self,i):
-        for t in range(1,self.B): self.cPy(i,t).wait_recv()
+            T[k,f,self.Pown]=(T[k,f,self.Pown].astype(f32)+self.RPX[i,f].astype(f32)).astype(bf16); return 0
+        lax.fori_loop(0,self.p.F,body,0)
+        for t in range(1,self.p.B): self.go(self.cPy(i,t),("T",k))
+    def s4(self,i):
+        T,k=self.T,i%3
+        for t in range(1,self.p.B): self.cQy(i,t).wait_recv()
+        def body(a,_):
+            fo=a*self.p.B+self.p.b
+            v=T[k,fo,self.Qall].astype(f32)
+            for t in range(1,self.p.B): v=v+self.RQY[i,t-1,a].astype(f32)
+            T[k,fo,self.Qall]=v.astype(bf16); return 0
+        lax.fori_loop(0,self.p.A,body,0)
+        self.go(self.cQx(i),("T",k))
+    def s5(self,i):
+        T,k,k3=self.T,i%3,i%3
+        self.free(("T3",k3))
+        for t in range(1,self.p.B): self.cPy(i,t).wait_recv()
         self.cQx(i).wait_recv()
         def body(a,_):
-            fo=a*self.B+self.b
-            v=self.T[i,fo,self.Pown].astype(f32)
-            for t in range(1,self.B): v=v+self.RPY[i,t-1,a].astype(f32)
-            self.T3[i,a,0:self.hp]=v.astype(bf16)
-            self.T3[i,a,self.hp:self.hp+self.hq]=(self.T[i,fo,self.Qown].astype(f32)+self.RQX[i,a].astype(f32)).astype(bf16)
+            fo=a*self.p.B+self.p.b
+            v=T[k,fo,self.Pown].astype(f32)
+            for t in range(1,self.p.B): v=v+self.RPY[i,t-1,a].astype(f32)
+            self.T3[k3,a,0:self.hp]=v.astype(bf16)
+            self.T3[k3,a,self.hp:self.hp+self.hq]=(T[k,fo,self.Qown].astype(f32)+self.RQX[i,a].astype(f32)).astype(bf16)
             return 0
-        lax.fori_loop(0,self.A,body,0)
-        for s in range(1,self.A): self.go(self.cZ(i,s))
-    def cZ(self,i,s): return self.rc(i,self.kZ(s),self.T3.at[i,(self.a+s)%self.A],self.RZ.at[i,s-1],self.Zd(s))
-    def cO(self,i,s): return self.rc(i,self.kO(s),self.TO.at[i],self.RO.at[i,s-1],((self.d+4*s)%self.D,self.f))
-    def put(self,i,v):
-        v=v.astype(bf16)
-        self.fin[i,self.Pown,self.mycols]=v[:self.hp]; self.fin[i,self.Qown,self.mycols]=v[self.hp:]
-        self.go(self.cFX(i,0)); self.go(self.cFX(i,1))
-    def cFX(self,i,w):
-        r=(self.Pown,self.Qown)[w]; v=self.fin.at[i,r,self.mycols]
-        return self.rc(i,3+w,v,v,(self.xd,self.f))
-    def rFX(self,i,w):
-        r=(self.Poth,self.Qoth)[w]; v=self.fin.at[i,r,self.mycols]
-        return self.rc(i,3+w,v,v,(self.xd,self.f))
-    def s4(self,i):
-        v=self.T3[i,self.a].astype(f32)
-        for s in range(1,self.A):
+        lax.fori_loop(0,self.p.A,body,0)
+        for s in range(1,self.p.A): self.go(self.cZ(i,s),("T3",k3))
+    def s6(self,i):
+        v=self.T3[i%3,self.p.a].astype(f32)
+        for s in range(1,self.p.A):
             self.cZ(i,s).wait_recv()
             v=v+self.RZ[i,s-1].astype(f32)
-        if self.O>1:
+        if self.p.O>1:
             self.TO[i]=v.astype(bf16)
-            for s in range(1,self.O): self.go(self.cO(i,s))
-            for s in range(1,self.O):
+            for s in range(1,self.p.O): self.go(self.cO(i,s))
+            for s in range(1,self.p.O):
                 self.cO(i,s).wait_recv(); v=v+self.RO[i,s-1].astype(f32)
-        self.put(i,v)
-    def s5(self,i):
-        for w in (0,1): self.rFX(i,w).wait_recv()
-        v=self.fin.at[i,:,self.mycols]; self.go(self.rc(i,5,v,v,(self.cd,self.f)))
-    def s6(self,i):
-        v=self.fin.at[i,:,self.ocols]; self.rc(i,5,v,v,(self.cd,self.f)).wait_recv()
+        v=v.astype(bf16)
+        self.FIN[i,self.Pown,self.mycols]=v[:self.hp]; self.FIN[i,self.Qown,self.mycols]=v[self.hp:]
+        for w in (0,1): self.go(self.cFX(i,w))
+    def s7(self,i):
+        for w in (0,1): self.cFX(i,w,False).wait_recv()
+        self.go(self.cFC(i))
+    def outcps(self,i):
+        l=1-i//3; kind=i%3; r=self.r; oq,op,oe,os=self.outs; F=self.FIN.at[i]
+        if kind==0: pairs=[(F,os.at[l])]
+        elif kind==1: pairs=[(F.at[pl.ds(j*r,r)],oe.at[l,:,pl.ds(j*768,768)]) for j in range(4)]
+        else: pairs=[(F.at[pl.ds(j*r,r)],oq.at[l,:,pl.ds(j*768,768)]) for j in range(3)]+[(F.at[pl.ds(3*r,r)],op.at[l])]
+        return [pltpu.make_async_copy(s,d,self.OS.at[i,j]) for j,(s,d) in enumerate(pairs)]
+    def s8(self,i):
+        self.cFC(i,False).wait_recv()
+        for cp in self.outcps(i): cp.start()
     def vstage(self,k):
-        st=[(self.VRC,[(self.cd,self.f)],0),(self.VRX,[(self.xd,self.f)],1),(self.VRY,[self.Yd(t) for t in range(1,self.B)],8),(self.VRZ,[self.Zd(s) for s in range(1,self.A)],8+self.B)]
-        if self.O>1: st.append((self.VRO,[((self.d+4*s)%self.D,self.f) for s in range(1,self.O)],8+self.B+self.A))
+        B,A,O=self.p.B,self.p.A,self.p.O
+        st=[(self.VRC,[self.C],0),(self.VRX,[self.X],1),(self.VRY,[self.Y(t) for t in range(1,B)],2),(self.VRZ,[self.Z(s) for s in range(1,A)],2+B)]
+        if O>1: st.append((self.VRO,[self.Oo(s) for s in range(1,O)],2+B+A))
         def cps(k):
             buf,devs,k0=st[k]
-            return [pltpu.make_async_remote_copy(self.VS.at[k],buf.at[q],self.VSS.at[k0+q],self.VRS.at[k0+q],device_id=dv,device_id_type=MESH) for q,dv in enumerate(devs)]
-        if k==0: self.VS[0]=self.vin[...]
-        elif k<=len(st):
+            return [remote(self.VS.at[k],buf.at[q],self.VSS.at[k0+q],self.VRS.at[k0+q],dv) for q,dv in enumerate(devs)]
+        if k>len(st): return
+        if k>0:
             v=self.VS[k-1]
             for q,cp in enumerate(cps(k-1)):
                 cp.wait_recv(); v=v+st[k-1][0][q]
@@ -655,33 +548,192 @@
         if k<len(st):
             for cp in cps(k): self.go(cp)
     def finish(self):
-        for cp in self.pending: cp.wait_send()
-
-def rs_kernel(D,F,names,dgs,vin,fin,vout,*scr):
-    buf=dict(zip(names,scr))
-    n=4*(768//F)
-    NP=3*len(dgs)
-    src=lambda i: dgs[i//3].at[:,pl.ds((2-i%3)*n,n),:]
-    R=Reduce(D,F,src,fin,vin,vout,buf)
-    bar=pltpu.get_barrier_semaphore(); ps=R.peers()
-    for p in ps: pl.semaphore_signal(bar,inc=1,device_id=p,device_id_type=MESH)
-    pl.semaphore_wait(bar,len(ps))
-    stages=[R.s0,R.s1,R.s2,R.s3,R.s4,R.s5,R.s6]
-    for t in range(NP+6):
-        if t<6: R.vstage(t)
-        for i in range(NP):
-            if 0<=t-i<=6: stages[t-i](i)
-    R.finish()
-
-def reduce_grads(D,F,dgs,vin,cid):
-    n,np_,nq=sizes(F); NP=3*len(dgs)
-    buf=rs_scratch(D,F,NP); sd=jax.ShapeDtypeStruct
-    V=pl.BlockSpec(memory_space=pltpu.VMEM); ANY=pl.BlockSpec(memory_space=pl.ANY)
-    def k(*refs):
-        nd=len(dgs)
-        rs_kernel(D,F,list(buf),refs[:nd],refs[nd],refs[nd+1],refs[nd+2],*refs[nd+3:])
-    return pl.pallas_call(k,out_shape=[sd((NP,n,768),bf16),sd((32,768),f32)],in_specs=[ANY]*len(dgs)+[V],out_specs=[V,V],
-        scratch_shapes=list(buf.values()),compiler_params=pltpu.CompilerParams(collective_id=cid,has_side_effects=True,vmem_limit_bytes=61<<20),name="reduce_grads")(*dgs,vin)
+        for key in list(self.busy): self.free(key)
+        for cp in self.rest: cp.wait_send()
+        for i in range(6):
+            for cp in self.outcps(i): cp.wait()
+
+class Backward:
+    NAMES=("qkv","pb","ctx","xh1","rs1","h1","xh2","rs2","x")
+    SAME={"xh1":"xh","xh2":"xh","rs1":"rsd","rs2":"rsd"}
+    def __init__(self,lens,gp,vecs,g,dg,saved,xs,R,dx):
+        self.lens,self.gp,self.vecs,self.g,self.dg,self.saved,self.xs,self.dx=lens,gp,vecs,g,dg,saved,xs,dx
+        self.__dict__.update(R)
+        self.F=g.shape[1]; self.r=768//self.F; self.rs=3072//self.F
+        self.slot=0; self.stage={}; self.blocks={}
+        self.chunkno=0
+    def cp(self,l,name):
+        src=self.xs[l] if name=="x" else self.saved[l][SAVED.index(name)]
+        return pltpu.make_async_copy(src,self.__dict__[self.SAME.get(name,name)],self.isem.at[self.NAMES.index(name)])
+    def fetch(self,l,*names):
+        if l<0: return
+        for n in names: self.cp(l,n).start()
+    def need(self,l,*names):
+        for n in names: self.cp(l,n).wait()
+    def wcp(self,l,j): return pltpu.make_async_copy(self.g.at[l,:,pl.ds(j*self.r,self.r),:],self.wa.at[j],self.wsem.at[j])
+    def ccps(self,l,j):
+        s=j%2; F=self.F; cols=pl.ds(j*768,768)
+        srcs=[(self.g.at[l,:,pl.ds((4+j)*self.r,self.r),:],self.we.at[s]),(self.g.at[l,pl.ds(j*(F//4),F//4),pl.ds(8*self.r,self.rs),:],self.wsx.at[s]),
+              (self.saved[l][SAVED.index("act")].at[:,cols],self.act.at[s]),(self.saved[l][SAVED.index("der")].at[:,cols],self.der.at[s])]
+        return [pltpu.make_async_copy(a,b,self.csem.at[s,k]) for k,(a,b) in enumerate(srcs)]
+    def fetch_chunk(self,l,j):
+        if j>=4: l,j=l-1,j-4
+        if l<0: return
+        for c in self.ccps(l,j): c.start()
+    def fetch_w(self,l,*js):
+        if l<0: return
+        for j in js: self.wcp(l,j).start()
+    def put(self,l,j,val):
+        k=self.slot; self.slot=(k+1)%3
+        if k in self.stage: self.stage.pop(k).wait()
+        self.st[k]=val.astype(bf16)
+        if j<8: src,dst=self.st.at[k].reshape(self.F,self.r,768),self.dg.at[l,:,pl.ds(j*self.r,self.r)]
+        else:
+            q=j-8; n=self.F//4
+            src,dst=self.st.at[k].reshape(n,self.rs,768),self.dg.at[l,pl.ds(q*n,n),pl.ds(8*self.r,self.rs)]
+        cp=pltpu.make_async_copy(src,dst,self.ssem.at[k]); cp.start()
+        self.stage[k]=cp; self.blocks[k]=(l,j)
+    def flush(self,i):
+        l=1-i//3; lo={0:8,1:4,2:0}[i%3]
+        for k in list(self.stage):
+            bl,bj=self.blocks[k]
+            if bl==l and lo<=bj<lo+4: self.stage.pop(k).wait()
+    def first(self):
+        l=1
+        self.fetch(l,"xh2","rs2"); self.fetch_chunk(l,0); self.fetch(l,"h1"); self.fetch_chunk(l,1)
+        self.fetch(l,"ctx"); self.fetch_w(l,3); self.fetch(l,"qkv","pb"); self.fetch_w(l,0,1,2); self.fetch(l,"x")
+        self.VS[0]=jnp.zeros(self.VS.shape[1:],f32)
+    def vrow(self,l,k,val): self.VS[0,l*12+k:l*12+k+1,:]=jnp.sum(val,0,keepdims=True)
+    def steps(self,l):
+        V=lambda i: self.vecs[l,i:i+1,:]
+        r=self.r
+        def ln_back(dy,xh,rstd,gain):
+            t=dy*gain
+            return rstd*(t-jnp.mean(t,-1,keepdims=True)-xh*jnp.mean(t*xh,-1,keepdims=True))
+        def second():
+            if l==1:
+                tpos=lax.broadcasted_iota(jnp.int32,(256,768),0)
+                for c in range(2): self.acc[c*256:(c+1)*256,:]=jnp.where(tpos<self.lens[c],self.gp[c:c+1,:],0.0)
+            dy=self.acc[...]
+            self.need(l,"xh2","rs2")
+            xh=self.xh[...]
+            self.vrow(l,6,dy*xh); self.vrow(l,7,dy)
+            d2=ln_back(dy,xh,self.rsd[:,0:1],V(6))
+            self.acc[...]=d2
+            self.dr[...]=d2.astype(bf16)
+            self.vrow(l,5,self.dr[...].astype(f32))
+            self.fetch(l,"xh1","rs1")
+        def ffn(j):
+            s=j%2
+            for c in self.ccps(l,j): c.wait()
+            if j==0: self.need(l,"h1")
+            E=self.we[s].reshape(768,768); S=self.wsx[s].reshape(768,768)
+            self.put(l,8+j,tdot(self.act[s],self.dr[...]))
+            du=(dot_t(self.dr[...],S)*self.der[s].astype(f32)).astype(bf16)
+            self.vrow(l,8+j,du.astype(f32))
+            self.put(l,4+j,tdot(self.h1[...],du))
+            self.acc[...]+=dot_t(du,E)
+            self.fetch_chunk(l,j+2)
+            if j==3: self.fetch(l-1,"h1")
+        def middle():
+            self.need(l,"xh1","rs1","ctx")
+            dh=self.acc[...]; xh=self.xh[...]
+            self.vrow(l,3,dh*xh); self.vrow(l,4,dh)
+            d1=ln_back(dh,xh,self.rsd[:,0:1],V(3))
+            self.acc[...]=d1
+            self.dr[...]=d1.astype(bf16)
+            self.vrow(l,2,self.dr[...].astype(f32))
+            self.wcp(l,3).wait()
+            self.put(l,3,tdot(self.ctx[...],self.dr[...]))
+            self.ctx[...]=dot_t(self.dr[...],self.wa[3].reshape(768,768)).astype(bf16)
+            self.fetch(l-1,"xh2","rs2"); self.fetch_w(l-1,3)
+        lane=lax.broadcasted_iota(jnp.int32,(256,128),1); low_half=lane<64
+        def pair(i,_):
+            c=i//6; p=i-c*6; qkv=self.qkv
+            rows=pl.ds(pl.multiple_of(c*256,256),256); o=pl.multiple_of(p*128,128)
+            o1=pl.multiple_of(768+o,128); o2=pl.multiple_of(1536+o,128)
+            q2=qkv[rows,pl.ds(o,128)]; k2=qkv[rows,pl.ds(o1,128)]; v2=qkv[rows,pl.ds(o2,128)]
+            dc=self.ctx[rows,pl.ds(o,128)]
+            res=[]
+            for hh in range(2):
+                m=low_half if hh==0 else jnp.logical_not(low_half)
+                P=self.pb[i*2+hh]; pf=P.astype(f32)
+                dP=dot_t(jnp.where(m,dc,jnp.zeros_like(dc)),v2)
+                pd=pf*dP
+                dS=(pd-pf*jnp.sum(pd,-1,keepdims=True)).astype(bf16)
+                res.append((dot(dS,k2),tdot(dS,q2),tdot(P,dc)))
+            sel=lambda t: jnp.where(low_half,res[0][t],res[1][t])
+            qkv[rows,pl.ds(o,128)]=(sel(0)*0.125).astype(bf16)
+            qkv[rows,pl.ds(o1,128)]=(sel(1)*0.125).astype(bf16)
+            qkv[rows,pl.ds(o2,128)]=sel(2).astype(bf16)
+            return 0
+        def attend(s):
+            if s==0: self.need(l,"qkv","pb")
+            lax.fori_loop(4*s,4*s+4,pair,0,unroll=2)
+            if s==2: self.fetch(l-1,"pb","ctx")
+        def mixed(j):
+            self.wcp(l,j).wait()
+            if j==0: self.need(l,"x")
+            dm=self.qkv[:,j*768:(j+1)*768]
+            if j!=1: self.vrow(l,0 if j==0 else 1,dm.astype(f32))
+            self.put(l,j,tdot(self.x[...],dm))
+            self.acc[...]+=dot_t(dm,self.wa[j].reshape(768,768))
+            self.fetch_w(l-1,j)
+            if j==2:
+                self.fetch(l-1,"qkv","x")
+                if l==0: self.dx[...]=self.acc[...].astype(bf16)
+        P=functools.partial
+        return [second]+[P(ffn,j) for j in range(4)]+[middle]+[P(attend,s) for s in range(3)]+[P(mixed,j) for j in range(3)]
+
+def backward_kernel(D,F,order,names,lens,gp,vecs,g,x0,y0,*rest):
+    saved=(rest[0:10],rest[10:20]); dg,dx,oq,op,oe,os,vout,rcv=rest[20:28]; R=dict(zip(names,rest[28:])); R["RC"]=rcv
+    pos=Place(D,F); n=4*(768//F)
+    bar=pltpu.get_barrier_semaphore()
+    peers=[(pos.xd,pos.f),(pos.cd,pos.f)]+[(pos.d,(pos.f+s)%F) for s in range(1,F)]+[((pos.d+4*s)%D,pos.f) for s in range(1,pos.O)]
+    for dev in peers: pl.semaphore_signal(bar,inc=1,device_id=dev,device_id_type=MESH)
+    Bw=Backward(lens,gp,vecs,g,dg,saved,(x0,y0),R,dx)
+    Bw.first()
+    src=lambda i: dg.at[1-i//3,:,pl.ds((2-i%3)*n,n),:]
+    Rd=Reduce(pos,src,Bw.flush,R,(oq,op,oe,os),768//F); Rd.vout=vout
+    work={1:Bw.steps(1),0:Bw.steps(0)}
+    stages=[Rd.s0,Rd.s1,Rd.s2,Rd.s3,Rd.s4,Rd.s5,Rd.s6,Rd.s7,Rd.s8]
+    pl.semaphore_wait(bar,len(peers))
+    for kind,i,k in order:
+        if kind==0: work[i][k]()
+        elif kind==1: stages[k](i)
+        else: Rd.vstage(k)
+    Rd.finish()
+
+def backward(D,F,lens,gp,vecs,g,x0,y0,saved0,saved1,cid,order=None):
+    sd=jax.ShapeDtypeStruct; S=pltpu.SemaphoreType.DMA; VM=pltpu.VMEM
+    V=pl.BlockSpec(memory_space=pltpu.VMEM); ANY=pl.BlockSpec(memory_space=pl.ANY); SM=pl.BlockSpec(memory_space=pltpu.SMEM)
+    A=4;B=F//4;O=D//4; r=768//F; rs=3072//F; n,np_,nq=piece_sizes(F); nh=n//2; K=8+2*B+A+O
+    shp=dict(zip(SAVED,saved_shapes()))
+    buf={k:VM(shp[k].shape,shp[k].dtype) for k in ("qkv","pb","ctx","h1")}
+    buf.update(xh=VM((512,768),f32),rsd=VM((512,128),f32))
+    buf.update(x=VM((512,768),bf16),act=VM((2,512,768),bf16),der=VM((2,512,768),bf16),wa=VM((4,F,r,768),bf16),we=VM((2,F,r,768),bf16),wsx=VM((2,F//4,rs,768),bf16),
+        acc=VM((512,768),f32),dr=VM((512,768),bf16),st=VM((3,768,768),bf16),
+        T=VM((3,F,n,384),bf16),RCV=VM((F,n,384),bf16),RPX=VM((6,F,np_//2,384),bf16),RPY=VM((6,B-1,A,np_//2,384),bf16),RQY=VM((6,B-1,A,nq,384),bf16),
+        RQX=VM((6,A,nq//2,384),bf16),T3=VM((3,A,nh,384),bf16),RZ=VM((6,A-1,nh,384),bf16),FIN=VM((6,n,768),bf16),
+        VS=VM((5,24,768),f32),VRC=VM((1,24,768),f32),VRX=VM((1,24,768),f32),VRY=VM((B-1,24,768),f32),VRZ=VM((A-1,24,768),f32),
+        isem=S((9,)),wsem=S((4,)),csem=S((2,4)),ssem=S((3,)),LS=S((6,2)),OS=S((6,4)),SS=S((6,K)),RS=S((6,K)),VSS=S((K,)),VRS=S((K,)))
+    if O>1: buf.update(RO=VM((6,O-1,nh,384),bf16),TO=VM((6,nh,384),bf16),VRO=VM((O-1,24,768),f32))
+    outs=[sd((2,F,12*r,768),bf16),sd((512,768),bf16),sd((2,r,2304),bf16),sd((2,r,768),bf16),sd((2,r,3072),bf16),sd((2,rs,768),bf16),sd((24,768),f32),sd((6,F,n,384),bf16)]
+    res=pl.pallas_call(functools.partial(backward_kernel,D,F,BORDER if order is None else order,list(buf)),out_shape=outs,
+        in_specs=[SM,V,V]+[ANY]*23,out_specs=[ANY,V,ANY,ANY,ANY,ANY,V,ANY],scratch_shapes=list(buf.values()),
+        compiler_params=pltpu.CompilerParams(collective_id=cid,has_side_effects=True,vmem_limit_bytes=62<<20),name="backward")(lens,gp,vecs,g,x0,y0,*saved0,*saved1)
+    return res[1:7]
+BORDER = (
+    (0, 1, 0), (0, 1, 1), (0, 1, 2), (0, 1, 3), (0, 1, 4), (1, 0, 0), (1, 1, 0), (0, 1, 5), (0, 1, 6), (1, 0, 1),
+    (0, 1, 7), (1, 0, 2), (1, 1, 1), (0, 1, 8), (1, 1, 2), (0, 1, 9), (0, 1, 10), (1, 0, 3), (0, 1, 11), (1, 2, 0),
+    (0, 0, 0), (0, 0, 1), (1, 0, 4), (1, 1, 3), (1, 2, 1), (0, 0, 2), (1, 2, 2), (0, 0, 3), (1, 1, 4), (0, 0, 4),
+    (1, 0, 5), (1, 2, 3), (1, 3, 0), (1, 4, 0), (0, 0, 5), (0, 0, 6), (1, 1, 5), (1, 3, 1), (0, 0, 7), (1, 0, 6),
+    (1, 3, 2), (1, 4, 1), (0, 0, 8), (1, 0, 7), (1, 2, 4), (1, 4, 2), (1, 0, 8), (0, 0, 9), (1, 1, 6), (0, 0, 10),
+    (1, 3, 3), (0, 0, 11), (1, 5, 0), (2, 0, 0), (2, 0, 1), (1, 2, 5), (1, 3, 4), (1, 5, 1), (2, 0, 2), (1, 5, 2),
+    (2, 0, 3), (1, 4, 3), (2, 0, 4), (1, 1, 7), (2, 0, 5), (1, 1, 8), (1, 2, 6), (1, 4, 4), (1, 3, 5), (1, 5, 3),
+    (1, 2, 7), (1, 2, 8), (1, 3, 6), (1, 5, 4), (1, 3, 7), (1, 4, 5), (1, 3, 8), (1, 5, 5), (1, 4, 6), (1, 4, 7),
+    (1, 4, 8), (1, 5, 6), (1, 5, 7), (1, 5, 8),
+)
 
 
 def on_device(dp, fsdp, x_query, x_key, len_query, len_key, queue, *params):
@@ -703,17 +755,10 @@
     (gathered, vecs, y0, y1, loss, grad_pooled), saved0, saved1 = forward(
         dp, fsdp, len_query, len_key, x0, xk, queue, msg,
         [query_params[i] for i in big], [key_params[i] for i in big], 1)
-    dx1, d1, v1 = layer_bwd(1, True, len_query, grad_pooled, y0, vecs[1], gathered, saved1, f32)
-    dx0, d0, v0 = layer_bwd(0, False, len_query, dx1, x0, vecs[0], gathered, saved0, bf16)
-    fin, vsum = reduce_grads(dp, fsdp, [d1, d0], jnp.concatenate([v1, v0], 0), 2)
+    dx0, *grads, vsum = backward(dp, fsdp, len_query, grad_pooled, vecs, gathered, x0, y0, saved0, saved1, 2)
+    grad_qkv, grad_proj, grad_expand, sh_g = [v.astype(f32) for v in grads]
     me = lax.axis_index("fsdp")
-    n = fin.shape[1]
-    fin = fin.astype(f32).reshape(2, 3, n, width)[::-1]
-    sh_g, ex_g, at_g = fin[:, 0], fin[:, 1], fin[:, 2]
-    grad_qkv = jnp.concatenate([at_g[:, i * r : (i + 1) * r] for i in range(3)], 2)
-    grad_proj = at_g[:, 3 * r :]
-    grad_expand = jnp.concatenate([ex_g[:, i * r : (i + 1) * r] for i in range(4)], 2)
-    vsum = vsum.reshape(2, 16, width)[::-1]
+    vsum = vsum.reshape(2, 12, width)
     mine = lax.dynamic_slice_in_dim(vsum[:, :8], me * r, r, 2)
     ebg = lax.dynamic_slice_in_dim(vsum[:, 8:12].reshape(2, 4 * width), me * 4 * r, 4 * r, 1)
     qb, vb, pb, g1, b1, sb, g2, b2 = [mine[:, i] for i in range(8)]

time: 532 us -> 486 us (0.914)
  Pallas kernels: 493 us -> 454 us
    pallas_call x3 -> x1, Pallas kernels: 244 us -> 205 us  [backward(): pl.pallas_call(functools.partial(backward_kernel, D, F, BORDER if order i...]
    convert_element_type x0 -> x4, other arithmetic: none -> 6.78 us  [on_device(): grad_qkv, grad_proj, grad_expand, sh_g = [v.astype(f32) for v in grads]]
    unnamed x28 -> x33, local copies, waits for them, and re-layouts: 11.2 us -> 11.2 us
where the time goes in v4:
time: 486 us; the launch traced here: 478 us
  Pallas kernels  454 us (93%)
  local copies, waits for them, and re-layouts  14.5 us (3%)
  other arithmetic  8.83 us (2%)
    pallas_call x1, Pallas kernels, forward(): pl.pallas_call(functools.partial(forward_kernel, D, F, ORDER if order is...  249 us
    pallas_call x1, Pallas kernels, backward(): pl.pallas_call(functools.partial(backward_kernel, D, F, BORDER if order i...  205 us
    unnamed x33, local copies, waits for them, and re-layouts  11.2 us

profile of v4, /device:TPU:11, one launch (start us, length us, event | category | flops | bytes accessed | tf_op | source)
XLA Modules:
  0.0 477.9 jit_solution(2597486836821026614)
XLA Ops:
  0.6 0.7 constant_dynamic-update-slice_fusion.7
  1.3 0.7 constant_dynamic-update-slice_fusion.6
  2.0 0.7 constant_dynamic-update-slice_fusion.5
  2.6 0.7 constant_dynamic-update-slice_fusion.4
  3.3 0.7 constant_dynamic-update-slice_fusion.3
  4.0 0.7 constant_dynamic-update-slice_fusion.2
  4.6 0.7 constant_dynamic-update-slice_fusion.1
  5.3 0.7 constant_dynamic-update-slice_fusion
  5.9 0.7 constant_dynamic-update-slice_fusion.15
  6.6 0.7 constant_dynamic-update-slice_fusion.14
  7.3 0.7 constant_dynamic-update-slice_fusion.13
  8.0 0.7 constant_dynamic-update-slice_fusion.12
  8.7 0.7 constant_dynamic-update-slice_fusion.11
  9.4 0.7 constant_dynamic-update-slice_fusion.10
  10.0 0.7 constant_dynamic-update-slice_fusion.9
  10.7 0.7 constant_dynamic-update-slice_fusion.8
  11.5 0.7 add_convert_fusion.1
  12.2 0.7 maximum_bitcast_fusion
  12.9 0.6 fusion.1.msg
  13.5 249.0 %forward.1 = (bf16[4,8,1152,768]{3,2,1,0:T(8,128)(2,1)}, f32[4,16,768]{2,1,0:T(8,128)}, bf16[512,768]{1,0:T(8,128)(2,1)}, bf16[512,768]{1,0:T(8,128)(2,1)}, f32[...) custom-call(s32[2]{0:T(128)} %lens.1, s32[2]{0:T(128)} %lenk.1, ...), custom_call_target="tpu_custom_call" | custom-call | tf_op jit(solution)/shard_map/forward/pallas_call | solution.py:392
  262.5 204.5 %backward.1 = (bf16[2,8,1152,768]{3,2,1,0:T(8,128)(2,1)}, bf16[512,768]{1,0:T(8,128)(2,1)}, bf16[2,96,2304]{2,1,0:T(8,128)(2,1)}, bf16[2,96,768]{2,1,0:T(8,128)(...) custom-call(s32[2]{0:T(128)} %lens.1, ...), custom_call_target="tpu_custom_call" | custom-call | tf_op jit(solution)/shard_map/backward/pallas_call | solution.py:722
  467.1 0.0 copy-start
  467.1 3.0 convert_element_type.34
  470.1 0.0 copy-start.1
  470.1 0.0 copy-done
  470.1 0.0 copy-start.4
  470.1 1.6 convert_element_type.35
  471.7 0.0 copy-start.5
  471.7 0.0 copy-start.6
  471.7 0.0 copy-start.2
  471.7 0.0 copy-done.1
  471.7 0.0 copy-start.3
  471.7 1.3 convert_element_type.32
  473.0 0.0 copy-done.4
  473.0 0.9 convert_element_type.33
  473.9 0.0 copy-done.5
  473.9 0.7 constant_dynamic-slice_fusion.8
  474.6 0.6 constant_dynamic-slice_fusion.7
  475.2 0.0 copy-done.6
  475.2 0.6 slice_reduce_fusion
  475.9 0.0 copy-done.2
  475.9 0.9 copy.72
  476.7 0.0 copy-done.3
  476.7 0.9 copy.73
  (9 shorter events, 0.1 us)
Async XLA Ops:
  467.1 3.0 copy-start
  470.1 1.6 copy-start.1
  470.1 2.9 copy-start.4
  471.7 2.2 copy-start.5
  471.7 3.5 copy-start.6
  471.7 4.2 copy-start.2
  471.7 5.0 %copy-start.3 = (bf16[512,768]{1,0:T(8,128)(2,1)S(1)}, bf16[512,768]{1,0:T(8,128)(2,1)}, u32[]{:S(2)}) copy-start(bf16[512,768]{1,0:T(8,128)(2,1)} %get-tuple-element.73) | copy-start | bytes 2359300

commit v5 on v4

--- a/solution.py
+++ b/solution.py
@@ -412,20 +412,30 @@
     (5, 7, 2), (5, 7, 3), (5, 7, 4),
 )
 
-def piece_sizes(F):
-    n=4*(768//F); np_=n//3
-    return n,np_,n-np_
-
+PROWS=(32,64,192,192,64,64,160,32,128)
+class Piece:
+    pass
+def pieces(F):
+    r=768//F; fine=r%32==0
+    ffn=[range(4,6),range(6,8),range(8,12)]
+    attn=[range(3,4),range(0,3)] if fine else [range(0,4)]
+    out=[]; o=dict(n=0,hp=0,q=0,hq=0,h=0)
+    for l,parts in ((1,ffn+[range(0,4)]),(0,ffn+attn)):
+        for blocks in parts:
+            p=Piece(); p.l,p.blocks,p.row,p.n=l,blocks,blocks[0]*r,len(blocks)*r
+            p.np=PROWS[len(out)]*r//96 if fine else p.n//96*32
+            p.nq=p.n-p.np; p.hp,p.hq=p.np//2,p.nq//2; p.h=p.hp+p.hq
+            p.on,p.ohp,p.oq,p.ohq,p.oh=o["n"],o["hp"],o["q"],o["hq"],o["h"]
+            o["n"]+=p.n; o["hp"]+=p.hp; o["q"]+=p.nq; o["hq"]+=p.hq; o["h"]+=p.h
+            out.append(p)
+    return out,o
 class Reduce:
-    def __init__(self,pos,src,flush,R,outs,r):
-        self.p,self.src,self.flush,self.outs,self.r=pos,src,flush,outs,r
+    def __init__(self,pos,dg,flush,R,outs,r):
+        self.p,self.dg,self.flush,self.outs,self.r=pos,dg,flush,outs,r
         self.__dict__.update(R)
-        self.n,self.np,self.nq=piece_sizes(pos.F); self.hp=self.np//2; self.hq=self.nq//2
-        m=pl.multiple_of; c,x=pos.c,pos.x
+        self.pc,_=pieces(pos.F)
+        m=pl.multiple_of; c=pos.c
         self.mycols=pl.ds(m(c*384,128),384); self.ocols=pl.ds(m((1-c)*384,128),384)
-        self.Pown=pl.ds(m(x*self.hp,16),self.hp); self.Poth=pl.ds(m((1-x)*self.hp,16),self.hp)
-        self.Qown=pl.ds(m(self.np+x*self.hq,16),self.hq); self.Qoth=pl.ds(m(self.np+(1-x)*self.hq,16),self.hq)
-        self.Qall=pl.ds(self.np,self.nq)
         self.X=(pos.xd,pos.f); self.C=(pos.cd,pos.f)
         self.busy={}
         self.rest=[]
@@ -443,90 +453,111 @@
     def kq(self,t): return 5+self.p.B+t
     def kz(self,s): return 5+2*self.p.B+s
     def ko(self,s): return 5+2*self.p.B+self.p.A+s
-    def Tv(self,i): return self.T.at[i%3].reshape(self.p.A,self.p.B,self.n,384)
-    def cC(self,i): return self.rc(i,0,self.src(i).at[:,:,self.ocols],self.RC.at[i],self.C)
-    def cPx(self,i): return self.rc(i,1,self.T.at[i%3,:,self.Poth],self.RPX.at[i],self.X)
-    def cPy(self,i,t): return self.rc(i,self.ky(t),self.Tv(i).at[:,(self.p.b+t)%self.p.B,self.Pown],self.RPY.at[i,t-1],self.Y(t))
-    def cQy(self,i,t): return self.rc(i,self.kq(t),self.Tv(i).at[:,(self.p.b+t)%self.p.B,self.Qall],self.RQY.at[i,t-1],self.Y(t))
-    def cQx(self,i): return self.rc(i,2,self.Tv(i).at[:,self.p.b,self.Qoth],self.RQX.at[i],self.X)
-    def cZ(self,i,s): return self.rc(i,self.kz(s),self.T3.at[i%3,(self.p.a+s)%self.p.A],self.RZ.at[i,s-1],self.Z(s))
-    def cO(self,i,s): return self.rc(i,self.ko(s),self.TO.at[i],self.RO.at[i,s-1],self.Oo(s))
+    def Prow(self,i,mine):
+        q=self.pc[i]; x=self.p.x if mine else 1-self.p.x
+        return pl.ds(pl.multiple_of(x*q.hp,16),q.hp)
+    def Qrow(self,i,mine):
+        q=self.pc[i]; x=self.p.x if mine else 1-self.p.x
+        return pl.ds(pl.multiple_of(q.np+x*q.hq,16),q.hq)
+    def Qall(self,i): return pl.ds(self.pc[i].np,self.pc[i].nq)
+    def src(self,i): q=self.pc[i]; return self.dg.at[q.l,:,pl.ds(q.row,q.n)]
+    def Tv(self,i): return self.T.at[i%3].reshape(self.p.A,self.p.B,self.T.shape[2],384)
+    def bhp(self,i): return pl.ds(self.pc[i].ohp,self.pc[i].hp)
+    def bq(self,i): return pl.ds(self.pc[i].oq,self.pc[i].nq)
+    def bhq(self,i): return pl.ds(self.pc[i].ohq,self.pc[i].hq)
+    def bh(self,i): return pl.ds(self.pc[i].oh,self.pc[i].h)
+    def bn(self,i): return pl.ds(self.pc[i].on,self.pc[i].n)
+    def cC(self,i): return self.rc(i,0,self.src(i).at[:,:,self.ocols],self.RC.at[:,self.bn(i)],self.C)
+    def cPx(self,i): return self.rc(i,1,self.T.at[i%3,:,self.Prow(i,False)],self.RPX.at[:,self.bhp(i)],self.X)
+    def cPy(self,i,t): return self.rc(i,self.ky(t),self.Tv(i).at[:,(self.p.b+t)%self.p.B,self.Prow(i,True)],self.RPY.at[t-1,:,self.bhp(i)],self.Y(t))
+    def cQy(self,i,t): return self.rc(i,self.kq(t),self.Tv(i).at[:,(self.p.b+t)%self.p.B,self.Qall(i)],self.RQY.at[t-1,:,self.bq(i)],self.Y(t))
+    def cQx(self,i): return self.rc(i,2,self.Tv(i).at[:,self.p.b,self.Qrow(i,False)],self.RQX.at[:,self.bhq(i)],self.X)
+    def cZ(self,i,s): return self.rc(i,self.kz(s),self.T3.at[i%3,(self.p.a+s)%self.p.A,0:self.pc[i].h],self.RZ.at[s-1,self.bh(i)],self.Z(s))
+    def cO(self,i,s): return self.rc(i,self.ko(s),self.TO.at[self.bh(i)],self.RO.at[s-1,self.bh(i)],self.Oo(s))
+    def fin(self,i,rows): return pl.ds(pl.multiple_of(self.pc[i].on+rows.start,16),rows.size)
     def cFX(self,i,w,mine=True):
-        r=((self.Pown,self.Qown) if mine else (self.Poth,self.Qoth))[w]; v=self.FIN.at[i,r,self.mycols]
+        r=(self.Prow,self.Qrow)[w](i,mine); v=self.FIN.at[self.fin(i,r),self.mycols]
         return self.rc(i,3+w,v,v,self.X)
     def cFC(self,i,mine=True):
-        v=self.FIN.at[i,:,self.mycols if mine else self.ocols]
+        v=self.FIN.at[self.bn(i),self.mycols if mine else self.ocols]
         return self.rc(i,5,v,v,self.C)
     def s0(self,i):
-        self.flush(i)
+        self.flush(self.pc[i])
         self.go(self.cC(i))
     def loads(self,i):
-        return [pltpu.make_async_copy(self.src(i).at[:,:,self.mycols],self.T.at[i%3],self.LS.at[i,0]),
-                pltpu.make_async_copy(self.RC.at[i],self.RCV,self.LS.at[i,1])]
+        n=self.pc[i].n
+        return [pltpu.make_async_copy(self.src(i).at[:,:,self.mycols],self.T.at[i%3,:,0:n],self.LS.at[i,0]),
+                pltpu.make_async_copy(self.RC.at[:,self.bn(i)],self.RCV.at[:,0:n],self.LS.at[i,1])]
     def s1(self,i):
         self.free(("T",i%3))
         self.cC(i).wait_recv()
         for cp in self.loads(i): cp.start()
     def s2(self,i):
-        T,k=self.T,i%3
+        T,k,n=self.T,i%3,self.pc[i].n
         for cp in self.loads(i): cp.wait()
         def body(f,_):
-            T[k,f]=(T[k,f].astype(f32)+self.RCV[f].astype(f32)).astype(bf16); return 0
+            T[k,f,0:n]=(T[k,f,0:n].astype(f32)+self.RCV[f,0:n].astype(f32)).astype(bf16); return 0
         lax.fori_loop(0,self.p.F,body,0)
         self.go(self.cPx(i),("T",k))
         for t in range(1,self.p.B): self.go(self.cQy(i,t),("T",k))
     def s3(self,i):
-        T,k=self.T,i%3
+        T,k=self.T,i%3; own=self.Prow(i,True)
         self.cPx(i).wait_recv()
         def body(f,_):
-            T[k,f,self.Pown]=(T[k,f,self.Pown].astype(f32)+self.RPX[i,f].astype(f32)).astype(bf16); return 0
+            T[k,f,own]=(T[k,f,own].astype(f32)+self.RPX[f,self.bhp(i)].astype(f32)).astype(bf16); return 0
         lax.fori_loop(0,self.p.F,body,0)
         for t in range(1,self.p.B): self.go(self.cPy(i,t),("T",k))
     def s4(self,i):
-        T,k=self.T,i%3
+        T,k=self.T,i%3; al=self.Qall(i)
         for t in range(1,self.p.B): self.cQy(i,t).wait_recv()
         def body(a,_):
             fo=a*self.p.B+self.p.b
-            v=T[k,fo,self.Qall].astype(f32)
-            for t in range(1,self.p.B): v=v+self.RQY[i,t-1,a].astype(f32)
-            T[k,fo,self.Qall]=v.astype(bf16); return 0
+            v=T[k,fo,al].astype(f32)
+            for t in range(1,self.p.B): v=v+self.RQY[t-1,a,self.bq(i)].astype(f32)
+            T[k,fo,al]=v.astype(bf16); return 0
         lax.fori_loop(0,self.p.A,body,0)
         self.go(self.cQx(i),("T",k))
     def s5(self,i):
-        T,k,k3=self.T,i%3,i%3
-        self.free(("T3",k3))
+        T,k=self.T,i%3; q=self.pc[i]
+        self.free(("T3",k))
         for t in range(1,self.p.B): self.cPy(i,t).wait_recv()
         self.cQx(i).wait_recv()
         def body(a,_):
             fo=a*self.p.B+self.p.b
-            v=T[k,fo,self.Pown].astype(f32)
-            for t in range(1,self.p.B): v=v+self.RPY[i,t-1,a].astype(f32)
-            self.T3[k3,a,0:self.hp]=v.astype(bf16)
-            self.T3[k3,a,self.hp:self.hp+self.hq]=(T[k,fo,self.Qown].astype(f32)+self.RQX[i,a].astype(f32)).astype(bf16)
+            v=T[k,fo,self.Prow(i,True)].astype(f32)
+            for t in range(1,self.p.B): v=v+self.RPY[t-1,a,self.bhp(i)].astype(f32)
+            self.T3[k,a,0:q.hp]=v.astype(bf16)
+            self.T3[k,a,q.hp:q.h]=(T[k,fo,self.Qrow(i,True)].astype(f32)+self.RQX[a,self.bhq(i)].astype(f32)).astype(bf16)
             return 0
         lax.fori_loop(0,self.p.A,body,0)
-        for s in range(1,self.p.A): self.go(self.cZ(i,s),("T3",k3))
+        for s in range(1,self.p.A): self.go(self.cZ(i,s),("T3",k))
     def s6(self,i):
-        v=self.T3[i%3,self.p.a].astype(f32)
+        q=self.pc[i]
+        v=self.T3[i%3,self.p.a,0:q.h].astype(f32)
         for s in range(1,self.p.A):
             self.cZ(i,s).wait_recv()
-            v=v+self.RZ[i,s-1].astype(f32)
+            v=v+self.RZ[s-1,self.bh(i)].astype(f32)
         if self.p.O>1:
-            self.TO[i]=v.astype(bf16)
+            self.TO[self.bh(i)]=v.astype(bf16)
             for s in range(1,self.p.O): self.go(self.cO(i,s))
             for s in range(1,self.p.O):
-                self.cO(i,s).wait_recv(); v=v+self.RO[i,s-1].astype(f32)
+                self.cO(i,s).wait_recv(); v=v+self.RO[s-1,self.bh(i)].astype(f32)
         v=v.astype(bf16)
-        self.FIN[i,self.Pown,self.mycols]=v[:self.hp]; self.FIN[i,self.Qown,self.mycols]=v[self.hp:]
+        self.FIN[self.fin(i,self.Prow(i,True)),self.mycols]=v[:q.hp]; self.FIN[self.fin(i,self.Qrow(i,True)),self.mycols]=v[q.hp:]
         for w in (0,1): self.go(self.cFX(i,w))
     def s7(self,i):
         for w in (0,1): self.cFX(i,w,False).wait_recv()
         self.go(self.cFC(i))
     def outcps(self,i):
-        l=1-i//3; kind=i%3; r=self.r; oq,op,oe,os=self.outs; F=self.FIN.at[i]
-        if kind==0: pairs=[(F,os.at[l])]
-        elif kind==1: pairs=[(F.at[pl.ds(j*r,r)],oe.at[l,:,pl.ds(j*768,768)]) for j in range(4)]
-        else: pairs=[(F.at[pl.ds(j*r,r)],oq.at[l,:,pl.ds(j*768,768)]) for j in range(3)]+[(F.at[pl.ds(3*r,r)],op.at[l])]
+        q=self.pc[i]; r=self.r; oq,op,oe,os=self.outs
+        if q.blocks[0]==8: pairs=[(self.FIN.at[self.bn(i)],os.at[q.l])]
+        else:
+            pairs=[]
+            for k,b in enumerate(q.blocks):
+                v=self.FIN.at[pl.ds(q.on+k*r,r)]
+                if b<3: pairs.append((v,oq.at[q.l,:,pl.ds(b*768,768)]))
+                elif b==3: pairs.append((v,op.at[q.l]))
+                else: pairs.append((v,oe.at[q.l,:,pl.ds((b-4)*768,768)]))
         return [pltpu.make_async_copy(s,d,self.OS.at[i,j]) for j,(s,d) in enumerate(pairs)]
     def s8(self,i):
         self.cFC(i,False).wait_recv()
@@ -550,7 +581,7 @@
     def finish(self):
         for key in list(self.busy): self.free(key)
         for cp in self.rest: cp.wait_send()
-        for i in range(6):
+        for i in range(len(self.pc)):
             for cp in self.outcps(i): cp.wait()
 
 class Backward:
@@ -593,11 +624,10 @@
             src,dst=self.st.at[k].reshape(n,self.rs,768),self.dg.at[l,pl.ds(q*n,n),pl.ds(8*self.r,self.rs)]
         cp=pltpu.make_async_copy(src,dst,self.ssem.at[k]); cp.start()
         self.stage[k]=cp; self.blocks[k]=(l,j)
-    def flush(self,i):
-        l=1-i//3; lo={0:8,1:4,2:0}[i%3]
+    def flush(self,piece):
         for k in list(self.stage):
-            bl,bj=self.blocks[k]
-            if bl==l and lo<=bj<lo+4: self.stage.pop(k).wait()
+            l,j=self.blocks[k]
+            if l==piece.l and j in piece.blocks: self.stage.pop(k).wait()
     def first(self):
         l=1
         self.fetch(l,"xh2","rs2"); self.fetch_chunk(l,0); self.fetch(l,"h1"); self.fetch_chunk(l,1)
@@ -687,14 +717,13 @@
 
 def backward_kernel(D,F,order,names,lens,gp,vecs,g,x0,y0,*rest):
     saved=(rest[0:10],rest[10:20]); dg,dx,oq,op,oe,os,vout,rcv=rest[20:28]; R=dict(zip(names,rest[28:])); R["RC"]=rcv
-    pos=Place(D,F); n=4*(768//F)
+    pos=Place(D,F)
     bar=pltpu.get_barrier_semaphore()
     peers=[(pos.xd,pos.f),(pos.cd,pos.f)]+[(pos.d,(pos.f+s)%F) for s in range(1,F)]+[((pos.d+4*s)%D,pos.f) for s in range(1,pos.O)]
     for dev in peers: pl.semaphore_signal(bar,inc=1,device_id=dev,device_id_type=MESH)
     Bw=Backward(lens,gp,vecs,g,dg,saved,(x0,y0),R,dx)
     Bw.first()
-    src=lambda i: dg.at[1-i//3,:,pl.ds((2-i%3)*n,n),:]
-    Rd=Reduce(pos,src,Bw.flush,R,(oq,op,oe,os),768//F); Rd.vout=vout
+    Rd=Reduce(pos,dg,Bw.flush,R,(oq,op,oe,os),768//F); Rd.vout=vout
     work={1:Bw.steps(1),0:Bw.steps(0)}
     stages=[Rd.s0,Rd.s1,Rd.s2,Rd.s3,Rd.s4,Rd.s5,Rd.s6,Rd.s7,Rd.s8]
     pl.semaphore_wait(bar,len(peers))
@@ -707,32 +736,48 @@
 def backward(D,F,lens,gp,vecs,g,x0,y0,saved0,saved1,cid,order=None):
     sd=jax.ShapeDtypeStruct; S=pltpu.SemaphoreType.DMA; VM=pltpu.VMEM
     V=pl.BlockSpec(memory_space=pltpu.VMEM); ANY=pl.BlockSpec(memory_space=pl.ANY); SM=pl.BlockSpec(memory_space=pltpu.SMEM)
-    A=4;B=F//4;O=D//4; r=768//F; rs=3072//F; n,np_,nq=piece_sizes(F); nh=n//2; K=8+2*B+A+O
+    A=4;B=F//4;O=D//4; r=768//F; rs=3072//F; n=4*r; pcs,o=pieces(F); NP=len(pcs); hmax=max(p.h for p in pcs); K=8+2*B+A+O
     shp=dict(zip(SAVED,saved_shapes()))
     buf={k:VM(shp[k].shape,shp[k].dtype) for k in ("qkv","pb","ctx","h1")}
     buf.update(xh=VM((512,768),f32),rsd=VM((512,128),f32))
     buf.update(x=VM((512,768),bf16),act=VM((2,512,768),bf16),der=VM((2,512,768),bf16),wa=VM((4,F,r,768),bf16),we=VM((2,F,r,768),bf16),wsx=VM((2,F//4,rs,768),bf16),
         acc=VM((512,768),f32),dr=VM((512,768),bf16),st=VM((3,768,768),bf16),
-        T=VM((3,F,n,384),bf16),RCV=VM((F,n,384),bf16),RPX=VM((6,F,np_//2,384),bf16),RPY=VM((6,B-1,A,np_//2,384),bf16),RQY=VM((6,B-1,A,nq,384),bf16),
-        RQX=VM((6,A,nq//2,384),bf16),T3=VM((3,A,nh,384),bf16),RZ=VM((6,A-1,nh,384),bf16),FIN=VM((6,n,768),bf16),
+        T=VM((3,F,n,384),bf16),RCV=VM((F,n,384),bf16),RPX=VM((F,o["hp"],384),bf16),RPY=VM((B-1,A,o["hp"],384),bf16),RQY=VM((B-1,A,o["q"],384),bf16),
+        RQX=VM((A,o["hq"],384),bf16),T3=VM((3,A,hmax,384),bf16),RZ=VM((A-1,o["h"],384),bf16),FIN=VM((o["n"],768),bf16),
         VS=VM((5,24,768),f32),VRC=VM((1,24,768),f32),VRX=VM((1,24,768),f32),VRY=VM((B-1,24,768),f32),VRZ=VM((A-1,24,768),f32),
-        isem=S((9,)),wsem=S((4,)),csem=S((2,4)),ssem=S((3,)),LS=S((6,2)),OS=S((6,4)),SS=S((6,K)),RS=S((6,K)),VSS=S((K,)),VRS=S((K,)))
-    if O>1: buf.update(RO=VM((6,O-1,nh,384),bf16),TO=VM((6,nh,384),bf16),VRO=VM((O-1,24,768),f32))
-    outs=[sd((2,F,12*r,768),bf16),sd((512,768),bf16),sd((2,r,2304),bf16),sd((2,r,768),bf16),sd((2,r,3072),bf16),sd((2,rs,768),bf16),sd((24,768),f32),sd((6,F,n,384),bf16)]
-    res=pl.pallas_call(functools.partial(backward_kernel,D,F,BORDER if order is None else order,list(buf)),out_shape=outs,
+        isem=S((9,)),wsem=S((4,)),csem=S((2,4)),ssem=S((3,)),LS=S((NP,2)),OS=S((NP,4)),SS=S((NP,K)),RS=S((NP,K)),VSS=S((K,)),VRS=S((K,)))
+    if O>1: buf.update(RO=VM((O-1,o["h"],384),bf16),TO=VM((o["h"],384),bf16),VRO=VM((O-1,24,768),f32))
+    outs=[sd((2,F,12*r,768),bf16),sd((512,768),bf16),sd((2,r,2304),bf16),sd((2,r,768),bf16),sd((2,r,3072),bf16),sd((2,rs,768),bf16),sd((24,768),f32),sd((F,o["n"],384),bf16)]
+    res=pl.pallas_call(functools.partial(backward_kernel,D,F,(BORDER if r%32==0 else BORDER_COARSE) if order is None else order,list(buf)),out_shape=outs,
         in_specs=[SM,V,V]+[ANY]*23,out_specs=[ANY,V,ANY,ANY,ANY,ANY,V,ANY],scratch_shapes=list(buf.values()),
         compiler_params=pltpu.CompilerParams(collective_id=cid,has_side_effects=True,vmem_limit_bytes=62<<20),name="backward")(lens,gp,vecs,g,x0,y0,*saved0,*saved1)
     return res[1:7]
 BORDER = (
-    (0, 1, 0), (0, 1, 1), (0, 1, 2), (0, 1, 3), (0, 1, 4), (1, 0, 0), (1, 1, 0), (0, 1, 5), (0, 1, 6), (1, 0, 1),
-    (0, 1, 7), (1, 0, 2), (1, 1, 1), (0, 1, 8), (1, 1, 2), (0, 1, 9), (0, 1, 10), (1, 0, 3), (0, 1, 11), (1, 2, 0),
-    (0, 0, 0), (0, 0, 1), (1, 0, 4), (1, 1, 3), (1, 2, 1), (0, 0, 2), (1, 2, 2), (0, 0, 3), (1, 1, 4), (0, 0, 4),
-    (1, 0, 5), (1, 2, 3), (1, 3, 0), (1, 4, 0), (0, 0, 5), (0, 0, 6), (1, 1, 5), (1, 3, 1), (0, 0, 7), (1, 0, 6),
-    (1, 3, 2), (1, 4, 1), (0, 0, 8), (1, 0, 7), (1, 2, 4), (1, 4, 2), (1, 0, 8), (0, 0, 9), (1, 1, 6), (0, 0, 10),
-    (1, 3, 3), (0, 0, 11), (1, 5, 0), (2, 0, 0), (2, 0, 1), (1, 2, 5), (1, 3, 4), (1, 5, 1), (2, 0, 2), (1, 5, 2),
-    (2, 0, 3), (1, 4, 3), (2, 0, 4), (1, 1, 7), (2, 0, 5), (1, 1, 8), (1, 2, 6), (1, 4, 4), (1, 3, 5), (1, 5, 3),
-    (1, 2, 7), (1, 2, 8), (1, 3, 6), (1, 5, 4), (1, 3, 7), (1, 4, 5), (1, 3, 8), (1, 5, 5), (1, 4, 6), (1, 4, 7),
-    (1, 4, 8), (1, 5, 6), (1, 5, 7), (1, 5, 8),
+    (0, 1, 0), (0, 1, 1), (0, 1, 2), (1, 0, 0), (0, 1, 3), (1, 0, 1), (0, 1, 4), (1, 0, 2), (1, 1, 0), (1, 2, 0),
+    (0, 1, 5), (1, 0, 3), (1, 1, 1), (0, 1, 6), (1, 1, 2), (1, 2, 1), (0, 1, 7), (1, 0, 4), (1, 2, 2), (1, 1, 3),
+    (0, 1, 8), (0, 1, 9), (1, 0, 5), (1, 1, 4), (0, 1, 10), (0, 1, 11), (1, 3, 0), (0, 0, 0), (1, 0, 6), (0, 0, 1),
+    (1, 2, 3), (1, 2, 4), (1, 1, 5), (1, 3, 1), (0, 0, 2), (1, 0, 7), (1, 3, 2), (1, 4, 0), (0, 0, 3), (1, 0, 8),
+    (1, 1, 6), (1, 2, 5), (1, 4, 1), (0, 0, 4), (1, 4, 2), (1, 5, 0), (1, 6, 0), (0, 0, 5), (1, 1, 7), (1, 3, 3),
+    (1, 3, 4), (1, 5, 1), (1, 7, 0), (1, 4, 3), (0, 0, 6), (1, 1, 8), (1, 2, 6), (1, 4, 4), (1, 5, 2), (0, 0, 7),
+    (1, 2, 7), (1, 3, 5), (1, 6, 1), (0, 0, 8), (1, 2, 8), (1, 4, 5), (1, 6, 2), (1, 7, 1), (0, 0, 9), (1, 5, 3),
+    (1, 5, 4), (1, 7, 2), (0, 0, 10), (0, 0, 11), (1, 3, 6), (1, 8, 0), (2, 0, 0), (1, 6, 3), (2, 0, 1), (1, 4, 6),
+    (1, 6, 4), (2, 0, 2), (1, 5, 5), (1, 7, 3), (1, 8, 1), (2, 0, 3), (1, 8, 2), (1, 3, 7), (1, 7, 4), (1, 4, 7),
+    (2, 0, 4), (1, 3, 8), (1, 4, 8), (1, 5, 6), (2, 0, 5), (1, 6, 5), (1, 8, 3), (1, 8, 4), (1, 7, 5), (1, 5, 7),
+    (1, 5, 8), (1, 6, 6), (1, 8, 5), (1, 7, 6), (1, 6, 7), (1, 7, 7), (1, 6, 8), (1, 7, 8), (1, 8, 6), (1, 8, 7),
+    (1, 8, 8),
+)
+BORDER_COARSE = (
+    (0, 1, 0), (0, 1, 1), (0, 1, 2), (1, 0, 0), (0, 1, 3), (1, 0, 1), (0, 1, 4), (1, 0, 2), (1, 1, 0), (1, 2, 0),
+    (0, 1, 5), (1, 1, 1), (0, 1, 6), (1, 0, 3), (1, 1, 2), (1, 0, 4), (1, 2, 1), (0, 1, 7), (1, 2, 2), (1, 1, 3),
+    (0, 1, 8), (1, 0, 5), (0, 1, 9), (1, 1, 4), (0, 1, 10), (0, 1, 11), (1, 3, 0), (1, 2, 3), (1, 0, 6), (0, 0, 0),
+    (0, 0, 1), (1, 0, 7), (1, 2, 4), (1, 3, 1), (0, 0, 2), (1, 0, 8), (1, 1, 5), (1, 3, 2), (1, 4, 0), (0, 0, 3),
+    (1, 2, 5), (1, 4, 1), (0, 0, 4), (1, 1, 6), (1, 3, 3), (1, 4, 2), (1, 5, 0), (1, 6, 0), (0, 0, 5), (1, 1, 7),
+    (1, 5, 1), (1, 3, 4), (1, 4, 3), (0, 0, 6), (1, 1, 8), (1, 2, 6), (1, 5, 2), (0, 0, 7), (1, 3, 5), (1, 6, 1),
+    (0, 0, 8), (1, 2, 7), (1, 4, 4), (1, 6, 2), (1, 2, 8), (1, 5, 3), (0, 0, 9), (0, 0, 10), (1, 4, 5), (1, 5, 4),
+    (0, 0, 11), (1, 3, 6), (1, 7, 0), (2, 0, 0), (1, 6, 3), (2, 0, 1), (1, 4, 6), (1, 7, 1), (2, 0, 2), (1, 7, 2),
+    (1, 3, 7), (2, 0, 3), (1, 6, 4), (1, 3, 8), (1, 4, 7), (1, 5, 5), (2, 0, 4), (1, 4, 8), (2, 0, 5), (1, 7, 3),
+    (1, 5, 6), (1, 6, 5), (1, 5, 7), (1, 5, 8), (1, 7, 4), (1, 6, 6), (1, 7, 5), (1, 6, 7), (1, 6, 8), (1, 7, 6),
+    (1, 7, 7), (1, 7, 8),
 )
 
 
@@ -741,8 +786,15 @@
     num_crops, seq_len, width = x_query.shape
     r = width // fsdp
     order = (1, 2, 4, 5, 6, 10, 11, 12)
-    small_q = jnp.stack([query_params[i] for i in order], 1)
-    small_k = jnp.stack([key_params[i] for i in order], 1)
+    row = lax.broadcasted_iota(jnp.int32, (2, 8, r), 1)
+
+    def stacked(params):
+        out = params[order[0]][:, None, :]
+        for k in range(1, 8):
+            out = jnp.where(row == k, params[order[k]][:, None, :], out)
+        return out
+
+    small_q, small_k = stacked(query_params), stacked(key_params)
     bias_q, bias_k = query_params[8], key_params[8]
     mix = lambda k, q: (MOM * k + (1.0 - MOM) * q.astype(f32)).astype(bf16)
     small = jnp.concatenate([small_q, mix(small_k, small_q)], 0).reshape(32, r)

time: 486 us -> 449 us (0.924)
  Pallas kernels: 454 us -> 426 us
  local copies, waits for them, and re-layouts: 14.5 us -> 3.73 us
    pallas_call x1, Pallas kernels: 205 us -> 177 us  [backward(): pl.pallas_call(functools.partial(backward_kernel, D, F, (BORDER if r % 32...]
    unnamed x33 -> x19, local copies, waits for them, and re-layouts: 11.2 us -> 1.81 us
where the time goes in v5:
time: 449 us; the launch traced here: 441 us
  Pallas kernels  426 us (95%)
  other arithmetic  10.6 us (2%)
    pallas_call x1, Pallas kernels, forward(): pl.pallas_call(functools.partial(forward_kernel, D, F, ORDER if order is...  249 us
    pallas_call x1, Pallas kernels, backward(): pl.pallas_call(functools.partial(backward_kernel, D, F, (BORDER if r % 32...  177 us

profile of v5, /device:TPU:11, one launch (start us, length us, event | category | flops | bytes accessed | tf_op | source)
XLA Modules:
  0.0 441.1 jit_solution(1406642936250250760)
XLA Ops:
  0.7 0.9 select_select_fusion
  1.6 0.9 add_convert_fusion
  2.5 0.7 add_convert_fusion.1
  3.2 0.7 maximum_bitcast_fusion.1
  3.9 0.6 fusion.1.msg
  4.5 249.0 %forward.1 = (bf16[4,8,1152,768]{3,2,1,0:T(8,128)(2,1)}, f32[4,16,768]{2,1,0:T(8,128)}, bf16[512,768]{1,0:T(8,128)(2,1)}, bf16[512,768]{1,0:T(8,128)(2,1)}, f32[...) custom-call(s32[2]{0:T(128)} %lens.1, s32[2]{0:T(128)} %lenk.1, ...), custom_call_target="tpu_custom_call" | custom-call | tf_op jit(solution)/shard_map/forward/pallas_call | solution.py:392
  253.6 176.7 %backward.1 = (bf16[2,8,1152,768]{3,2,1,0:T(8,128)(2,1)}, bf16[512,768]{1,0:T(8,128)(2,1)}, bf16[2,96,2304]{2,1,0:T(8,128)(2,1)}, bf16[2,96,768]{2,1,0:T(8,128)(...) custom-call(s32[2]{0:T(128)} %lens.1, ...), custom_call_target="tpu_custom_call" | custom-call | tf_op jit(solution)/shard_map/backward/pallas_call | solution.py:751
  430.3 0.0 copy-start
  430.3 3.0 convert_element_type.34
  433.3 0.0 copy-start.1
  433.4 0.0 copy-done
  433.4 0.0 copy-start.4
  433.4 1.6 convert_element_type.35
  434.9 0.0 copy-start.5
  434.9 0.0 copy-start.6
  434.9 0.0 copy-start.2
  434.9 0.0 copy-done.1
  434.9 0.0 copy-start.3
  435.0 1.3 convert_element_type.32
  436.3 0.0 copy-done.4
  436.3 0.9 convert_element_type.33
  437.1 0.0 copy-done.5
  437.2 0.7 constant_dynamic-slice_fusion.8
  437.9 0.6 constant_dynamic-slice_fusion.7
  438.5 0.0 copy-done.6
  438.5 0.6 slice_reduce_fusion
  439.1 0.0 copy-done.2
  439.1 0.9 copy.54
  440.0 0.0 copy-done.3
  440.0 0.9 copy.55
  (11 shorter events, 0.1 us)
Async XLA Ops:
  430.3 3.0 copy-start
  433.3 1.6 copy-start.1
  433.4 2.9 copy-start.4
  434.9 2.2 copy-start.5
  434.9 3.5 copy-start.6
  434.9 4.2 copy-start.2
  434.9 5.0 %copy-start.3 = (bf16[512,768]{1,0:T(8,128)(2,1)S(1)}, bf16[512,768]{1,0:T(8,128)(2,1)}, u32[]{:S(2)}) copy-start(bf16[512,768]{1,0:T(8,128)(2,1)} %get-tuple-element.73) | copy-start | bytes 2359300
